TPU v7x, 256 devices: a whole 4x4x8 slice. The times are simulated.
256 devices in a mesh: aux: 8 (over x_hi, y), blk: 32 (over z, x_lo, core).
Axes of the slice: x: 4 (x_hi: 2, x_lo: 2; x = x_hi * 2 + x_lo), y: 4, z: 8, core: 2. Of those that a mesh axis runs over, the one named last changes fastest.
Arguments:
- three_center: bfloat16 [3072, 8, 128, 128], P(('aux', 'blk')), may hold values from -6 to 6
- slot_block: int32 [3072], P(('aux', 'blk')), may hold values from 0 to 47
- slot_aux: int32 [3072], P(('aux', 'blk')), may hold values from 0 to 1
- live_slots: int32 [256], P(('aux', 'blk')), may hold values from 1 to 12, as said below
- vir_coef: bfloat16 [6144, 256], replicated, may hold values from -0.00169145587 to 0.00169145587
- eps_occ: float32 [4000], replicated, may hold values from -1.5 to -0.3
- eps_vir: float32 [256], replicated, may hold values from 0.2 to 3
- occ_index: int32 [8], replicated, may hold values from 0 to 3999, as said below
Outputs:
- amplitudes: float32 [8, 256, 8, 256], P('aux', 'blk')
- pair_energy: float32 [8, 8], P('aux')
Inputs may be any that keep to these rules, and one draw needn't show every extreme that they name: The slots in use on a device are its first live_slots ones; the others hold data that is not used. Some device holds exactly 12 slots in use in every draw. `occ_index`: the indices are distinct; the first and the last occupied orbital of the system are in every batch.
All inputs are finite; a program needn't handle non-finite values.
Results may differ from a plain program's by a relative error of at most 0.0035.
Values may be sent and summed in bfloat16 or wider, within the bound.
No kernel may reach another device: no remote copies, remote signals or barrier semaphores. Data moves between devices by JAX's collectives and lax.ppermute only.
A program may use at most 64 MiB of HBM per device.

v0:
```python
import jax
import jax.numpy as jnp
from jax import lax
from jax.sharding import PartitionSpec as P

AUX_BLOCKS_DEV = 2


def in_blocks(x, dim, peers):
    lengths = x.shape
    blocks = x.reshape(*lengths[:dim], peers, lengths[dim] // peers, *lengths[dim + 1 :])
    return jnp.moveaxis(blocks, dim, 0)


def sent_and_summed(x, axis, dim):
    peers = lax.axis_size(axis)
    blocks = lax.all_to_all(in_blocks(x, dim, peers), axis, 0, 0, tiled=True)
    return jnp.sum(blocks, axis=0)


def from_everyone(x, axis):
    copies = jnp.broadcast_to(x, (lax.axis_size(axis), *x.shape))
    return lax.all_to_all(copies, axis, split_axis=0, concat_axis=0, tiled=True)


def taken_together(x, axis):
    everything = from_everyone(x, axis)
    return jnp.sum(everything, axis=0)


def body(three_center, slot_block, slot_aux, live_slots, vir_coef, eps_occ, eps_vir, occ_index):
    blk_count = lax.axis_size("blk")
    occ_row = lax.axis_index("aux")
    slot_count = three_center.shape[0]
    occ_count = three_center.shape[1]
    ao_span = three_center.shape[3]
    vir_count = vir_coef.shape[1]
    coef_blocks = vir_coef.reshape(vir_coef.shape[0] // ao_span, ao_span, vir_count)
    coefficients = jnp.take(coef_blocks, slot_block, axis=0)
    products = jnp.einsum(
        "soqn,snv->soqv", three_center, coefficients, preferred_element_type=jnp.float32
    )
    keep = (jnp.arange(slot_count) < live_slots[0]).astype(jnp.float32)
    select = (slot_aux[:, None] == jnp.arange(AUX_BLOCKS_DEV)[None, :]).astype(jnp.float32)
    select = select * keep[:, None]
    local_rows = jnp.einsum("sk,soqv->kqov", select, products).astype(jnp.bfloat16)
    halfed = lax.all_gather(local_rows, "aux", axis=0, tiled=True)
    own_rows = lax.dynamic_index_in_dim(halfed, occ_row, 2, keepdims=False)
    rows_dev = vir_count // blk_count
    direct = sent_and_summed(
        lax.dot_general(
            own_rows, halfed, (((0, 1), (0, 1)), ((), ())), preferred_element_type=jnp.float32
        ),
        "blk",
        0,
    )
    swapped = lax.all_to_all(
        direct.astype(jnp.bfloat16), "blk", split_axis=2, concat_axis=0, tiled=True
    ).astype(direct.dtype)
    crossed = jnp.transpose(swapped, (2, 1, 0))
    first_vir = lax.axis_index("blk") * rows_dev
    occ_levels = jnp.take(eps_occ, occ_index)
    own_level = jnp.sum(jnp.where(jnp.arange(occ_count) == occ_row, occ_levels, 0.0))
    vir_levels = lax.dynamic_slice_in_dim(eps_vir, first_vir, rows_dev, 0)
    denominator = (
        own_level + occ_levels[None, :, None] - vir_levels[:, None, None] - eps_vir[None, None, :]
    )
    amplitudes = (direct / denominator)[None]
    pair_part = jnp.sum(direct * (2.0 * direct - crossed) / denominator, axis=(0, 2))
    pair_energy = taken_together(pair_part, "blk")[None]
    return (amplitudes, pair_energy)


def solution(mesh):
    in_specs = (
        P(("aux", "blk"), None, None, None),
        P(("aux", "blk")),
        P(("aux", "blk")),
        P(("aux", "blk")),
        P(),
        P(),
        P(),
        P(),
    )
    out_specs = (P("aux", "blk", None, None), P("aux", None))
    return jax.shard_map(body, mesh=mesh, in_specs=in_specs, out_specs=out_specs, check_vma=False)
```

profile of v0, /device:TPU:1, one launch (start us, length us, event | category | flops | bytes accessed | tf_op | source)
XLA Modules:
  0.0 279.1 jit_solution(5928779925349590584)
XLA Ops:
  7.2 0.0 copy-start
  7.2 0.0 all-gather.2.cloned.1.call-start
  7.2 0.8 compare_select_fusion.1
  8.0 0.8 compare_and_fusion
  8.8 3.4 %gather_fusion = bf16[12,128,256]{2,1,0:T(8,128)(2,1)} fusion(bf16[48,128,256]{2,1,0:T(8,128)(2,1)} %bitcast.56, s32[1024]{0:T(1024)S(1)} %pad_clamp_fusion.1), kind=kCustom, calls=%fused_computation | custom fusion | bytes 1572912 | tf_op jit(solution)/shard_map/jit(_take)/gather | solution.py:39
  12.2 0.0 copy-done
  12.2 5.8 %convolution_bitcast_fusion = bf16[12,8,128,256]{2,3,1,0:T(8,128)(2,1)} fusion(bf16[12,8,128,128]{3,2,1,0:T(8,128)(2,1)S(1)} %copy-done, bf16[12,128,256]{2,1,0:T(8,128)(2,1)} %gather_fusion, pred[12]{0:T(512)(128)(4,1)S(1)} %compare_and_fusion), kind=kOutput, calls=%fused_computation.4 | convolution fusion | flops 805699584 | bytes 10223628 | tf_op jit(solution)/shard_map/soqn,snv->soqv/dot_general | solution.py:40
  18.1 0.0 copy-start.4
  18.1 11.5 %copy.67 = bf16[12,8,128,256]{3,0,2,1:T(8,128)(2,1)} copy(bf16[12,8,128,256]{2,3,1,0:T(8,128)(2,1)} %convolution_bitcast_fusion) | data formatting | bytes 12582912 | tf_op jit(solution)/shard_map/soqn,snv->soqv/dot_general | solution.py:40
  30.2 0.0 copy-done.4
  30.3 4.6 %fusion.5 = bf16[2,128,8,256]{3,0,1,2:T(2,128)(2,1)S(1)} fusion(bf16[12,8,128,256]{3,0,2,1:T(8,128)(2,1)} %copy.67, bf16[12]{0:T(256)(128)(2,1)S(1)} %compare_convert_fusion, s32[12]{0:T(128)S(1)} %copy-done.4), kind=kOutput, calls=%fused_computation.7 | convolution fusion | flops 12582960 | bytes 7340104 | tf_op jit(solution)/shard_map/sk,soqv->kqov/dot_general | solution.py:46
  34.9 1.6 copy.68
  36.5 0.0 all-gather.2.cloned.1.call-update
  36.5 115.7 %all-gather.2.cloned.1.call-done = bf16[16,128,8,256]{3,2,1,0:T(8,128)(2,1)} async-done(((bf16[2,128,8,256]{3,2,1,0:T(8,128)(2,1)}), bf16[16,128,8,256]{3,2,1,0:T(8,128)(2,1)}) %all-gather.2.cloned.1.call-update) | async-done | bytes 8388624 | tf_op jit(solution)/shard_map/all_gather | solution.py:47
  152.2 8.6 %copy.69 = bf16[16,128,8,256]{3,1,0,2:T(8,128)(2,1)} copy(bf16[16,128,8,256]{3,2,1,0:T(8,128)(2,1)} %all-gather.2.cloned.1.call-done) | data formatting | bytes 16777216 | tf_op jit(solution)/shard_map/all_gather | solution.py:47
  160.8 2.3 dynamic-slice_bitcast_fusion
  163.1 2.6 copy.70
  165.8 0.0 copy-start.2
  165.8 0.0 copy-start.3
  165.8 0.0 copy-start.1
  165.8 7.5 %fusion.2 = f32[32,8,8,256]{3,1,2,0:T(8,128)} fusion(bf16[32,8,16,128,1]{3,2,1,0,4:T(8,128)(2,1)} %bitcast.55, bf16[16,128,8,256]{3,2,1,0:T(8,128)(2,1)} %all-gather.2.cloned.1.call-done), kind=kOutput, calls=%fused_computation.5 | convolution fusion | flops 2147483648 | bytes 11534336 | tf_op jit(solution)/shard_map/dot_general | solution.py:51
  173.3 8.3 %all-to-all-start = ((f32[32,8,8,256]{3,1,2,0:T(8,128)}), f32[32,8,8,256]{3,1,2,0:T(8,128)}, u32[]{:S(2)}, u32[]{:S(2)}) async-start(f32[32,8,8,256]{3,1,2,0:T(8,128)} %fusion.2), calls=%async_computation | async-start | bytes 4194304 | tf_op jit(solution)/shard_map/all_to_all | solution.py:17
  181.6 0.0 copy-done.2
  181.6 0.1 dynamic_slice.8
  181.7 0.0 copy-done.3
  181.7 0.0 copy-done.1
  181.7 0.6 gather_fusion.1
  182.4 0.6 fusion.17
  183.0 0.7 broadcast_add_fusion
  183.6 48.1 %all-to-all-done = f32[32,8,8,256]{3,1,2,0:T(8,128)} async-done(((f32[32,8,8,256]{3,1,2,0:T(8,128)}), f32[32,8,8,256]{3,1,2,0:T(8,128)}, u32[]{:S(2)}, u32[]{:S(2)}) %all-to-all-start) | async-done | bytes 2097184 | tf_op jit(solution)/shard_map/all_to_all | solution.py:17
  231.7 1.7 reduce_sum.38
  233.5 1.1 copy.73
  234.5 2.2 reshape.111
  236.7 4.9 %all-to-all-start.1 = ((bf16[32,2,256]{2,1,0:T(2,128)(2,1)}), bf16[32,2,256]{2,1,0:T(2,128)(2,1)S(1)}, u32[]{:S(2)}, u32[]{:S(2)}) async-start(bf16[32,2,256]{2,1,0:T(2,128)(2,1)} %reshape.111), calls=%async_computation.1 | async-start | bytes 65536 | tf_op jit(solution)/shard_map/all_to_all | solution.py:57
  241.6 0.1 broadcast_subtract_fusion
  241.7 8.0 %all-to-all-done.1 = bf16[32,2,256]{2,1,0:T(2,128)(2,1)S(1)} async-done(((bf16[32,2,256]{2,1,0:T(2,128)(2,1)}), bf16[32,2,256]{2,1,0:T(2,128)(2,1)S(1)}, u32[]{:S(2)}, u32[]{:S(2)}) %all-to-all-start.1) | async-done | bytes 32800 | tf_op jit(solution)/shard_map/all_to_all | solution.py:57
  249.7 1.4 reshape.112
  251.1 1.4 copy.74
  252.5 1.6 reshape.87
  254.1 3.1 %copy.75 = f32[32,8,8,8]{1,0,3,2:T(8,128)} copy(f32[32,8,8,8]{3,0,2,1:T(8,128)} %bitcast.52) | data formatting | bytes 131072 | tf_op jit(solution)/shard_map/transpose | solution.py:60
  257.2 1.8 reshape.86
  259.0 0.2 fusion.13
  259.2 0.6 broadcast_in_dim.38
  259.8 3.9 %all-to-all-start.2 = ((f32[32,1,8]{2,1,0:T(1,128)}), f32[32,1,8]{2,1,0:T(1,128)S(1)}, u32[]{:S(2)}, u32[]{:S(2)}) async-start(f32[32,1,8]{2,1,0:T(1,128)} %broadcast_in_dim.38), calls=%async_computation.2 | async-start | bytes 32768 | tf_op jit(solution)/shard_map/all_to_all | solution.py:23
  263.7 0.1 bitcast_divide_fusion
  263.8 0.7 copy.77
  264.4 7.2 %all-to-all-done.2 = f32[32,1,8]{2,1,0:T(1,128)S(1)} async-done(((f32[32,1,8]{2,1,0:T(1,128)}), f32[32,1,8]{2,1,0:T(1,128)S(1)}, u32[]{:S(2)}, u32[]{:S(2)}) %all-to-all-start.2) | async-done | bytes 1056 | tf_op jit(solution)/shard_map/all_to_all | solution.py:23
  271.7 0.6 reduce_sum.42
  (5 shorter events, 0.0 us)
Async XLA Ops:
  7.2 5.0 %copy-start = (bf16[12,8,128,128]{3,2,1,0:T(8,128)(2,1)S(1)}, bf16[12,8,128,128]{3,2,1,0:T(8,128)(2,1)}, u32[]{:S(2)}) copy-start(bf16[12,8,128,128]{3,2,1,0:T(8,128)(2,1)} %param.8) | copy-start | bytes 9437188
  7.2 145.0 %all-gather.2.cloned.1.call-start = ((), (), s32[]{:S(2)}) async-start(), calls=%async_computation.3 | async-start | bytes 9437184 | tf_op jit(solution)/shard_map/all_gather | solution.py:47
  18.1 12.2 %copy-start.4 = (s32[12]{0:T(128)S(1)}, s32[12]{0:T(128)}, u32[]{:S(2)}) copy-start(s32[12]{0:T(128)} %param.10) | copy-start | bytes 148
  165.8 15.8 %copy-start.2 = (f32[256]{0:T(256)S(1)}, f32[256]{0:T(256)}, u32[]{:S(2)}) copy-start(f32[256]{0:T(256)} %param.14) | copy-start | bytes 3076
  165.8 15.9 %copy-start.3 = (s32[8]{0:T(128)S(1)}, s32[8]{0:T(128)}, u32[]{:S(2)}) copy-start(s32[8]{0:T(128)} %param.15) | copy-start | bytes 100
  165.8 15.9 %copy-start.1 = (f32[4000]{0:T(1024)S(1)}, f32[4000]{0:T(1024)}, u32[]{:S(2)}) copy-start(f32[4000]{0:T(1024)} %param.13) | copy-start | bytes 48004
  173.3 58.4 %all-to-all-start = ((f32[32,8,8,256]{3,1,2,0:T(8,128)}), f32[32,8,8,256]{3,1,2,0:T(8,128)}, u32[]{:S(2)}, u32[]{:S(2)}) async-start(f32[32,8,8,256]{3,1,2,0:T(8,128)} %fusion.2), calls=%async_computation | async-start | bytes 4194304 | tf_op jit(solution)/shard_map/all_to_all | solution.py:17
  236.7 13.0 %all-to-all-start.1 = ((bf16[32,2,256]{2,1,0:T(2,128)(2,1)}), bf16[32,2,256]{2,1,0:T(2,128)(2,1)S(1)}, u32[]{:S(2)}, u32[]{:S(2)}) async-start(bf16[32,2,256]{2,1,0:T(2,128)(2,1)} %reshape.111), calls=%async_computation.1 | async-start | bytes 65536 | tf_op jit(solution)/shard_map/all_to_all | solution.py:57
  259.8 11.9 %all-to-all-start.2 = ((f32[32,1,8]{2,1,0:T(1,128)}), f32[32,1,8]{2,1,0:T(1,128)S(1)}, u32[]{:S(2)}, u32[]{:S(2)}) async-start(f32[32,1,8]{2,1,0:T(1,128)} %broadcast_in_dim.38), calls=%async_computation.2 | async-start | bytes 32768 | tf_op jit(solution)/shard_map/all_to_all | solution.py:23
Sparse Core Ops, SparseCore 0:
  36.7 115.5 all-gather.1
where the time goes:
time: 280 us; the launch traced here: 279 us
  waiting for transfers between devices  179 us (64%)
  local copies, waits for them, and re-layouts  44.7 us (16%)
  matrix products  18 us (6%)
  starting transfers between devices  17.1 us (6%)
  between operations  14.8 us (5%)
  other arithmetic  5.51 us (2%)
    all_gather x1, waiting for transfers between devices, body(): halfed = lax.all_gather(local_rows, 'aux', axis=0, tiled=True)  116 us
    all_to_all x1, waiting for transfers between devices, sent_and_summed(): blocks = lax.all_to_all(in_blocks(x, dim, peers), axis, 0, 0, tiled=True)  48.1 us
    dot_general x1, local copies, waits for them, and re-layouts, body(): jnp.einsum('soqn,snv->soqv', three_center, coefficients, preferred_elemen...  11.5 us
    all_gather x1, local copies, waits for them, and re-layouts, body(): halfed = lax.all_gather(local_rows, 'aux', axis=0, tiled=True)  8.63 us
    all_to_all x1, starting transfers between devices, sent_and_summed(): blocks = lax.all_to_all(in_blocks(x, dim, peers), axis, 0, 0, tiled=True)  8.31 us
    all_to_all x1, waiting for transfers between devices, body(): lax.all_to_all(direct.astype(jnp.bfloat16), 'blk', split_axis=2, concat_a...  8.04 us
    dot_general x1, matrix products, body(): lax.dot_general(own_rows, halfed, (((0, 1), (0, 1)), ((), ())), preferred...  7.5 us
    all_to_all x1, waiting for transfers between devices, from_everyone(): return lax.all_to_all(copies, axis, split_axis=0, concat_axis=0, tiled=True)  7.23 us
  transfers between devices with their start and end apart: 4, of which 4 were waited for; matrix products, arithmetic and copies ran while one was open for 1% of the time, Pallas kernels for 0%

commit v1 on v0

v1 whole, which is shorter than its diff:
```python
import functools

import jax
import jax.numpy as jnp
from jax import lax
from jax.experimental import pallas as pl
from jax.experimental.pallas import tpu as pltpu
from jax.sharding import Mesh
from jax.sharding import PartitionSpec as P

F32 = jnp.float32
BF16 = jnp.bfloat16
OCC = 8
VIR = 256
SPAN = 128
SLOTS = 12
KINDS = 2
ROWS = 256
AUX = ("xh", "y")
BLK = ("z", "xl", "core")
X = ("xh", "xl")

VMEM = pl.BlockSpec(memory_space=pltpu.VMEM)
SMEM = pl.BlockSpec(memory_space=pltpu.SMEM)
ANYWHERE = pl.BlockSpec(memory_space=pl.ANY)


def params(mib):
    return pltpu.CompilerParams(vmem_limit_bytes=mib * 2**20)


def half_kernel(block_ref, kind_ref, live_ref, three_ref, coef_ref, out_ref, three, coef, weights, sems):
    copies = []
    for s in range(SLOTS):
        first = pl.multiple_of(block_ref[s] * SPAN, SPAN)
        copies.append(pltpu.make_async_copy(coef_ref.at[pl.ds(first, SPAN)], coef.at[s], sems.at[s]))
    for s in range(SLOTS):
        copies.append(
            pltpu.make_async_copy(three_ref.at[s], three.at[:, :, pl.ds(s * SPAN, SPAN)], sems.at[SLOTS + s])
        )
    for copy in copies:
        copy.start()
    for s in range(SLOTS):
        copies[s].wait()
        values = coef[s]
        for k in range(KINDS):
            used = jnp.logical_and(kind_ref[s] == k, s < live_ref[0])
            weights[pl.ds(s * SPAN, SPAN), pl.ds(k * VIR, VIR)] = jnp.where(used, values, jnp.zeros_like(values))
    for s in range(SLOTS):
        copies[SLOTS + s].wait()
    for o in range(0, OCC, 4):
        left = three[pl.ds(o, 4)].reshape(4 * SPAN, SLOTS * SPAN)
        done = jnp.dot(left, weights[...], preferred_element_type=F32).astype(BF16)
        for i in range(4):
            for k in range(KINDS):
                out_ref[o + i, pl.ds(k * SPAN, SPAN), :] = done[i * SPAN : (i + 1) * SPAN, k * VIR : (k + 1) * VIR]


def half_transform(slot_block, slot_aux, live_slots, three_center, vir_coef):
    return pl.pallas_call(
        half_kernel,
        out_shape=jax.ShapeDtypeStruct((OCC, ROWS, VIR), BF16),
        in_specs=[SMEM, SMEM, SMEM, ANYWHERE, ANYWHERE],
        out_specs=VMEM,
        scratch_shapes=[
            pltpu.VMEM((OCC, SPAN, SLOTS * SPAN), BF16),
            pltpu.VMEM((SLOTS, SPAN, VIR), BF16),
            pltpu.VMEM((SLOTS * SPAN, KINDS * VIR), BF16),
            pltpu.SemaphoreType.DMA((2 * SLOTS,)),
        ],
        compiler_params=params(24),
    )(slot_block, slot_aux, live_slots, three_center, vir_coef)


def partial_kernel(place_ref, own_ref, other_ref, *rest):
    outs, left = rest[:10], rest[10]
    x, y, core = place_ref[0], place_ref[1], place_ref[2]
    row = lax.broadcasted_iota(jnp.int32, (128, VIR), 0)
    col = lax.broadcasted_iota(jnp.int32, (128, VIR), 1)
    low, z, r = row // 64, (row // 8) % 8, row % 8
    pick = (col == z * 32 + low * 16 + core * 8 + r).astype(F32).astype(BF16)

    def turned(ref, o, rows):
        return lax.dot_general(rows, ref[o], (((1,), (1,)), ((), ())), preferred_element_type=F32).astype(BF16)

    def send(axis, first_j):
        ahead, back, one, minus, own = outs[axis * 5 : axis * 5 + 5]
        places = {
            (2, 0): (ahead, 0), (1, 1): (ahead, 1), (2, 1): (back, 0), (3, 0): (back, 1),
            (1, 0): (one, None), (3, 1): (minus, None), (0, 0): (own, 0), (0, 1): (own, 1),
        }
        for j in range(4):
            right = jnp.concatenate([own_ref[first_j + j], other_ref[first_j + j]], axis=0)
            done = jnp.dot(left[...], right, preferred_element_type=F32).astype(BF16)
            for d in range(4):
                for h in range(2):
                    ref, which = places[d, h]
                    for u in range(2):
                        at = (d * 4 + h * 2 + u) * 64
                        part = done[at : at + 64]
                        if which is None:
                            ref[u, j] = part
                        else:
                            ref[which, u, j] = part

    for d in range(4):
        for h in range(2):
            o = h * 4 + lax.rem(y + d, 4)
            rows = pl.ds((d * 2 + h) * 128, 128)
            left[rows, pl.ds(0, ROWS)] = turned(own_ref, o, pick)
            left[rows, pl.ds(ROWS, ROWS)] = turned(other_ref, o, pick)
    send(0, 0)
    row = lax.broadcasted_iota(jnp.int32, (64, VIR), 0)
    col = lax.broadcasted_iota(jnp.int32, (64, VIR), 1)
    for d in range(4):
        to = lax.rem(x + d, 4)
        pick = (col == row // 8 * 32 + lax.rem(to, 2) * 16 + core * 8 + row % 8).astype(F32).astype(BF16)
        for h in range(4):
            o = to // 2 * 4 + h
            rows = pl.ds((d * 4 + h) * 64, 64)
            left[rows, pl.ds(0, ROWS)] = turned(own_ref, o, pick)
            left[rows, pl.ds(ROWS, ROWS)] = turned(other_ref, o, pick)
    send(1, 4)


def partial(place, own, other):
    pair = jax.ShapeDtypeStruct((2, 2, 4, 64, VIR), BF16)
    single = jax.ShapeDtypeStruct((2, 4, 64, VIR), BF16)
    return pl.pallas_call(
        partial_kernel,
        out_shape=[pair, pair, single, single, pair] * 2,
        in_specs=[SMEM, VMEM, VMEM],
        out_specs=[VMEM] * 10,
        scratch_shapes=[pltpu.VMEM((1024, 2 * ROWS), BF16)],
        compiler_params=params(40),
    )(place, own, other)


def first_sum_kernel(place_ref, *refs):
    ins, outs, kept = refs[:10], refs[10:18], refs[18]
    for axis in range(2):
        own, from_back, from_ahead, last_back, last_ahead = ins[axis * 5 : axis * 5 + 5]
        at = place_ref[axis]
        for h, (one, two) in enumerate(((from_ahead, last_back), (from_back, last_ahead))):
            for u in range(2):
                for j in range(4):
                    total = own[h, u, j].astype(F32) + one[1, u, j].astype(F32) + two[u, j].astype(F32)
                    kept[h * 2 + u, j] = total.astype(BF16)
        for d in range(4):
            outs[axis * 4 + d][...] = kept[lax.rem(at + d, 4)]


def first_sum(place, ins):
    out = jax.ShapeDtypeStruct((4, 64, VIR), BF16)
    return pl.pallas_call(
        first_sum_kernel,
        out_shape=[out] * 8,
        in_specs=[SMEM] + [VMEM] * 10,
        out_specs=[VMEM] * 8,
        scratch_shapes=[pltpu.VMEM((4, 4, 64, VIR), BF16)],
        compiler_params=params(24),
    )(place, *ins)


def second_sum_kernel(*refs):
    ins, out = refs[:8], refs[8]
    for half in range(2):
        for j in range(4):
            total = ins[half * 4][j].astype(F32)
            for d in range(1, 4):
                total = total + ins[half * 4 + d][j].astype(F32)
            for z in range(8):
                out[z, half * 4 + j] = total[z * 8 : z * 8 + 8]


def second_sum(ins):
    return pl.pallas_call(
        second_sum_kernel,
        out_shape=jax.ShapeDtypeStruct((8, OCC, 8, VIR), F32),
        in_specs=[VMEM] * 8,
        out_specs=VMEM,
        compiler_params=params(24),
    )(*ins)


def finish_kernel(parts_ref, below_ref, direct_ref, cross_ref, amp_ref):
    total = parts_ref[0]
    for z in range(1, 8):
        total = total + parts_ref[z]
    direct_ref[...] = total
    cross_ref[...] = total.astype(BF16)
    amp = total / below_ref[...]
    for j in range(OCC):
        for r in range(8):
            amp_ref[r, pl.ds(j, 1), :] = amp[j, r : r + 1, :]


def finish(parts, below):
    full = (OCC, 8, VIR)
    return pl.pallas_call(
        finish_kernel,
        out_shape=[jax.ShapeDtypeStruct(full, F32), jax.ShapeDtypeStruct(full, BF16), jax.ShapeDtypeStruct((8, OCC, VIR), F32)],
        in_specs=[VMEM] * 2,
        out_specs=[VMEM] * 3,
        compiler_params=params(16),
    )(parts, below)


def energy_kernel(direct_ref, cross_ref, below_ref, out_ref):
    direct = direct_ref[...]
    terms = direct * (2.0 * direct - cross_ref[...].astype(F32)) / below_ref[...]
    out_ref[...] = jnp.broadcast_to(jnp.sum(terms, axis=(1, 2), keepdims=True)[:, 0], (OCC, 128))


def energy(direct, cross, below):
    return pl.pallas_call(
        energy_kernel,
        out_shape=jax.ShapeDtypeStruct((OCC, 128), F32),
        in_specs=[VMEM] * 3,
        out_specs=VMEM,
        compiler_params=params(16),
    )(direct, cross, below)


def moved(x, axis, by):
    n = lax.axis_size(axis)
    return lax.ppermute(x, axis, [(i, (i + by) % n) for i in range(n)])


def body(three_center, slot_block, slot_aux, live_slots, vir_coef, eps_occ, eps_vir, occ_index):
    x, y, core = lax.axis_index(X), lax.axis_index("y"), lax.axis_index("core")
    place = jnp.stack([x, y, core]).astype(jnp.int32)
    own = half_transform(slot_block, slot_aux, live_slots, three_center, vir_coef)
    other = moved(own, "core", 1)
    parts = partial(place, own, other)
    got = []
    for axis, (ahead, back, one, minus, mine) in zip(("y", X), (parts[:5], parts[5:])):
        got.append((axis, moved(ahead, axis, 1), moved(back, axis, -1), one, minus, mine))
    ins = []
    for axis, from_back, from_ahead, one, minus, mine in got:
        one = (one.astype(F32) + from_back[0].astype(F32)).astype(BF16)
        minus = (minus.astype(F32) + from_ahead[0].astype(F32)).astype(BF16)
        ins += [mine, from_back, from_ahead, moved(one, axis, 1), moved(minus, axis, -1)]
    parts = first_sum(place, ins)
    ins = []
    for axis, group in zip((X, "y"), (parts[:4], parts[4:])):
        ins += [group[0]] + [moved(group[d], axis, d) for d in range(1, 4)]
    parts = lax.all_to_all(second_sum(ins), "z", 0, 0, tiled=True)

    occ_row, first_vir = lax.axis_index(AUX), lax.axis_index(BLK) * 8
    levels = jnp.take(eps_occ, occ_index)
    own_level = jnp.sum(jnp.where(jnp.arange(OCC) == occ_row, levels, 0.0))
    vir_levels = lax.dynamic_slice_in_dim(eps_vir, first_vir, 8, 0)
    below = own_level + levels[:, None, None] - vir_levels[None, :, None] - eps_vir[None, None, :]

    direct, cross, amplitudes = finish(parts, below)
    cross = lax.all_to_all(cross, AUX, 0, 0, tiled=True)
    pair = energy(direct, cross, below)
    copies = jnp.broadcast_to(pair, (32, OCC, 128))
    pair = jnp.sum(lax.all_to_all(copies, BLK, 0, 0, tiled=True), axis=0)[:, 0]
    return amplitudes[None], pair[None]


def solution(mesh):
    fine = Mesh(mesh.devices.reshape(2, 4, 8, 2, 2), ("xh", "y", "z", "xl", "core"))
    every = AUX + BLK
    in_specs = (P(every, None, None, None), P(every), P(every), P(every), P(), P(), P(), P())
    out_specs = (P(AUX, BLK, None, None), P(AUX, None))
    return jax.shard_map(body, mesh=fine, in_specs=in_specs, out_specs=out_specs, check_vma=False)
```

time: 280 us -> 113 us (0.40)
  waiting for transfers between devices: 179 us -> 34.2 us
  local copies, waits for them, and re-layouts: 44.7 us -> 6.45 us
  blocking collectives: 0 us -> 30.9 us
  matrix products: 18 us -> 0 us
  between operations: 14.8 us -> 1.45 us
  Pallas kernels: 0 us -> 11.7 us
  starting transfers between devices: 17.1 us -> 25.8 us
  other arithmetic: 5.51 us -> 1.8 us
    all_gather x1 -> x0, waiting for transfers between devices: 116 us -> none  [body(): halfed = lax.all_gather(local_rows, 'aux', axis=0, tiled=True)]
    all_to_all x3 -> x1, waiting for transfers between devices: 63.4 us -> 9.9 us  [body(): parts = lax.all_to_all(second_sum(ins), 'z', 0, 0, tiled=True)]
    all_to_all x0 -> x2, blocking collectives: none -> 30.9 us  [the longest x1 20.2 us: body(): pair = jnp.sum(lax.all_to_all(copies, BLK, 0, 0, tiled=True), axis=0)[:, 0]]
    ppermute x0 -> x15, waiting for transfers between devices: none -> 24.3 us  [moved(): return lax.ppermute(x, axis, [(i, (i + by) % n) for i in range(n)])]
    dot_general x3 -> x0, matrix products: 18 us -> none  [the longest x1 7.5 us: body(): lax.dot_general(own_rows, halfed, (((0, 1), (0, 1)), ((), ())), preferred...]
    ppermute x0 -> x15, starting transfers between devices: none -> 17.6 us  [moved(): return lax.ppermute(x, axis, [(i, (i + by) % n) for i in range(n)])]
    dot_general x3 -> x0, local copies, waits for them, and re-layouts: 16.5 us -> none  [the longest x1 11.5 us: body(): jnp.einsum('soqn,snv->soqv', three_center, coefficients, preferred_elemen...]
    pallas_call x0 -> x6, Pallas kernels: none -> 11.7 us  [the longest x1 4.77 us: partial(): pl.pallas_call(partial_kernel, out_shape=[pair, pair, single, single, pai...]
  transfers between devices with their start and end apart: 4 -> 16, of which waited for: 4 -> 11; matrix products, arithmetic and copies ran while one was open for 1% -> 2% of each run, Pallas kernels for 0% -> 0%
where the time goes in v1:
time: 113 us; the launch traced here: 112 us
  waiting for transfers between devices  34.2 us (30%)
  blocking collectives  30.9 us (27%)
  starting transfers between devices  25.8 us (23%)
  Pallas kernels  11.7 us (10%)
  local copies, waits for them, and re-layouts  6.45 us (6%)
  other arithmetic  1.8 us (2%)
  between operations  1.45 us (1%)
    ppermute x15, waiting for transfers between devices, moved(): return lax.ppermute(x, axis, [(i, (i + by) % n) for i in range(n)])  24.3 us
    all_to_all x1, blocking collectives, body(): pair = jnp.sum(lax.all_to_all(copies, BLK, 0, 0, tiled=True), axis=0)[:, 0]  20.2 us
    ppermute x15, starting transfers between devices, moved(): return lax.ppermute(x, axis, [(i, (i + by) % n) for i in range(n)])  17.6 us
    all_to_all x1, blocking collectives, body(): cross = lax.all_to_all(cross, AUX, 0, 0, tiled=True)  10.6 us
    all_to_all x1, waiting for transfers between devices, body(): parts = lax.all_to_all(second_sum(ins), 'z', 0, 0, tiled=True)  9.9 us
    all_to_all x1, starting transfers between devices, body(): parts = lax.all_to_all(second_sum(ins), 'z', 0, 0, tiled=True)  8.21 us
    unnamed x14, local copies, waits for them, and re-layouts  5.1 us
    pallas_call x1, Pallas kernels, partial(): pl.pallas_call(partial_kernel, out_shape=[pair, pair, single, single, pai...  4.77 us
  transfers between devices with their start and end apart: 16, of which 11 were waited for; matrix products, arithmetic and copies ran while one was open for 2% of the time, Pallas kernels for 0%

profile of v1, /device:TPU:1, one launch (start us, length us, event | category | flops | bytes accessed | tf_op | source)
XLA Modules:
  0.0 112.3 jit_solution(9145536058113465242)
XLA Ops:
  1.3 1.9 %copy-done.1 = bf16[12,8,128,128]{3,2,1,0:T(8,128)(2,1)S(1)} copy-done((bf16[12,8,128,128]{3,2,1,0:T(8,128)(2,1)S(1)}, bf16[12,8,128,128]{3,2,1,0:T(8,128)(2,1)}, u32[]{:S(2)}) %copy-start.1) | copy-done | bytes 3145752
  3.2 1.9 %copy-done.2 = bf16[6144,256]{1,0:T(8,128)(2,1)S(1)} copy-done((bf16[6144,256]{1,0:T(8,128)(2,1)S(1)}, bf16[6144,256]{1,0:T(8,128)(2,1)}, u32[]{:S(2)}) %copy-start.2) | copy-done | bytes 3145752
  5.1 0.7 copy-done.3
  5.7 0.7 copy-done.4
  6.4 4.3 %shard_map.95.own_ref = bf16[8,256,256]{2,1,0:T(8,128)(2,1)S(1)} custom-call(s32[12]{0:T(128)S(1)} %copy-done.3, s32[12]{0:T(128)S(1)} %copy-done.4, s32[1]{0:T(128)S(6)} %copy.10.live_ref, bf16[12,8,128,128]{3,2,1,0:T(8,128)(2,1)S(1)} %copy-done.1, bf16[6144,256]{1,0:T(8,128)(2,1)S(1)} %copy-done.2), custom_call_target="tpu_custom_call" | custom-call | tf_op jit(solution)/shard_map/pallas_call | solution.py:60
  10.7 3.3 %collective-permute-start = (bf16[8,256,256]{2,1,0:T(8,128)(2,1)S(1)}, bf16[8,256,256]{2,1,0:T(8,128)(2,1)S(1)}, u32[]{:S(2)}, u32[]{:S(2)}) collective-permute-start(bf16[8,256,256]{2,1,0:T(8,128)(2,1)S(1)} %shard_map.95.own_ref), channel_id=1, source_target_pairs={{0,1},{1,0},{2,3},{3,2},{4,5},{5,4},{6,7},{7,6},{8,9},{9,8},{10,11... | collective-permute-start | bytes 3145736 | tf_op jit(solution)/shard_map/ppermute | solution.py:227
  14.1 0.1 pad_add_fusion.place_ref
  14.1 2.2 %collective-permute-done.other_ref = bf16[8,256,256]{2,1,0:T(8,128)(2,1)S(1)} collective-permute-done((bf16[8,256,256]{2,1,0:T(8,128)(2,1)S(1)}, bf16[8,256,256]{2,1,0:T(8,128)(2,1)S(1)}, u32[]{:S(2)}, u32[]{:S(2)}) %collective-permute-start) | collective-permute-done | bytes 1048608 | tf_op jit(solution)/shard_map/ppermute | solution.py:227
  16.3 4.8 %shard_map.96 = (bf16[2,2,4,64,256]{4,3,2,1,0:T(8,128)(2,1)S(1)}, bf16[2,2,4,64,256]{4,3,2,1,0:T(8,128)(2,1)S(1)}, bf16[2,4,64,256]{3,2,1,0:T(8,128)(2,1)S(1)}, ...) custom-call(s32[3]{0:T(128)S(1)} %pad_add_fusion.place_ref, ...), custom_call_target="tpu_custom_call" | custom-call | tf_op jit(solution)/shard_map/pallas_call | solution.py:129
  21.1 0.8 collective-permute-start.6
  21.9 0.7 collective-permute-start.5
  22.7 2.0 %collective-permute-start.2 = (bf16[2,2,4,64,256]{4,3,2,1,0:T(8,128)(2,1)S(1)}, bf16[2,2,4,64,256]{4,3,2,1,0:T(8,128)(2,1)S(1)}, u32[]{:S(2)}, u32[]{:S(2)}) collective-permute-start(bf16[2,2,4,64,256]{4,3,2,1,0:T(8,128)(2,1)S(1)} %get-tuple-element.25), channel_id=1, source_target_pairs={{0,96},{32,0},{64,32},{96,64},{1,97},{33,1},{65,33},{97,65},{2,98}... | collective-permute-start | bytes 1572872 | tf_op jit(solution)/shard_map/ppermute | solution.py:227
  24.7 9.7 %collective-permute-done.6.refs_7_ = bf16[2,2,4,64,256]{4,3,2,1,0:T(8,128)(2,1)S(1)} collective-permute-done((bf16[2,2,4,64,256]{4,3,2,1,0:T(8,128)(2,1)S(1)}, bf16[2,2,4,64,256]{4,3,2,1,0:T(8,128)(2,1)S(1)}, u32[]{:S(2)}, u32[]{:S(2)}) %collective-permute-start.6) | collective-permute-done | bytes 524320 | tf_op jit(solution)/shard_map/ppermute | solution.py:227
  34.3 0.1 fusion
  34.4 2.0 %collective-permute-start.8 = (bf16[2,4,64,256]{3,2,1,0:T(8,128)(2,1)S(1)}, bf16[2,4,64,256]{3,2,1,0:T(8,128)(2,1)S(1)}, u32[]{:S(2)}, u32[]{:S(2)}) collective-permute-start(bf16[2,4,64,256]{3,2,1,0:T(8,128)(2,1)S(1)} %fusion), channel_id=1, source_target_pairs={{0,130},{2,0},{128,2},{130,128},{1,131},{3,1},{129,3},{131,129},{4... | collective-permute-start | bytes 786440 | tf_op jit(solution)/shard_map/ppermute | solution.py:227
  36.5 0.1 fusion.1
  36.5 0.1 collective-permute-start.7
  36.6 0.1 fusion.2
  36.7 2.8 %collective-permute-start.4 = (bf16[2,4,64,256]{3,2,1,0:T(8,128)(2,1)S(1)}, bf16[2,4,64,256]{3,2,1,0:T(8,128)(2,1)S(1)}, u32[]{:S(2)}, u32[]{:S(2)}) collective-permute-start(bf16[2,4,64,256]{3,2,1,0:T(8,128)(2,1)S(1)} %fusion.2), channel_id=1, source_target_pairs={{0,96},{32,0},{64,32},{96,64},{1,97},{33,1},{65,33},{97,65},{2,98}... | collective-permute-start | bytes 786440 | tf_op jit(solution)/shard_map/ppermute | solution.py:227
  39.6 0.3 collective-permute-start.3
  39.8 1.3 %collective-permute-done.8.refs_9_ = bf16[2,4,64,256]{3,2,1,0:T(8,128)(2,1)S(1)} collective-permute-done((bf16[2,4,64,256]{3,2,1,0:T(8,128)(2,1)S(1)}, bf16[2,4,64,256]{3,2,1,0:T(8,128)(2,1)S(1)}, u32[]{:S(2)}, u32[]{:S(2)}) %collective-permute-start.8) | collective-permute-done | bytes 262176 | tf_op jit(solution)/shard_map/ppermute | solution.py:227
  41.1 3.0 %collective-permute-done.7.refs_8_ = bf16[2,4,64,256]{3,2,1,0:T(8,128)(2,1)S(1)} collective-permute-done((bf16[2,4,64,256]{3,2,1,0:T(8,128)(2,1)S(1)}, bf16[2,4,64,256]{3,2,1,0:T(8,128)(2,1)S(1)}, u32[]{:S(2)}, u32[]{:S(2)}) %collective-permute-start.7) | collective-permute-done | bytes 262176 | tf_op jit(solution)/shard_map/ppermute | solution.py:227
  44.1 2.9 %collective-permute-done.3.refs_3_ = bf16[2,4,64,256]{3,2,1,0:T(8,128)(2,1)S(1)} collective-permute-done((bf16[2,4,64,256]{3,2,1,0:T(8,128)(2,1)S(1)}, bf16[2,4,64,256]{3,2,1,0:T(8,128)(2,1)S(1)}, u32[]{:S(2)}, u32[]{:S(2)}) %collective-permute-start.3) | collective-permute-done | bytes 262176 | tf_op jit(solution)/shard_map/ppermute | solution.py:227
  47.1 0.9 shard_map.97
  48.0 1.3 %collective-permute-start.10 = (bf16[4,64,256]{2,1,0:T(8,128)(2,1)S(1)}, bf16[4,64,256]{2,1,0:T(8,128)(2,1)S(1)}, u32[]{:S(2)}, u32[]{:S(2)}) collective-permute-start(bf16[4,64,256]{2,1,0:T(8,128)(2,1)S(1)} %get-tuple-element.35), channel_id=1, source_target_pairs={{0,128},{2,130},{128,0},{130,2},{1,129},{3,131},{129,1},{131,3},{4... | collective-permute-start | bytes 393224 | tf_op jit(solution)/shard_map/ppermute | solution.py:227
  49.3 1.3 %collective-permute-start.11 = (bf16[4,64,256]{2,1,0:T(8,128)(2,1)S(1)}, bf16[4,64,256]{2,1,0:T(8,128)(2,1)S(1)}, u32[]{:S(2)}, u32[]{:S(2)}) collective-permute-start(bf16[4,64,256]{2,1,0:T(8,128)(2,1)S(1)} %get-tuple-element.36), channel_id=1, source_target_pairs={{0,130},{2,0},{128,2},{130,128},{1,131},{3,1},{129,3},{131,129},{4... | collective-permute-start | bytes 393224 | tf_op jit(solution)/shard_map/ppermute | solution.py:227
  50.6 1.1 %collective-permute-start.13 = (bf16[4,64,256]{2,1,0:T(8,128)(2,1)S(1)}, bf16[4,64,256]{2,1,0:T(8,128)(2,1)S(1)}, u32[]{:S(2)}, u32[]{:S(2)}) collective-permute-start(bf16[4,64,256]{2,1,0:T(8,128)(2,1)S(1)} %get-tuple-element.39), channel_id=1, source_target_pairs={{0,64},{32,96},{64,0},{96,32},{1,65},{33,97},{65,1},{97,33},{2,66}... | collective-permute-start | bytes 393224 | tf_op jit(solution)/shard_map/ppermute | solution.py:227
  51.7 1.5 %collective-permute-start.14 = (bf16[4,64,256]{2,1,0:T(8,128)(2,1)S(1)}, bf16[4,64,256]{2,1,0:T(8,128)(2,1)S(1)}, u32[]{:S(2)}, u32[]{:S(2)}) collective-permute-start(bf16[4,64,256]{2,1,0:T(8,128)(2,1)S(1)} %get-tuple-element.40), channel_id=1, source_target_pairs={{0,96},{32,0},{64,32},{96,64},{1,97},{33,1},{65,33},{97,65},{2,98}... | collective-permute-start | bytes 393224 | tf_op jit(solution)/shard_map/ppermute | solution.py:227
  53.2 0.2 collective-permute-done.10.refs_2_
  53.4 0.3 collective-permute-start.9
  53.7 1.1 collective-permute-done.11.refs_3_
  54.9 2.1 %collective-permute-done.12.refs_5_ = bf16[4,64,256]{2,1,0:T(8,128)(2,1)S(1)} collective-permute-done((bf16[4,64,256]{2,1,0:T(8,128)(2,1)S(1)}, bf16[4,64,256]{2,1,0:T(8,128)(2,1)S(1)}, u32[]{:S(2)}, u32[]{:S(2)}) %collective-permute-start.12) | collective-permute-done | bytes 131104 | tf_op jit(solution)/shard_map/ppermute | solution.py:227
  57.0 0.9 collective-permute-done.14.refs_7_
  57.9 0.8 collective-permute-done.9.refs_1_
  58.7 0.9 shard_map.98
  59.7 8.2 %all-to-all-start = ((f32[8,8,8,256]{3,2,1,0:T(8,128)}), f32[8,8,8,256]{3,2,1,0:T(8,128)S(1)}, u32[]{:S(2)}, u32[]{:S(2)}) async-start(f32[8,8,8,256]{3,2,1,0:T(8,128)} %shard_map.98), calls=%async_computation | async-start | bytes 1048576 | tf_op jit(solution)/shard_map/all_to_all | solution.py:248
  67.9 0.1 dynamic_slice.3
  68.0 0.6 gather_fusion
  68.7 0.6 fusion.4
  69.3 0.7 broadcast_add_fusion
  69.9 0.1 broadcast_subtract_fusion.1
  70.0 0.1 broadcast_subtract_fusion.below_ref
  70.1 9.9 %all-to-all-done.parts_ref = f32[8,8,8,256]{3,2,1,0:T(8,128)S(1)} async-done(((f32[8,8,8,256]{3,2,1,0:T(8,128)}), f32[8,8,8,256]{3,2,1,0:T(8,128)S(1)}, u32[]{:S(2)}, u32[]{:S(2)}) %all-to-all-start) | async-done | bytes 524320 | tf_op jit(solution)/shard_map/all_to_all | solution.py:248
  80.0 0.7 shard_map.99
  80.6 10.6 %all_to_all.15.cross_ref = bf16[8,8,256]{2,1,0:T(8,128)(2,1)S(1)} all-to-all(bf16[8,8,256]{2,1,0:T(8,128)(2,1)S(1)} %get-tuple-element.43), channel_id=1, replica_groups=mesh['xh'=2,'y'=4,'z'=8,'xl'=2,'core'=2] {'xh','y'}, dimensions={0} | all-to-all | bytes 65536 | tf_op jit(solution)/shard_map/all_to_all | solution.py:257
  91.3 0.1 shard_map.100
  91.4 20.2 %all_to_all.16 = f32[32,8,128]{2,1,0:T(8,128)S(1)} all-to-all(f32[32,8,128]{2,1,0:T(8,128)S(1)} %broadcast_in_dim.20), channel_id=1, replica_groups=mesh['xh'=2,'y'=4,'z'=8,'xl'=2,'core'=2] {'z','xl','core'}, dimensions={0} | all-to-all | bytes 262144 | tf_op jit(solution)/shard_map/all_to_all | solution.py:260
  111.7 0.6 slice_reduce_fusion
  (22 shorter events, 0.2 us)
Async XLA Ops:
  0.6 67.4 %copy-start = (f32[4000]{0:T(1024)S(1)}, f32[4000]{0:T(1024)}, u32[]{:S(2)}) copy-start(f32[4000]{0:T(1024)} %param.13) | copy-start | bytes 48004
  1.3 1.9 %copy-start.1 = (bf16[12,8,128,128]{3,2,1,0:T(8,128)(2,1)S(1)}, bf16[12,8,128,128]{3,2,1,0:T(8,128)(2,1)}, u32[]{:S(2)}) copy-start(bf16[12,8,128,128]{3,2,1,0:T(8,128)(2,1)} %three_ref.1) | copy-start | bytes 9437188
  3.2 1.9 %copy-start.2 = (bf16[6144,256]{1,0:T(8,128)(2,1)S(1)}, bf16[6144,256]{1,0:T(8,128)(2,1)}, u32[]{:S(2)}) copy-start(bf16[6144,256]{1,0:T(8,128)(2,1)} %coef_ref.1) | copy-start | bytes 9437188
  5.1 0.7 copy-start.3
  5.7 0.7 copy-start.4
  10.7 5.6 %collective-permute-start = (bf16[8,256,256]{2,1,0:T(8,128)(2,1)S(1)}, bf16[8,256,256]{2,1,0:T(8,128)(2,1)S(1)}, u32[]{:S(2)}, u32[]{:S(2)}) collective-permute-start(bf16[8,256,256]{2,1,0:T(8,128)(2,1)S(1)} %shard_map.95.own_ref), channel_id=1, source_target_pairs={{0,1},{1,0},{2,3},{3,2},{4,5},{5,4},{6,7},{7,6},{8,9},{9,8},{10,11... | collective-permute-start | bytes 3145736 | tf_op jit(solution)/shard_map/ppermute | solution.py:227
  21.1 13.2 %collective-permute-start.6 = (bf16[2,2,4,64,256]{4,3,2,1,0:T(8,128)(2,1)S(1)}, bf16[2,2,4,64,256]{4,3,2,1,0:T(8,128)(2,1)S(1)}, u32[]{:S(2)}, u32[]{:S(2)}) collective-permute-start(bf16[2,2,4,64,256]{4,3,2,1,0:T(8,128)(2,1)S(1)} %get-tuple-element.30), channel_id=1, source_target_pairs={{0,130},{2,0},{128,2},{130,128},{1,131},{3,1},{129,3},{131,129},{4... | collective-permute-start | bytes 1572872 | tf_op jit(solution)/shard_map/ppermute | solution.py:227
  21.9 14.5 %collective-permute-start.5 = (bf16[2,2,4,64,256]{4,3,2,1,0:T(8,128)(2,1)S(1)}, bf16[2,2,4,64,256]{4,3,2,1,0:T(8,128)(2,1)S(1)}, u32[]{:S(2)}, u32[]{:S(2)}) collective-permute-start(bf16[2,2,4,64,256]{4,3,2,1,0:T(8,128)(2,1)S(1)} %get-tuple-element.29), channel_id=1, source_target_pairs={{0,2},{2,128},{128,130},{130,0},{1,3},{3,129},{129,131},{131,1},{4... | collective-permute-start | bytes 1572872 | tf_op jit(solution)/shard_map/ppermute | solution.py:227
  22.7 13.9 %collective-permute-start.2 = (bf16[2,2,4,64,256]{4,3,2,1,0:T(8,128)(2,1)S(1)}, bf16[2,2,4,64,256]{4,3,2,1,0:T(8,128)(2,1)S(1)}, u32[]{:S(2)}, u32[]{:S(2)}) collective-permute-start(bf16[2,2,4,64,256]{4,3,2,1,0:T(8,128)(2,1)S(1)} %get-tuple-element.25), channel_id=1, source_target_pairs={{0,96},{32,0},{64,32},{96,64},{1,97},{33,1},{65,33},{97,65},{2,98}... | collective-permute-start | bytes 1572872 | tf_op jit(solution)/shard_map/ppermute | solution.py:227
  24.7 14.8 %collective-permute-start.1 = (bf16[2,2,4,64,256]{4,3,2,1,0:T(8,128)(2,1)S(1)}, bf16[2,2,4,64,256]{4,3,2,1,0:T(8,128)(2,1)S(1)}, u32[]{:S(2)}, u32[]{:S(2)}) collective-permute-start(bf16[2,2,4,64,256]{4,3,2,1,0:T(8,128)(2,1)S(1)} %get-tuple-element.24), channel_id=1, source_target_pairs={{0,32},{32,64},{64,96},{96,0},{1,33},{33,65},{65,97},{97,1},{2,34}... | collective-permute-start | bytes 1572872 | tf_op jit(solution)/shard_map/ppermute | solution.py:227
  34.4 6.7 %collective-permute-start.8 = (bf16[2,4,64,256]{3,2,1,0:T(8,128)(2,1)S(1)}, bf16[2,4,64,256]{3,2,1,0:T(8,128)(2,1)S(1)}, u32[]{:S(2)}, u32[]{:S(2)}) collective-permute-start(bf16[2,4,64,256]{3,2,1,0:T(8,128)(2,1)S(1)} %fusion), channel_id=1, source_target_pairs={{0,130},{2,0},{128,2},{130,128},{1,131},{3,1},{129,3},{131,129},{4... | collective-permute-start | bytes 786440 | tf_op jit(solution)/shard_map/ppermute | solution.py:227
  36.5 7.6 %collective-permute-start.7 = (bf16[2,4,64,256]{3,2,1,0:T(8,128)(2,1)S(1)}, bf16[2,4,64,256]{3,2,1,0:T(8,128)(2,1)S(1)}, u32[]{:S(2)}, u32[]{:S(2)}) collective-permute-start(bf16[2,4,64,256]{3,2,1,0:T(8,128)(2,1)S(1)} %fusion.1), channel_id=1, source_target_pairs={{0,2},{2,128},{128,130},{130,0},{1,3},{3,129},{129,131},{131,1},{4... | collective-permute-start | bytes 786440 | tf_op jit(solution)/shard_map/ppermute | solution.py:227
  36.7 7.4 %collective-permute-start.4 = (bf16[2,4,64,256]{3,2,1,0:T(8,128)(2,1)S(1)}, bf16[2,4,64,256]{3,2,1,0:T(8,128)(2,1)S(1)}, u32[]{:S(2)}, u32[]{:S(2)}) collective-permute-start(bf16[2,4,64,256]{3,2,1,0:T(8,128)(2,1)S(1)} %fusion.2), channel_id=1, source_target_pairs={{0,96},{32,0},{64,32},{96,64},{1,97},{33,1},{65,33},{97,65},{2,98}... | collective-permute-start | bytes 786440 | tf_op jit(solution)/shard_map/ppermute | solution.py:227
  39.6 7.5 %collective-permute-start.3 = (bf16[2,4,64,256]{3,2,1,0:T(8,128)(2,1)S(1)}, bf16[2,4,64,256]{3,2,1,0:T(8,128)(2,1)S(1)}, u32[]{:S(2)}, u32[]{:S(2)}) collective-permute-start(bf16[2,4,64,256]{3,2,1,0:T(8,128)(2,1)S(1)} %fusion.3), channel_id=1, source_target_pairs={{0,32},{32,64},{64,96},{96,0},{1,33},{33,65},{65,97},{97,1},{2,34}... | collective-permute-start | bytes 786440 | tf_op jit(solution)/shard_map/ppermute | solution.py:227
  47.1 20.8 %copy-start.5 = (s32[8]{0:T(128)S(1)}, s32[8]{0:T(128)}, u32[]{:S(2)}) copy-start(s32[8]{0:T(128)} %param.15) | copy-start | bytes 100
  47.1 20.9 %copy-start.6 = (f32[256]{0:T(256)S(1)}, f32[256]{0:T(256)}, u32[]{:S(2)}) copy-start(f32[256]{0:T(256)} %param.14) | copy-start | bytes 3076
  48.0 5.4 %collective-permute-start.10 = (bf16[4,64,256]{2,1,0:T(8,128)(2,1)S(1)}, bf16[4,64,256]{2,1,0:T(8,128)(2,1)S(1)}, u32[]{:S(2)}, u32[]{:S(2)}) collective-permute-start(bf16[4,64,256]{2,1,0:T(8,128)(2,1)S(1)} %get-tuple-element.35), channel_id=1, source_target_pairs={{0,128},{2,130},{128,0},{130,2},{1,129},{3,131},{129,1},{131,3},{4... | collective-permute-start | bytes 393224 | tf_op jit(solution)/shard_map/ppermute | solution.py:227
  49.3 5.6 %collective-permute-start.11 = (bf16[4,64,256]{2,1,0:T(8,128)(2,1)S(1)}, bf16[4,64,256]{2,1,0:T(8,128)(2,1)S(1)}, u32[]{:S(2)}, u32[]{:S(2)}) collective-permute-start(bf16[4,64,256]{2,1,0:T(8,128)(2,1)S(1)} %get-tuple-element.36), channel_id=1, source_target_pairs={{0,130},{2,0},{128,2},{130,128},{1,131},{3,1},{129,3},{131,129},{4... | collective-permute-start | bytes 393224 | tf_op jit(solution)/shard_map/ppermute | solution.py:227
  50.6 6.4 %collective-permute-start.12 = (bf16[4,64,256]{2,1,0:T(8,128)(2,1)S(1)}, bf16[4,64,256]{2,1,0:T(8,128)(2,1)S(1)}, u32[]{:S(2)}, u32[]{:S(2)}) collective-permute-start(bf16[4,64,256]{2,1,0:T(8,128)(2,1)S(1)} %get-tuple-element.38), channel_id=1, source_target_pairs={{0,32},{32,64},{64,96},{96,0},{1,33},{33,65},{65,97},{97,1},{2,34}... | collective-permute-start | bytes 393224 | tf_op jit(solution)/shard_map/ppermute | solution.py:227
  50.6 6.4 %collective-permute-start.13 = (bf16[4,64,256]{2,1,0:T(8,128)(2,1)S(1)}, bf16[4,64,256]{2,1,0:T(8,128)(2,1)S(1)}, u32[]{:S(2)}, u32[]{:S(2)}) collective-permute-start(bf16[4,64,256]{2,1,0:T(8,128)(2,1)S(1)} %get-tuple-element.39), channel_id=1, source_target_pairs={{0,64},{32,96},{64,0},{96,32},{1,65},{33,97},{65,1},{97,33},{2,66}... | collective-permute-start | bytes 393224 | tf_op jit(solution)/shard_map/ppermute | solution.py:227
  51.7 6.2 %collective-permute-start.14 = (bf16[4,64,256]{2,1,0:T(8,128)(2,1)S(1)}, bf16[4,64,256]{2,1,0:T(8,128)(2,1)S(1)}, u32[]{:S(2)}, u32[]{:S(2)}) collective-permute-start(bf16[4,64,256]{2,1,0:T(8,128)(2,1)S(1)} %get-tuple-element.40), channel_id=1, source_target_pairs={{0,96},{32,0},{64,32},{96,64},{1,97},{33,1},{65,33},{97,65},{2,98}... | collective-permute-start | bytes 393224 | tf_op jit(solution)/shard_map/ppermute | solution.py:227
  53.4 5.3 %collective-permute-start.9 = (bf16[4,64,256]{2,1,0:T(8,128)(2,1)S(1)}, bf16[4,64,256]{2,1,0:T(8,128)(2,1)S(1)}, u32[]{:S(2)}, u32[]{:S(2)}) collective-permute-start(bf16[4,64,256]{2,1,0:T(8,128)(2,1)S(1)} %get-tuple-element.34), channel_id=1, source_target_pairs={{0,2},{2,128},{128,130},{130,0},{1,3},{3,129},{129,131},{131,1},{4... | collective-permute-start | bytes 393224 | tf_op jit(solution)/shard_map/ppermute | solution.py:227
  59.7 20.3 %all-to-all-start = ((f32[8,8,8,256]{3,2,1,0:T(8,128)}), f32[8,8,8,256]{3,2,1,0:T(8,128)S(1)}, u32[]{:S(2)}, u32[]{:S(2)}) async-start(f32[8,8,8,256]{3,2,1,0:T(8,128)} %shard_map.98), calls=%async_computation | async-start | bytes 1048576 | tf_op jit(solution)/shard_map/all_to_all | solution.py:248

commit v2 on v1

v2 whole, which is shorter than its diff:
```python
import jax
import jax.numpy as jnp
from jax import lax
from jax.experimental import pallas as pl
from jax.experimental.pallas import tpu as pltpu
from jax.sharding import Mesh
from jax.sharding import PartitionSpec as P

F32 = jnp.float32
BF16 = jnp.bfloat16
OCC = 8
VIR = 256
SPAN = 128
SLOTS = 12
KINDS = 2
ROWS = 256
AUX = ("xh", "y")
BLK = ("z", "xl", "core")
X = ("xh", "xl")

VMEM = pl.BlockSpec(memory_space=pltpu.VMEM)
SMEM = pl.BlockSpec(memory_space=pltpu.SMEM)
HBM = pl.BlockSpec(memory_space=pltpu.HBM)


def params(mib):
    return pltpu.CompilerParams(vmem_limit_bytes=mib * 2**20)


def half_kernel(block_hbm, kind_hbm, live_hbm, three_ref, coef_ref, out_ref, block_ref, kind_ref, live_ref, three, coef, weights, sems):
    small = [
        pltpu.make_async_copy(here, there, sems.at[3 * SLOTS + i])
        for i, (here, there) in enumerate(((block_hbm, block_ref), (kind_hbm, kind_ref), (live_hbm, live_ref)))
    ]
    for copy in small:
        copy.start()
    large = []
    for half in range(2):
        for s in range(SLOTS):
            rows, columns = pl.ds(half * 4, 4), pl.ds(s * SPAN, SPAN)
            large.append(
                pltpu.make_async_copy(three_ref.at[s, rows], three.at[rows, :, columns], sems.at[(1 + half) * SLOTS + s])
            )
    for copy in large[:SLOTS]:
        copy.start()
    for copy in small:
        copy.wait()
    copies = []
    for s in range(SLOTS):
        first = pl.multiple_of(block_ref[s] * SPAN, SPAN)
        copies.append(pltpu.make_async_copy(coef_ref.at[pl.ds(first, SPAN)], coef.at[s], sems.at[s]))
        copies[s].start()
    for copy in large[SLOTS:]:
        copy.start()
    for s in range(SLOTS):
        copies[s].wait()
        values = coef[s]
        for k in range(KINDS):
            used = jnp.logical_and(kind_ref[s] == k, s < live_ref[0])
            weights[pl.ds(s * SPAN, SPAN), pl.ds(k * VIR, VIR)] = jnp.where(used, values, jnp.zeros_like(values))
    for half in range(2):
        for s in range(SLOTS):
            large[half * SLOTS + s].wait()
        left = three[pl.ds(half * 4, 4)].reshape(4 * SPAN, SLOTS * SPAN)
        done = jnp.dot(left, weights[...], preferred_element_type=F32).astype(BF16)
        for i in range(4):
            for k in range(KINDS):
                out_ref[half * 4 + i, pl.ds(k * SPAN, SPAN), :] = done[i * SPAN : (i + 1) * SPAN, k * VIR : (k + 1) * VIR]


def half_transform(slot_block, slot_aux, live_slots, three_center, vir_coef):
    return pl.pallas_call(
        half_kernel,
        out_shape=jax.ShapeDtypeStruct((OCC, ROWS, VIR), BF16),
        in_specs=[HBM] * 5,
        out_specs=VMEM,
        scratch_shapes=[
            pltpu.SMEM((SLOTS,), jnp.int32),
            pltpu.SMEM((SLOTS,), jnp.int32),
            pltpu.SMEM((1,), jnp.int32),
            pltpu.VMEM((OCC, SPAN, SLOTS * SPAN), BF16),
            pltpu.VMEM((SLOTS, SPAN, VIR), BF16),
            pltpu.VMEM((SLOTS * SPAN, KINDS * VIR), BF16),
            pltpu.SemaphoreType.DMA((3 * SLOTS + 3,)),
        ],
        compiler_params=params(24),
    )(slot_block, slot_aux, live_slots, three_center, vir_coef)


PLACES = {
    (2, 0): (0, 0), (1, 1): (0, 1), (2, 1): (1, 0), (3, 0): (1, 1),
    (1, 0): (2, None), (3, 1): (3, None), (0, 0): (4, 0), (0, 1): (4, 1),
}


def product(core, first_j, turned, own_ref, other_ref, done):
    for half in range(2):
        columns = pl.ds(pl.multiple_of(lax.rem(core + half, 2) * 128, 128), 128)
        for pair in range(2):
            j = first_j + 2 * pair
            right = jnp.concatenate(
                [jnp.concatenate([ref[j + i, :, columns] for ref in (own_ref, other_ref)], axis=0) for i in range(2)],
                axis=1,
            )
            whole = jnp.dot(turned[half], right, preferred_element_type=F32).astype(BF16)
            done[half, pair] = whole.reshape(OCC, 128, 256)


def tile(done, half, j, o, low):
    lane = lax.broadcasted_iota(jnp.int32, (64, 128), 1)
    columns = pl.ds(j % 2 * 128, 128)
    first, second = done[half, j // 2, o, 0:64, columns], done[half, j // 2, o, 64:128, columns]
    return jnp.where(lax.rem(lane // 64 + low, 2) == 0, first.astype(F32), second.astype(F32)).astype(BF16)


def along_y_kernel(place_ref, own_ref, other_ref, *rest):
    outs, turned, done = rest[:5], rest[5], rest[6]
    y, core = place_ref[1], place_ref[2]
    unit = (
        lax.broadcasted_iota(jnp.int32, (128, 128), 0) == lax.broadcasted_iota(jnp.int32, (128, 128), 1)
    ).astype(F32).astype(BF16)
    for o in range(OCC):
        for half in range(2):
            for i, ref in enumerate((own_ref, other_ref)):
                across = lax.dot_general(
                    unit, ref[o, :, half * 128 : half * 128 + 128], (((1,), (1,)), ((), ())), preferred_element_type=F32
                )
                turned[half, pl.ds(o * 128, 128), pl.ds(i * ROWS, ROWS)] = across.astype(BF16)
    product(core, 0, turned, own_ref, other_ref, done)
    for d in range(4):
        for h in range(2):
            which, at = PLACES[d, h]
            for u in range(2):
                for j in range(4):
                    for half in range(2):
                        part = tile(done, half, j, h * 4 + lax.rem(y + d, 4), u)
                        if at is None:
                            outs[which][u, j, half] = part
                        else:
                            outs[which][at, u, j, half] = part


def along_x_kernel(place_ref, own_ref, other_ref, turned, *rest):
    outs, done = rest[:5], rest[5]
    x, core = place_ref[0], place_ref[2]
    product(core, 4, turned, own_ref, other_ref, done)
    for d in range(4):
        to = lax.rem(x + d, 4)
        for h in range(2):
            which, at = PLACES[d, h]
            for u in range(2):
                for j in range(4):
                    for half in range(2):
                        part = tile(done, half, j, to // 2 * 4 + h * 2 + u, lax.rem(to, 2))
                        if at is None:
                            outs[which][u, j, half] = part
                        else:
                            outs[which][at, u, j, half] = part


PART = (4, 2, 64, 128)


def partial(place, own, other):
    pair = jax.ShapeDtypeStruct((2, 2) + PART, BF16)
    single = jax.ShapeDtypeStruct((2,) + PART, BF16)
    outs = [pair, pair, single, single, pair]
    done = pltpu.VMEM((2, 2, OCC, 128, 256), BF16)
    *first, turned = pl.pallas_call(
        along_y_kernel,
        out_shape=outs + [jax.ShapeDtypeStruct((2, OCC * 128, 2 * ROWS), BF16)],
        in_specs=[SMEM, VMEM, VMEM],
        out_specs=[VMEM] * 6,
        scratch_shapes=[done],
        compiler_params=params(32),
    )(place, own, other)
    second = pl.pallas_call(
        along_x_kernel,
        out_shape=outs,
        in_specs=[SMEM, VMEM, VMEM, VMEM],
        out_specs=[VMEM] * 5,
        scratch_shapes=[done],
        compiler_params=params(32),
    )(place, own, other, turned)
    return first, second


def first_sum_kernel(place_ref, own, from_back, from_ahead, last_back, last_ahead, *rest, at):
    outs, kept = rest[:4], rest[4]
    for h, (one, two) in enumerate(((from_ahead, last_back), (from_back, last_ahead))):
        for u in range(2):
            total = own[h, u].astype(F32) + one[1, u].astype(F32) + two[u].astype(F32)
            kept[h * 2 + u] = total.astype(BF16)
    for d in range(4):
        outs[d][...] = kept[lax.rem(place_ref[at] + d, 4)]


def first_sum(place, at, ins):
    def kernel(*refs):
        first_sum_kernel(*refs, at=at)

    return pl.pallas_call(
        kernel,
        out_shape=[jax.ShapeDtypeStruct(PART, BF16)] * 4,
        in_specs=[SMEM] + [VMEM] * 5,
        out_specs=[VMEM] * 4,
        scratch_shapes=[pltpu.VMEM((4,) + PART, BF16)],
        compiler_params=params(16),
    )(place, *ins)


def second_sum_kernel(*refs):
    ins, out = refs[:8], refs[8]
    for half in range(2):
        total = ins[half * 4][...].astype(F32)
        for d in range(1, 4):
            total = total + ins[half * 4 + d][...].astype(F32)
        out[pl.ds(half * 4, 4)] = total


def second_sum(ins):
    return pl.pallas_call(
        second_sum_kernel,
        out_shape=jax.ShapeDtypeStruct((OCC, 2, 64, 128), F32),
        in_specs=[VMEM] * 8,
        out_specs=VMEM,
        compiler_params=params(16),
    )(*ins)


def finish_kernel(place_ref, parts_ref, below_ref, out_ref):
    core, low = place_ref[2], place_ref[3]
    total = parts_ref[0]
    for z in range(1, 8):
        total = total + parts_ref[z]
    across = [total[half].T for half in range(2)]
    crossed = []
    for half in range(2):
        source = jnp.where(core == 0, across[half], across[1 - half])
        same = jnp.concatenate([source[0:64], source[64:128]], axis=1)
        other = jnp.concatenate([source[64:128], source[0:64]], axis=1)
        crossed.append(jnp.where(low == 0, same, other))
    amplitudes = [total[half] / below_ref[half] for half in range(2)]
    terms = [amplitudes[half] * (2.0 * total[half] - crossed[half]) for half in range(2)]
    energy = jnp.sum(terms[0] + terms[1], axis=(0, 1), keepdims=True)
    lane = lax.broadcasted_iota(jnp.int32, (64, 128), 1)
    quarter = lax.rem(lane // 64 + low, 2)
    for half in range(2):
        for q in range(2):
            sent = jnp.where(quarter == q, amplitudes[half], jnp.broadcast_to(energy, (64, 128)))
            out_ref[pl.ds(half * 16 + q * 8, 8)] = sent.reshape(8, 8, 128)


def finish(place, parts, below):
    return pl.pallas_call(
        finish_kernel,
        out_shape=jax.ShapeDtypeStruct((32, 8, 128), F32),
        in_specs=[SMEM, VMEM, VMEM],
        out_specs=VMEM,
        compiler_params=params(16),
    )(place, parts, below)


def collect_kernel(place_ref, parts_ref, amp_ref, pair_ref):
    block = place_ref[4]
    half, quarter = block // 16, lax.rem(block // 8, 2)
    lane = lax.broadcasted_iota(jnp.int32, (8, 128), 1)
    ours = lane // 64 == quarter
    energies = jnp.zeros((8, 128), F32)
    for j in range(OCC):
        rest = jnp.zeros((8, 128), F32)
        for side in range(2):
            core = lax.rem(half + side, 2)
            one, two = parts_ref[j * 4 + core], parts_ref[j * 4 + 2 + core]
            amp = jnp.where(ours, one, two)
            rest = rest + jnp.where(ours, two, one)
            for r in range(8):
                amp_ref[r, pl.ds(j, 1), pl.ds(side * 128, 128)] = amp[r : r + 1, :]
        total = rest[:, 0:1] + rest[:, 64:65]
        energies = jnp.where(lane == j, jnp.broadcast_to(total, (8, 128)), energies)
    pair_ref[...] = energies[0:1, 0:OCC]


def collect(place, parts):
    return pl.pallas_call(
        collect_kernel,
        out_shape=[jax.ShapeDtypeStruct((8, OCC, VIR), F32), jax.ShapeDtypeStruct((1, OCC), F32)],
        in_specs=[SMEM, VMEM],
        out_specs=[VMEM, VMEM],
        compiler_params=params(16),
    )(place, parts)


def moved(x, axis, by):
    n = lax.axis_size(axis)
    return lax.ppermute(x, axis, [(i, (i + by) % n) for i in range(n)])


def denominators(eps_occ, eps_vir, occ_index, core, low):
    levels = jnp.take(eps_occ, occ_index)
    own = jnp.sum(jnp.where(jnp.arange(OCC) == lax.axis_index(AUX), levels, 0.0))
    other = jnp.sum(jnp.where(jnp.arange(OCC) == lax.axis_index("z"), levels, 0.0))
    quarters = eps_vir.reshape(2, 2, 64, 1)
    of_rows = jnp.where((jnp.arange(128) // 64 + low) % 2 == 0, quarters[:, 0], quarters[:, 1])
    halves = eps_vir.reshape(2, 1, 128)
    of_columns = jnp.where(core == 0, halves, halves[::-1])
    return own + other - of_rows - of_columns


def body(three_center, slot_block, slot_aux, live_slots, vir_coef, eps_occ, eps_vir, occ_index):
    x, y, core, low = lax.axis_index(X), lax.axis_index("y"), lax.axis_index("core"), lax.axis_index("xl")
    place = jnp.stack([x, y, core, low, lax.axis_index(BLK)]).astype(jnp.int32)
    own = half_transform(slot_block, slot_aux, live_slots, three_center, vir_coef)
    other = moved(own, "core", 1)
    below = denominators(eps_occ, eps_vir, occ_index, core, low)

    got = []
    for axis, (ahead, back, one, minus, mine) in zip(("y", X), partial(place, own, other)):
        got.append((axis, moved(ahead, axis, 1), moved(back, axis, -1), one, minus, mine))
    ins = []
    for at, (axis, from_back, from_ahead, one, minus, mine) in enumerate(got):
        one = (one.astype(F32) + from_back[0].astype(F32)).astype(BF16)
        minus = (minus.astype(F32) + from_ahead[0].astype(F32)).astype(BF16)
        last = moved(one, axis, 1), moved(minus, axis, -1)
        group = first_sum(place, at, (mine, from_back, from_ahead, *last))
        ins += [group[0]] + [moved(group[d], (X, "y")[at], d) for d in range(1, 4)]
    parts = lax.all_to_all(second_sum(ins), "z", 0, 0, tiled=True)
    sent = finish(place, parts, below)
    amplitudes, pair = collect(place, lax.all_to_all(sent, BLK, 0, 0, tiled=True))
    return amplitudes[None], pair


def solution(mesh):
    fine = Mesh(mesh.devices.reshape(2, 4, 8, 2, 2), ("xh", "y", "z", "xl", "core"))
    every = AUX + BLK
    in_specs = (P(every, None, None, None), P(every), P(every), P(every), P(), P(), P(), P())
    out_specs = (P(AUX, BLK, None, None), P(AUX, None))
    return jax.shard_map(body, mesh=fine, in_specs=in_specs, out_specs=out_specs, check_vma=False)
```

time: 113 us -> 96.5 us (0.85)
  blocking collectives: 30.9 us -> 18.6 us
  waiting for transfers between devices: 34.2 us -> 25.3 us
  starting transfers between devices: 25.8 us -> 28.3 us
  Pallas kernels: 11.7 us -> 14.1 us
  between operations: 1.45 us -> 2.8 us
    all_to_all x2 -> x1, blocking collectives: 30.9 us -> 18.6 us  [body(): lax.all_to_all(sent, BLK, 0, 0, tiled=True)]
    ppermute x15, waiting for transfers between devices: 24.3 us -> 16.1 us  [moved(): return lax.ppermute(x, axis, [(i, (i + by) % n) for i in range(n)])]
    ppermute x15, starting transfers between devices: 17.6 us -> 21.8 us  [moved(): return lax.ppermute(x, axis, [(i, (i + by) % n) for i in range(n)])]
    pallas_call x5 -> x7, Pallas kernels: 7.43 us -> 9.65 us  [the longest x1 2.66 us: partial(): pl.pallas_call(along_y_kernel, out_shape=outs + [jax.ShapeDtypeStruct((2,...]
    all_to_all x1, starting transfers between devices: 8.21 us -> 6.55 us  [body(): parts = lax.all_to_all(second_sum(ins), 'z', 0, 0, tiled=True)]
  transfers between devices with their start and end apart: 16 -> 16, of which waited for: 11 -> 8; matrix products, arithmetic and copies ran while one was open for 2% -> 2% of each run, Pallas kernels for 0% -> 4%
where the time goes in v2:
time: 96.5 us; the launch traced here: 96.1 us
  starting transfers between devices  28.3 us (29%)
  waiting for transfers between devices  25.3 us (26%)
  blocking collectives  18.6 us (19%)
  Pallas kernels  14.1 us (15%)
  local copies, waits for them, and re-layouts  5.93 us (6%)
  between operations  2.8 us (3%)
  other arithmetic  1.11 us (1%)
    ppermute x15, starting transfers between devices, moved(): return lax.ppermute(x, axis, [(i, (i + by) % n) for i in range(n)])  21.8 us
    all_to_all x1, blocking collectives, body(): lax.all_to_all(sent, BLK, 0, 0, tiled=True)  18.6 us
    ppermute x15, waiting for transfers between devices, moved(): return lax.ppermute(x, axis, [(i, (i + by) % n) for i in range(n)])  16.1 us
    all_to_all x1, waiting for transfers between devices, body(): parts = lax.all_to_all(second_sum(ins), 'z', 0, 0, tiled=True)  9.25 us
    all_to_all x1, starting transfers between devices, body(): parts = lax.all_to_all(second_sum(ins), 'z', 0, 0, tiled=True)  6.55 us
    unnamed x14, local copies, waits for them, and re-layouts  5.1 us
    pallas_call x1, Pallas kernels, half_transform(): pl.pallas_call(half_kernel, out_shape=jax.ShapeDtypeStruct((OCC, ROWS, VI...  4.42 us
    pallas_call x1, Pallas kernels, partial(): pl.pallas_call(along_y_kernel, out_shape=outs + [jax.ShapeDtypeStruct((2,...  2.66 us
  transfers between devices with their start and end apart: 16, of which 8 were waited for; matrix products, arithmetic and copies ran while one was open for 2% of the time, Pallas kernels for 4%

profile of v2, /device:TPU:1, one launch (start us, length us, event | category | flops | bytes accessed | tf_op | source)
XLA Modules:
  0.0 96.1 jit_solution(1515691817963204063)
XLA Ops:
  0.6 0.0 copy-start
  1.3 1.9 %copy-done.1 = bf16[12,8,128,128]{3,2,1,0:T(8,128)(2,1)S(1)} copy-done((bf16[12,8,128,128]{3,2,1,0:T(8,128)(2,1)S(1)}, bf16[12,8,128,128]{3,2,1,0:T(8,128)(2,1)}, u32[]{:S(2)}) %copy-start.1) | copy-done | bytes 3145752
  3.2 1.9 %copy-done.2 = bf16[6144,256]{1,0:T(8,128)(2,1)S(1)} copy-done((bf16[6144,256]{1,0:T(8,128)(2,1)S(1)}, bf16[6144,256]{1,0:T(8,128)(2,1)}, u32[]{:S(2)}) %copy-start.2) | copy-done | bytes 3145752
  5.1 0.7 copy-done.3
  5.7 0.7 copy-done.4
  6.4 4.4 %shard_map.95.own_ref = bf16[8,256,256]{2,1,0:T(8,128)(2,1)S(1)} custom-call(s32[12]{0:T(128)S(1)} %copy-done.3, s32[12]{0:T(128)S(1)} %copy-done.4, s32[1]{0:T(128)S(6)} %copy.10.live_hbm, bf16[12,8,128,128]{3,2,1,0:T(8,128)(2,1)S(1)} %copy-done.1, bf16[6144,256]{1,0:T(8,128)(2,1)S(1)} %copy-done.2), custom_call_target="tpu_custom_call" | custom-call | tf_op jit(solution)/shard_map/pallas_call | solution.py:72
  10.8 3.3 %collective-permute-start = (bf16[8,256,256]{2,1,0:T(8,128)(2,1)S(1)}, bf16[8,256,256]{2,1,0:T(8,128)(2,1)S(1)}, u32[]{:S(2)}, u32[]{:S(2)}) collective-permute-start(bf16[8,256,256]{2,1,0:T(8,128)(2,1)S(1)} %shard_map.95.own_ref), channel_id=1, source_target_pairs={{0,1},{1,0},{2,3},{3,2},{4,5},{5,4},{6,7},{7,6},{8,9},{9,8},{10,11... | collective-permute-start | bytes 3145736 | tf_op jit(solution)/shard_map/ppermute | solution.py:296
  14.2 0.1 stack.23.place_ref.refs_0_
  14.2 2.2 %collective-permute-done.other_ref = bf16[8,256,256]{2,1,0:T(8,128)(2,1)S(1)} collective-permute-done((bf16[8,256,256]{2,1,0:T(8,128)(2,1)S(1)}, bf16[8,256,256]{2,1,0:T(8,128)(2,1)S(1)}, u32[]{:S(2)}, u32[]{:S(2)}) %collective-permute-start) | collective-permute-done | bytes 1048608 | tf_op jit(solution)/shard_map/ppermute | solution.py:296
  16.4 2.7 %shard_map.96 = (bf16[2,2,4,2,64,128]{5,4,3,2,1,0:T(8,128)(2,1)S(1)}, bf16[2,2,4,2,64,128]{5,4,3,2,1,0:T(8,128)(2,1)S(1)}, bf16[2,4,2,64,128]{4,3,2,1,0:T(8,128)...) custom-call(s32[5]{0:T(128)S(1)} %stack.23.place_ref.refs_0_, ...), custom_call_target="tpu_custom_call" | custom-call | tf_op jit(solution)/shard_map/pallas_call | solution.py:169
  19.1 0.1 collective-permute-start.1
  19.2 2.7 %collective-permute-start.2 = (bf16[2,2,4,2,64,128]{5,4,3,2,1,0:T(8,128)(2,1)S(1)}, bf16[2,2,4,2,64,128]{5,4,3,2,1,0:T(8,128)(2,1)S(1)}, u32[]{:S(2)}, u32[]{:S(2)}) collective-permute-start(bf16[2,2,4,2,64,128]{5,4,3,2,1,0:T(8,128)(2,1)S(1)} %get-tuple-element.25), channel_id=1, source_target_pairs={{0,96},{32,0},{64,32},{96,64},{1,97},{33,1},{65,33},{97,65},{2,98}... | collective-permute-start | bytes 1572872 | tf_op jit(solution)/shard_map/ppermute | solution.py:296
  21.9 2.3 %shard_map.98 = (bf16[2,2,4,2,64,128]{5,4,3,2,1,0:T(8,128)(2,1)S(1)}, bf16[2,2,4,2,64,128]{5,4,3,2,1,0:T(8,128)(2,1)S(1)}, bf16[2,4,2,64,128]{4,3,2,1,0:T(8,128)...) custom-call(s32[5]{0:T(128)S(1)} %stack.23.place_ref.refs_0_, ...), custom_call_target="tpu_custom_call" | custom-call | tf_op jit(solution)/shard_map/pallas_call | solution.py:177
  24.2 0.1 collective-permute-start.8
  24.2 2.7 %collective-permute-start.9 = (bf16[2,2,4,2,64,128]{5,4,3,2,1,0:T(8,128)(2,1)S(1)}, bf16[2,2,4,2,64,128]{5,4,3,2,1,0:T(8,128)(2,1)S(1)}, u32[]{:S(2)}, u32[]{:S(2)}) collective-permute-start(bf16[2,2,4,2,64,128]{5,4,3,2,1,0:T(8,128)(2,1)S(1)} %get-tuple-element.35), channel_id=1, source_target_pairs={{0,130},{2,0},{128,2},{130,128},{1,131},{3,1},{129,3},{131,129},{4... | collective-permute-start | bytes 1572872 | tf_op jit(solution)/shard_map/ppermute | solution.py:296
  26.9 6.6 %collective-permute-done.1.refs_2_ = bf16[2,2,4,2,64,128]{5,4,3,2,1,0:T(8,128)(2,1)S(1)} collective-permute-done((bf16[2,2,4,2,64,128]{5,4,3,2,1,0:T(8,128)(2,1)S(1)}, bf16[2,2,4,2,64,128]{5,4,3,2,1,0:T(8,128)(2,1)S(1)}, u32[]{:S(2)}, u32[]{:S(2)}) %collective-permute-start.1) | collective-permute-done | bytes 524320 | tf_op jit(solution)/shard_map/ppermute | solution.py:296
  33.5 0.1 fusion.3
  33.6 0.1 collective-permute-start.3
  33.7 0.0 copy-start.6
  33.7 0.1 fusion.2
  33.8 2.7 %collective-permute-start.4 = (bf16[2,4,2,64,128]{4,3,2,1,0:T(8,128)(2,1)S(1)}, bf16[2,4,2,64,128]{4,3,2,1,0:T(8,128)(2,1)S(1)}, u32[]{:S(2)}, u32[]{:S(2)}) collective-permute-start(bf16[2,4,2,64,128]{4,3,2,1,0:T(8,128)(2,1)S(1)} %fusion.2), channel_id=1, source_target_pairs={{0,96},{32,0},{64,32},{96,64},{1,97},{33,1},{65,33},{97,65},{2,98}... | collective-permute-start | bytes 786440 | tf_op jit(solution)/shard_map/ppermute | solution.py:296
  36.5 1.4 %collective-permute-done.8.refs_2_ = bf16[2,2,4,2,64,128]{5,4,3,2,1,0:T(8,128)(2,1)S(1)} collective-permute-done((bf16[2,2,4,2,64,128]{5,4,3,2,1,0:T(8,128)(2,1)S(1)}, bf16[2,2,4,2,64,128]{5,4,3,2,1,0:T(8,128)(2,1)S(1)}, u32[]{:S(2)}, u32[]{:S(2)}) %collective-permute-start.8) | collective-permute-done | bytes 524320 | tf_op jit(solution)/shard_map/ppermute | solution.py:296
  37.9 0.1 fusion.1
  38.0 0.1 collective-permute-start.10
  38.1 0.0 collective-permute-done.9.refs_3_
  38.1 0.1 fusion
  38.2 2.9 %collective-permute-start.11 = (bf16[2,4,2,64,128]{4,3,2,1,0:T(8,128)(2,1)S(1)}, bf16[2,4,2,64,128]{4,3,2,1,0:T(8,128)(2,1)S(1)}, u32[]{:S(2)}, u32[]{:S(2)}) collective-permute-start(bf16[2,4,2,64,128]{4,3,2,1,0:T(8,128)(2,1)S(1)} %fusion), channel_id=1, source_target_pairs={{0,130},{2,0},{128,2},{130,128},{1,131},{3,1},{129,3},{131,129},{4... | collective-permute-start | bytes 786440 | tf_op jit(solution)/shard_map/ppermute | solution.py:296
  41.1 0.4 collective-permute-done.3.refs_4_
  41.5 0.8 shard_map.97
  42.3 0.1 collective-permute-start.5
  42.4 2.1 %collective-permute-start.6 = (bf16[4,2,64,128]{3,2,1,0:T(8,128)(2,1)S(1)}, bf16[4,2,64,128]{3,2,1,0:T(8,128)(2,1)S(1)}, u32[]{:S(2)}, u32[]{:S(2)}) collective-permute-start(bf16[4,2,64,128]{3,2,1,0:T(8,128)(2,1)S(1)} %get-tuple-element.30), channel_id=1, source_target_pairs={{0,128},{2,130},{128,0},{130,2},{1,129},{3,131},{129,1},{131,3},{4... | collective-permute-start | bytes 393224 | tf_op jit(solution)/shard_map/ppermute | solution.py:296
  44.6 1.1 %collective-permute-start.7 = (bf16[4,2,64,128]{3,2,1,0:T(8,128)(2,1)S(1)}, bf16[4,2,64,128]{3,2,1,0:T(8,128)(2,1)S(1)}, u32[]{:S(2)}, u32[]{:S(2)}) collective-permute-start(bf16[4,2,64,128]{3,2,1,0:T(8,128)(2,1)S(1)} %get-tuple-element.31), channel_id=1, source_target_pairs={{0,130},{2,0},{128,2},{130,128},{1,131},{3,1},{129,3},{131,129},{4... | collective-permute-start | bytes 393224 | tf_op jit(solution)/shard_map/ppermute | solution.py:296
  45.7 0.8 shard_map.99
  46.6 0.1 collective-permute-start.12
  46.7 3.7 %collective-permute-start.13 = (bf16[4,2,64,128]{3,2,1,0:T(8,128)(2,1)S(1)}, bf16[4,2,64,128]{3,2,1,0:T(8,128)(2,1)S(1)}, u32[]{:S(2)}, u32[]{:S(2)}) collective-permute-start(bf16[4,2,64,128]{3,2,1,0:T(8,128)(2,1)S(1)} %get-tuple-element.40), channel_id=1, source_target_pairs={{0,64},{32,96},{64,0},{96,32},{1,65},{33,97},{65,1},{97,33},{2,66}... | collective-permute-start | bytes 393224 | tf_op jit(solution)/shard_map/ppermute | solution.py:296
  50.4 1.6 %collective-permute-done.5.refs_1_ = bf16[4,2,64,128]{3,2,1,0:T(8,128)(2,1)S(1)} collective-permute-done((bf16[4,2,64,128]{3,2,1,0:T(8,128)(2,1)S(1)}, bf16[4,2,64,128]{3,2,1,0:T(8,128)(2,1)S(1)}, u32[]{:S(2)}, u32[]{:S(2)}) %collective-permute-start.5) | collective-permute-done | bytes 131104 | tf_op jit(solution)/shard_map/ppermute | solution.py:296
  52.1 2.1 %collective-permute-done.13.refs_6_ = bf16[4,2,64,128]{3,2,1,0:T(8,128)(2,1)S(1)} collective-permute-done((bf16[4,2,64,128]{3,2,1,0:T(8,128)(2,1)S(1)}, bf16[4,2,64,128]{3,2,1,0:T(8,128)(2,1)S(1)}, u32[]{:S(2)}, u32[]{:S(2)}) %collective-permute-start.13) | collective-permute-done | bytes 131104 | tf_op jit(solution)/shard_map/ppermute | solution.py:296
  54.1 1.7 %collective-permute-done.14.refs_7_ = bf16[4,2,64,128]{3,2,1,0:T(8,128)(2,1)S(1)} collective-permute-done((bf16[4,2,64,128]{3,2,1,0:T(8,128)(2,1)S(1)}, bf16[4,2,64,128]{3,2,1,0:T(8,128)(2,1)S(1)}, u32[]{:S(2)}, u32[]{:S(2)}) %collective-permute-start.14) | collective-permute-done | bytes 131104 | tf_op jit(solution)/shard_map/ppermute | solution.py:296
  55.8 0.9 shard_map.100
  56.8 6.5 %all-to-all-start = ((f32[8,2,64,128]{3,2,1,0:T(8,128)}), f32[8,2,64,128]{3,2,1,0:T(8,128)S(1)}, u32[]{:S(2)}, u32[]{:S(2)}) async-start(f32[8,2,64,128]{3,2,1,0:T(8,128)} %shard_map.100), calls=%async_computation | async-start | bytes 1048576 | tf_op jit(solution)/shard_map/all_to_all | solution.py:327
  63.3 0.1 reshape.25
  63.4 0.6 gather_fusion
  64.1 0.7 fusion.6
  66.1 0.1 subtract_subtract_fusion.below_ref
  66.2 9.2 %all-to-all-done.parts_ref = f32[8,2,64,128]{3,2,1,0:T(8,128)S(1)} async-done(((f32[8,2,64,128]{3,2,1,0:T(8,128)}), f32[8,2,64,128]{3,2,1,0:T(8,128)S(1)}, u32[]{:S(2)}, u32[]{:S(2)}) %all-to-all-start) | async-done | bytes 524320 | tf_op jit(solution)/shard_map/all_to_all | solution.py:327
  75.4 0.9 shard_map.101
  76.3 18.6 %all_to_all.10.parts_ref = f32[32,8,128]{2,1,0:T(8,128)S(1)} all-to-all(f32[32,8,128]{2,1,0:T(8,128)S(1)} %shard_map.101), channel_id=1, replica_groups=mesh['xh'=2,'y'=4,'z'=8,'xl'=2,'core'=2] {'z','xl','core'}, dimensions={0} | all-to-all | bytes 262144 | tf_op jit(solution)/shard_map/all_to_all | solution.py:329
  94.9 1.2 %shard_map.102 = (f32[8,8,256]{2,1,0:T(8,128)}, f32[1,8]{1,0:T(1,128)}) custom-call(s32[5]{0:T(128)S(1)} %stack.23.place_ref.refs_0_, f32[32,8,128]{2,1,0:T(8,128)S(1)} %all_to_all.10.parts_ref), custom_call_target="tpu_custom_call" | custom-call | tf_op jit(solution)/shard_map/pallas_call | solution.py:285
  (22 shorter events, 0.1 us)
Async XLA Ops:
  0.6 62.8 %copy-start = (f32[4000]{0:T(1024)S(1)}, f32[4000]{0:T(1024)}, u32[]{:S(2)}) copy-start(f32[4000]{0:T(1024)} %param.13) | copy-start | bytes 48004
  1.3 1.9 %copy-start.1 = (bf16[12,8,128,128]{3,2,1,0:T(8,128)(2,1)S(1)}, bf16[12,8,128,128]{3,2,1,0:T(8,128)(2,1)}, u32[]{:S(2)}) copy-start(bf16[12,8,128,128]{3,2,1,0:T(8,128)(2,1)} %three_ref.1) | copy-start | bytes 9437188
  3.2 1.9 %copy-start.2 = (bf16[6144,256]{1,0:T(8,128)(2,1)S(1)}, bf16[6144,256]{1,0:T(8,128)(2,1)}, u32[]{:S(2)}) copy-start(bf16[6144,256]{1,0:T(8,128)(2,1)} %coef_ref.1) | copy-start | bytes 9437188
  5.1 0.7 copy-start.3
  5.7 0.7 copy-start.4
  10.8 5.6 %collective-permute-start = (bf16[8,256,256]{2,1,0:T(8,128)(2,1)S(1)}, bf16[8,256,256]{2,1,0:T(8,128)(2,1)S(1)}, u32[]{:S(2)}, u32[]{:S(2)}) collective-permute-start(bf16[8,256,256]{2,1,0:T(8,128)(2,1)S(1)} %shard_map.95.own_ref), channel_id=1, source_target_pairs={{0,1},{1,0},{2,3},{3,2},{4,5},{5,4},{6,7},{7,6},{8,9},{9,8},{10,11... | collective-permute-start | bytes 3145736 | tf_op jit(solution)/shard_map/ppermute | solution.py:296
  19.1 14.4 %collective-permute-start.1 = (bf16[2,2,4,2,64,128]{5,4,3,2,1,0:T(8,128)(2,1)S(1)}, bf16[2,2,4,2,64,128]{5,4,3,2,1,0:T(8,128)(2,1)S(1)}, u32[]{:S(2)}, u32[]{:S(2)}) collective-permute-start(bf16[2,2,4,2,64,128]{5,4,3,2,1,0:T(8,128)(2,1)S(1)} %get-tuple-element.24), channel_id=1, source_target_pairs={{0,32},{32,64},{64,96},{96,0},{1,33},{33,65},{65,97},{97,1},{2,34}... | collective-permute-start | bytes 1572872 | tf_op jit(solution)/shard_map/ppermute | solution.py:296
  19.2 14.5 %collective-permute-start.2 = (bf16[2,2,4,2,64,128]{5,4,3,2,1,0:T(8,128)(2,1)S(1)}, bf16[2,2,4,2,64,128]{5,4,3,2,1,0:T(8,128)(2,1)S(1)}, u32[]{:S(2)}, u32[]{:S(2)}) collective-permute-start(bf16[2,2,4,2,64,128]{5,4,3,2,1,0:T(8,128)(2,1)S(1)} %get-tuple-element.25), channel_id=1, source_target_pairs={{0,96},{32,0},{64,32},{96,64},{1,97},{33,1},{65,33},{97,65},{2,98}... | collective-permute-start | bytes 1572872 | tf_op jit(solution)/shard_map/ppermute | solution.py:296
  24.2 13.8 %collective-permute-start.8 = (bf16[2,2,4,2,64,128]{5,4,3,2,1,0:T(8,128)(2,1)S(1)}, bf16[2,2,4,2,64,128]{5,4,3,2,1,0:T(8,128)(2,1)S(1)}, u32[]{:S(2)}, u32[]{:S(2)}) collective-permute-start(bf16[2,2,4,2,64,128]{5,4,3,2,1,0:T(8,128)(2,1)S(1)} %get-tuple-element.34), channel_id=1, source_target_pairs={{0,2},{2,128},{128,130},{130,0},{1,3},{3,129},{129,131},{131,1},{4... | collective-permute-start | bytes 1572872 | tf_op jit(solution)/shard_map/ppermute | solution.py:296
  24.2 13.9 %collective-permute-start.9 = (bf16[2,2,4,2,64,128]{5,4,3,2,1,0:T(8,128)(2,1)S(1)}, bf16[2,2,4,2,64,128]{5,4,3,2,1,0:T(8,128)(2,1)S(1)}, u32[]{:S(2)}, u32[]{:S(2)}) collective-permute-start(bf16[2,2,4,2,64,128]{5,4,3,2,1,0:T(8,128)(2,1)S(1)} %get-tuple-element.35), channel_id=1, source_target_pairs={{0,130},{2,0},{128,2},{130,128},{1,131},{3,1},{129,3},{131,129},{4... | collective-permute-start | bytes 1572872 | tf_op jit(solution)/shard_map/ppermute | solution.py:296
  33.6 7.9 %collective-permute-start.3 = (bf16[2,4,2,64,128]{4,3,2,1,0:T(8,128)(2,1)S(1)}, bf16[2,4,2,64,128]{4,3,2,1,0:T(8,128)(2,1)S(1)}, u32[]{:S(2)}, u32[]{:S(2)}) collective-permute-start(bf16[2,4,2,64,128]{4,3,2,1,0:T(8,128)(2,1)S(1)} %fusion.3), channel_id=1, source_target_pairs={{0,32},{32,64},{64,96},{96,0},{1,33},{33,65},{65,97},{97,1},{2,34}... | collective-permute-start | bytes 786440 | tf_op jit(solution)/shard_map/ppermute | solution.py:296
  33.7 18.3 %copy-start.6 = (s32[8]{0:T(128)S(1)}, s32[8]{0:T(128)}, u32[]{:S(2)}) copy-start(s32[8]{0:T(128)} %param.15) | copy-start | bytes 100
  33.8 7.7 %collective-permute-start.4 = (bf16[2,4,2,64,128]{4,3,2,1,0:T(8,128)(2,1)S(1)}, bf16[2,4,2,64,128]{4,3,2,1,0:T(8,128)(2,1)S(1)}, u32[]{:S(2)}, u32[]{:S(2)}) collective-permute-start(bf16[2,4,2,64,128]{4,3,2,1,0:T(8,128)(2,1)S(1)} %fusion.2), channel_id=1, source_target_pairs={{0,96},{32,0},{64,32},{96,64},{1,97},{33,1},{65,33},{97,65},{2,98}... | collective-permute-start | bytes 786440 | tf_op jit(solution)/shard_map/ppermute | solution.py:296
  38.0 7.7 %collective-permute-start.10 = (bf16[2,4,2,64,128]{4,3,2,1,0:T(8,128)(2,1)S(1)}, bf16[2,4,2,64,128]{4,3,2,1,0:T(8,128)(2,1)S(1)}, u32[]{:S(2)}, u32[]{:S(2)}) collective-permute-start(bf16[2,4,2,64,128]{4,3,2,1,0:T(8,128)(2,1)S(1)} %fusion.1), channel_id=1, source_target_pairs={{0,2},{2,128},{128,130},{130,0},{1,3},{3,129},{129,131},{131,1},{4... | collective-permute-start | bytes 786440 | tf_op jit(solution)/shard_map/ppermute | solution.py:296
  38.2 7.5 %collective-permute-start.11 = (bf16[2,4,2,64,128]{4,3,2,1,0:T(8,128)(2,1)S(1)}, bf16[2,4,2,64,128]{4,3,2,1,0:T(8,128)(2,1)S(1)}, u32[]{:S(2)}, u32[]{:S(2)}) collective-permute-start(bf16[2,4,2,64,128]{4,3,2,1,0:T(8,128)(2,1)S(1)} %fusion), channel_id=1, source_target_pairs={{0,130},{2,0},{128,2},{130,128},{1,131},{3,1},{129,3},{131,129},{4... | collective-permute-start | bytes 786440 | tf_op jit(solution)/shard_map/ppermute | solution.py:296
  41.5 21.8 %copy-start.5 = (f32[256]{0:T(256)S(1)}, f32[256]{0:T(256)}, u32[]{:S(2)}) copy-start(f32[256]{0:T(256)} %param.14) | copy-start | bytes 3076
  42.3 9.7 %collective-permute-start.5 = (bf16[4,2,64,128]{3,2,1,0:T(8,128)(2,1)S(1)}, bf16[4,2,64,128]{3,2,1,0:T(8,128)(2,1)S(1)}, u32[]{:S(2)}, u32[]{:S(2)}) collective-permute-start(bf16[4,2,64,128]{3,2,1,0:T(8,128)(2,1)S(1)} %get-tuple-element.29), channel_id=1, source_target_pairs={{0,2},{2,128},{128,130},{130,0},{1,3},{3,129},{129,131},{131,1},{4... | collective-permute-start | bytes 393224 | tf_op jit(solution)/shard_map/ppermute | solution.py:296
  42.4 9.6 %collective-permute-start.6 = (bf16[4,2,64,128]{3,2,1,0:T(8,128)(2,1)S(1)}, bf16[4,2,64,128]{3,2,1,0:T(8,128)(2,1)S(1)}, u32[]{:S(2)}, u32[]{:S(2)}) collective-permute-start(bf16[4,2,64,128]{3,2,1,0:T(8,128)(2,1)S(1)} %get-tuple-element.30), channel_id=1, source_target_pairs={{0,128},{2,130},{128,0},{130,2},{1,129},{3,131},{129,1},{131,3},{4... | collective-permute-start | bytes 393224 | tf_op jit(solution)/shard_map/ppermute | solution.py:296
  44.6 7.5 %collective-permute-start.7 = (bf16[4,2,64,128]{3,2,1,0:T(8,128)(2,1)S(1)}, bf16[4,2,64,128]{3,2,1,0:T(8,128)(2,1)S(1)}, u32[]{:S(2)}, u32[]{:S(2)}) collective-permute-start(bf16[4,2,64,128]{3,2,1,0:T(8,128)(2,1)S(1)} %get-tuple-element.31), channel_id=1, source_target_pairs={{0,130},{2,0},{128,2},{130,128},{1,131},{3,1},{129,3},{131,129},{4... | collective-permute-start | bytes 393224 | tf_op jit(solution)/shard_map/ppermute | solution.py:296
  46.6 5.5 %collective-permute-start.12 = (bf16[4,2,64,128]{3,2,1,0:T(8,128)(2,1)S(1)}, bf16[4,2,64,128]{3,2,1,0:T(8,128)(2,1)S(1)}, u32[]{:S(2)}, u32[]{:S(2)}) collective-permute-start(bf16[4,2,64,128]{3,2,1,0:T(8,128)(2,1)S(1)} %get-tuple-element.39), channel_id=1, source_target_pairs={{0,32},{32,64},{64,96},{96,0},{1,33},{33,65},{65,97},{97,1},{2,34}... | collective-permute-start | bytes 393224 | tf_op jit(solution)/shard_map/ppermute | solution.py:296
  46.7 7.5 %collective-permute-start.13 = (bf16[4,2,64,128]{3,2,1,0:T(8,128)(2,1)S(1)}, bf16[4,2,64,128]{3,2,1,0:T(8,128)(2,1)S(1)}, u32[]{:S(2)}, u32[]{:S(2)}) collective-permute-start(bf16[4,2,64,128]{3,2,1,0:T(8,128)(2,1)S(1)} %get-tuple-element.40), channel_id=1, source_target_pairs={{0,64},{32,96},{64,0},{96,32},{1,65},{33,97},{65,1},{97,33},{2,66}... | collective-permute-start | bytes 393224 | tf_op jit(solution)/shard_map/ppermute | solution.py:296
  52.0 3.8 %collective-permute-start.14 = (bf16[4,2,64,128]{3,2,1,0:T(8,128)(2,1)S(1)}, bf16[4,2,64,128]{3,2,1,0:T(8,128)(2,1)S(1)}, u32[]{:S(2)}, u32[]{:S(2)}) collective-permute-start(bf16[4,2,64,128]{3,2,1,0:T(8,128)(2,1)S(1)} %get-tuple-element.41), channel_id=1, source_target_pairs={{0,96},{32,0},{64,32},{96,64},{1,97},{33,1},{65,33},{97,65},{2,98}... | collective-permute-start | bytes 393224 | tf_op jit(solution)/shard_map/ppermute | solution.py:296
  56.8 18.7 %all-to-all-start = ((f32[8,2,64,128]{3,2,1,0:T(8,128)}), f32[8,2,64,128]{3,2,1,0:T(8,128)S(1)}, u32[]{:S(2)}, u32[]{:S(2)}) async-start(f32[8,2,64,128]{3,2,1,0:T(8,128)} %shard_map.100), calls=%async_computation | async-start | bytes 1048576 | tf_op jit(solution)/shard_map/all_to_all | solution.py:327

commit v3 on v2

--- a/solution.py
+++ b/solution.py
@@ -14,6 +14,8 @@
 SLOTS = 12
 KINDS = 2
 ROWS = 256
+STEPS = 32000.0
+TINY = 1e-37
 AUX = ("xh", "y")
 BLK = ("z", "xl", "core")
 X = ("xh", "xl")
@@ -25,6 +27,10 @@
 
 def params(mib):
     return pltpu.CompilerParams(vmem_limit_bytes=mib * 2**20)
+
+
+def in_hbm(x):
+    return pltpu.with_memory_space_constraint(x, pltpu.HBM)
 
 
 def half_kernel(block_hbm, kind_hbm, live_hbm, three_ref, coef_ref, out_ref, block_ref, kind_ref, live_ref, three, coef, weights, sems):
@@ -83,8 +89,8 @@
             pltpu.VMEM((SLOTS * SPAN, KINDS * VIR), BF16),
             pltpu.SemaphoreType.DMA((3 * SLOTS + 3,)),
         ],
-        compiler_params=params(24),
-    )(slot_block, slot_aux, live_slots, three_center, vir_coef)
+        compiler_params=params(12),
+    )(*(in_hbm(x) for x in (slot_block, slot_aux)), live_slots, in_hbm(three_center), in_hbm(vir_coef))
 
 
 PLACES = {
@@ -172,7 +178,7 @@
         in_specs=[SMEM, VMEM, VMEM],
         out_specs=[VMEM] * 6,
         scratch_shapes=[done],
-        compiler_params=params(32),
+        compiler_params=params(10),
     )(place, own, other)
     second = pl.pallas_call(
         along_x_kernel,
@@ -180,7 +186,7 @@
         in_specs=[SMEM, VMEM, VMEM, VMEM],
         out_specs=[VMEM] * 5,
         scratch_shapes=[done],
-        compiler_params=params(32),
+        compiler_params=params(10),
     )(place, own, other, turned)
     return first, second
 
@@ -205,34 +211,42 @@
         in_specs=[SMEM] + [VMEM] * 5,
         out_specs=[VMEM] * 4,
         scratch_shapes=[pltpu.VMEM((4,) + PART, BF16)],
-        compiler_params=params(16),
+        compiler_params=params(6),
     )(place, *ins)
 
 
 def second_sum_kernel(*refs):
     ins, out = refs[:8], refs[8]
     for half in range(2):
-        total = ins[half * 4][...].astype(F32)
-        for d in range(1, 4):
-            total = total + ins[half * 4 + d][...].astype(F32)
-        out[pl.ds(half * 4, 4)] = total
+        for j in range(4):
+            total = ins[half * 4][j].astype(F32)
+            for d in range(1, 4):
+                total = total + ins[half * 4 + d][j].astype(F32)
+            total = total.reshape(128, 128)
+            largest = jnp.max(jnp.abs(total), axis=(0, 1), keepdims=True)
+            power = jnp.ceil(jnp.log2(jnp.maximum(largest, TINY)))
+            steps = jnp.round(total * jnp.exp2(-power) * STEPS)
+            out[half * 4 + j, 0:128] = steps.astype(jnp.int32).astype(jnp.int16)
+            out[half * 4 + j, 128:144] = jnp.broadcast_to(power, (16, 128)).astype(jnp.int32).astype(jnp.int16)
 
 
 def second_sum(ins):
     return pl.pallas_call(
         second_sum_kernel,
-        out_shape=jax.ShapeDtypeStruct((OCC, 2, 64, 128), F32),
+        out_shape=jax.ShapeDtypeStruct((OCC, 144, 128), jnp.int16),
         in_specs=[VMEM] * 8,
         out_specs=VMEM,
-        compiler_params=params(16),
+        compiler_params=params(6),
     )(*ins)
 
 
 def finish_kernel(place_ref, parts_ref, below_ref, out_ref):
     core, low = place_ref[2], place_ref[3]
-    total = parts_ref[0]
-    for z in range(1, 8):
-        total = total + parts_ref[z]
+    total = jnp.zeros((128, 128), F32)
+    for z in range(8):
+        power = parts_ref[z, 128:144].astype(jnp.int32).astype(F32)[0:1]
+        total = total + parts_ref[z, 0:128].astype(jnp.int32).astype(F32) * (jnp.exp2(power) * (1.0 / STEPS))
+    total = total.reshape(2, 64, 128)
     across = [total[half].T for half in range(2)]
     crossed = []
     for half in range(2):
@@ -257,7 +271,7 @@
         out_shape=jax.ShapeDtypeStruct((32, 8, 128), F32),
         in_specs=[SMEM, VMEM, VMEM],
         out_specs=VMEM,
-        compiler_params=params(16),
+        compiler_params=params(6),
     )(place, parts, below)
 
 
@@ -287,7 +301,7 @@
         out_shape=[jax.ShapeDtypeStruct((8, OCC, VIR), F32), jax.ShapeDtypeStruct((1, OCC), F32)],
         in_specs=[SMEM, VMEM],
         out_specs=[VMEM, VMEM],
-        compiler_params=params(16),
+        compiler_params=params(6),
     )(place, parts)
 
 
@@ -313,6 +327,7 @@
     own = half_transform(slot_block, slot_aux, live_slots, three_center, vir_coef)
     other = moved(own, "core", 1)
     below = denominators(eps_occ, eps_vir, occ_index, core, low)
+    other, below = lax.optimization_barrier((other, below))
 
     got = []
     for axis, (ahead, back, one, minus, mine) in zip(("y", X), partial(place, own, other)):

time: 96.5 us -> 89 us (0.922)
  blocking collectives: 18.6 us -> 33.6 us
  waiting for transfers between devices: 25.3 us -> 15 us
  starting transfers between devices: 28.3 us -> 21.9 us
  local copies, waits for them, and re-layouts: 5.93 us -> 0.86 us
    all_to_all x0 -> x1, blocking collectives: none -> 16.1 us  [body(): parts = lax.all_to_all(second_sum(ins), 'z', 0, 0, tiled=True)]
    all_to_all x1 -> x0, waiting for transfers between devices: 9.25 us -> none  [body(): parts = lax.all_to_all(second_sum(ins), 'z', 0, 0, tiled=True)]
    all_to_all x1 -> x0, starting transfers between devices: 6.55 us -> none  [body(): parts = lax.all_to_all(second_sum(ins), 'z', 0, 0, tiled=True)]
    unnamed x14 -> x6, local copies, waits for them, and re-layouts: 5.1 us -> 0.02 us
    all_to_all x1, blocking collectives: 18.6 us -> 17.5 us  [body(): lax.all_to_all(sent, BLK, 0, 0, tiled=True)]
    ppermute x15, waiting for transfers between devices: 16.1 us -> 15 us  [moved(): return lax.ppermute(x, axis, [(i, (i + by) % n) for i in range(n)])]
  transfers between devices with their start and end apart: 16 -> 15, of which waited for: 8 -> 6; matrix products, arithmetic and copies ran while one was open for 2% -> 2% of each run, Pallas kernels for 4% -> 4%
where the time goes in v3:
time: 89 us; the launch traced here: 88.7 us
  blocking collectives  33.6 us (38%)
  starting transfers between devices  21.9 us (25%)
  waiting for transfers between devices  15 us (17%)
  Pallas kernels  13.5 us (15%)
  between operations  2.77 us (3%)
  other arithmetic  1.11 us (1%)
    ppermute x15, starting transfers between devices, moved(): return lax.ppermute(x, axis, [(i, (i + by) % n) for i in range(n)])  21.9 us
    all_to_all x1, blocking collectives, body(): lax.all_to_all(sent, BLK, 0, 0, tiled=True)  17.5 us
    all_to_all x1, blocking collectives, body(): parts = lax.all_to_all(second_sum(ins), 'z', 0, 0, tiled=True)  16.1 us
    ppermute x15, waiting for transfers between devices, moved(): return lax.ppermute(x, axis, [(i, (i + by) % n) for i in range(n)])  15 us
    pallas_call x1, Pallas kernels, half_transform(): pl.pallas_call(half_kernel, out_shape=jax.ShapeDtypeStruct((OCC, ROWS, VI...  4.36 us
    pallas_call x1, Pallas kernels, partial(): pl.pallas_call(along_y_kernel, out_shape=outs + [jax.ShapeDtypeStruct((2,...  2.72 us
    pallas_call x1, Pallas kernels, partial(): pl.pallas_call(along_x_kernel, out_shape=outs, in_specs=[SMEM, VMEM, VMEM...  2.28 us
  transfers between devices with their start and end apart: 15, of which 6 were waited for; matrix products, arithmetic and copies ran while one was open for 2% of the time, Pallas kernels for 4%

profile of v3, /device:TPU:1, one launch (start us, length us, event | category | flops | bytes accessed | tf_op | source)
XLA Modules:
  0.0 88.7 jit_solution(5555888202596288060)
XLA Ops:
  0.6 0.0 copy-start
  1.3 4.4 %shard_map.95.own_ref = bf16[8,256,256]{2,1,0:T(8,128)(2,1)S(1)} custom-call(s32[12]{0:T(128)} %block_hbm.1, s32[12]{0:T(128)} %kind_hbm.1, s32[1]{0:T(128)S(6)} %copy.10.live_hbm, bf16[12,8,128,128]{3,2,1,0:T(8,128)(2,1)} %three_ref.1, bf16[6144,256]{1,0:T(8,128)(2,1)} %coef_ref.1), custom_call_target="tpu_custom_call" | custom-call | tf_op jit(solution)/shard_map/pallas_call | solution.py:78
  5.7 3.4 %collective-permute-start = (bf16[8,256,256]{2,1,0:T(8,128)(2,1)S(1)}, bf16[8,256,256]{2,1,0:T(8,128)(2,1)S(1)}, u32[]{:S(2)}, u32[]{:S(2)}) collective-permute-start(bf16[8,256,256]{2,1,0:T(8,128)(2,1)S(1)} %shard_map.95.own_ref), channel_id=1, source_target_pairs={{0,1},{1,0},{2,3},{3,2},{4,5},{5,4},{6,7},{7,6},{8,9},{9,8},{10,11... | collective-permute-start | bytes 3145736 | tf_op jit(solution)/shard_map/ppermute | solution.py:310
  9.1 0.1 reshape.25
  9.2 0.6 gather_fusion
  9.8 0.7 fusion.6
  11.7 0.1 stack.23.place_ref.refs_0_
  11.9 0.1 subtract_subtract_fusion.below_ref
  12.0 0.0 collective-permute-done.other_ref
  12.0 2.7 %shard_map.96 = (bf16[2,2,4,2,64,128]{5,4,3,2,1,0:T(8,128)(2,1)S(1)}, bf16[2,2,4,2,64,128]{5,4,3,2,1,0:T(8,128)(2,1)S(1)}, bf16[2,4,2,64,128]{4,3,2,1,0:T(8,128)...) custom-call(s32[5]{0:T(128)S(1)} %stack.23.place_ref.refs_0_, ...), custom_call_target="tpu_custom_call" | custom-call | tf_op jit(solution)/shard_map/pallas_call | solution.py:175
  14.7 0.1 collective-permute-start.1
  14.8 2.7 %collective-permute-start.2 = (bf16[2,2,4,2,64,128]{5,4,3,2,1,0:T(8,128)(2,1)S(1)}, bf16[2,2,4,2,64,128]{5,4,3,2,1,0:T(8,128)(2,1)S(1)}, u32[]{:S(2)}, u32[]{:S(2)}) collective-permute-start(bf16[2,2,4,2,64,128]{5,4,3,2,1,0:T(8,128)(2,1)S(1)} %get-tuple-element.28), channel_id=1, source_target_pairs={{0,96},{32,0},{64,32},{96,64},{1,97},{33,1},{65,33},{97,65},{2,98}... | collective-permute-start | bytes 1572872 | tf_op jit(solution)/shard_map/ppermute | solution.py:310
  17.5 2.3 %shard_map.98 = (bf16[2,2,4,2,64,128]{5,4,3,2,1,0:T(8,128)(2,1)S(1)}, bf16[2,2,4,2,64,128]{5,4,3,2,1,0:T(8,128)(2,1)S(1)}, bf16[2,4,2,64,128]{4,3,2,1,0:T(8,128)...) custom-call(s32[5]{0:T(128)S(1)} %stack.23.place_ref.refs_0_, ...), custom_call_target="tpu_custom_call" | custom-call | tf_op jit(solution)/shard_map/pallas_call | solution.py:183
  19.8 0.1 collective-permute-start.8
  19.9 2.7 %collective-permute-start.9 = (bf16[2,2,4,2,64,128]{5,4,3,2,1,0:T(8,128)(2,1)S(1)}, bf16[2,2,4,2,64,128]{5,4,3,2,1,0:T(8,128)(2,1)S(1)}, u32[]{:S(2)}, u32[]{:S(2)}) collective-permute-start(bf16[2,2,4,2,64,128]{5,4,3,2,1,0:T(8,128)(2,1)S(1)} %get-tuple-element.38), channel_id=1, source_target_pairs={{0,130},{2,0},{128,2},{130,128},{1,131},{3,1},{129,3},{131,129},{4... | collective-permute-start | bytes 1572872 | tf_op jit(solution)/shard_map/ppermute | solution.py:310
  22.5 7.0 %collective-permute-done.1.refs_2_ = bf16[2,2,4,2,64,128]{5,4,3,2,1,0:T(8,128)(2,1)S(1)} collective-permute-done((bf16[2,2,4,2,64,128]{5,4,3,2,1,0:T(8,128)(2,1)S(1)}, bf16[2,2,4,2,64,128]{5,4,3,2,1,0:T(8,128)(2,1)S(1)}, u32[]{:S(2)}, u32[]{:S(2)}) %collective-permute-start.1) | collective-permute-done | bytes 524320 | tf_op jit(solution)/shard_map/ppermute | solution.py:310
  29.5 0.1 fusion.3
  29.6 0.1 collective-permute-start.3
  29.7 0.0 collective-permute-done.2.refs_3_
  29.7 0.1 fusion.2
  29.8 2.7 %collective-permute-start.4 = (bf16[2,4,2,64,128]{4,3,2,1,0:T(8,128)(2,1)S(1)}, bf16[2,4,2,64,128]{4,3,2,1,0:T(8,128)(2,1)S(1)}, u32[]{:S(2)}, u32[]{:S(2)}) collective-permute-start(bf16[2,4,2,64,128]{4,3,2,1,0:T(8,128)(2,1)S(1)} %fusion.2), channel_id=1, source_target_pairs={{0,96},{32,0},{64,32},{96,64},{1,97},{33,1},{65,33},{97,65},{2,98}... | collective-permute-start | bytes 786440 | tf_op jit(solution)/shard_map/ppermute | solution.py:310
  32.5 1.4 %collective-permute-done.8.refs_2_ = bf16[2,2,4,2,64,128]{5,4,3,2,1,0:T(8,128)(2,1)S(1)} collective-permute-done((bf16[2,2,4,2,64,128]{5,4,3,2,1,0:T(8,128)(2,1)S(1)}, bf16[2,2,4,2,64,128]{5,4,3,2,1,0:T(8,128)(2,1)S(1)}, u32[]{:S(2)}, u32[]{:S(2)}) %collective-permute-start.8) | collective-permute-done | bytes 524320 | tf_op jit(solution)/shard_map/ppermute | solution.py:310
  33.9 0.1 fusion.1
  34.0 0.1 collective-permute-start.10
  34.1 0.1 fusion
  34.2 2.9 %collective-permute-start.11 = (bf16[2,4,2,64,128]{4,3,2,1,0:T(8,128)(2,1)S(1)}, bf16[2,4,2,64,128]{4,3,2,1,0:T(8,128)(2,1)S(1)}, u32[]{:S(2)}, u32[]{:S(2)}) collective-permute-start(bf16[2,4,2,64,128]{4,3,2,1,0:T(8,128)(2,1)S(1)} %fusion), channel_id=1, source_target_pairs={{0,130},{2,0},{128,2},{130,128},{1,131},{3,1},{129,3},{131,129},{4... | collective-permute-start | bytes 786440 | tf_op jit(solution)/shard_map/ppermute | solution.py:310
  37.1 0.8 collective-permute-done.3.refs_4_
  37.9 0.0 collective-permute-done.4.refs_5_
  37.9 0.8 shard_map.97
  38.7 0.1 collective-permute-start.5
  38.8 2.1 %collective-permute-start.6 = (bf16[4,2,64,128]{3,2,1,0:T(8,128)(2,1)S(1)}, bf16[4,2,64,128]{3,2,1,0:T(8,128)(2,1)S(1)}, u32[]{:S(2)}, u32[]{:S(2)}) collective-permute-start(bf16[4,2,64,128]{3,2,1,0:T(8,128)(2,1)S(1)} %get-tuple-element.33), channel_id=1, source_target_pairs={{0,128},{2,130},{128,0},{130,2},{1,129},{3,131},{129,1},{131,3},{4... | collective-permute-start | bytes 393224 | tf_op jit(solution)/shard_map/ppermute | solution.py:310
  40.9 1.2 %collective-permute-start.7 = (bf16[4,2,64,128]{3,2,1,0:T(8,128)(2,1)S(1)}, bf16[4,2,64,128]{3,2,1,0:T(8,128)(2,1)S(1)}, u32[]{:S(2)}, u32[]{:S(2)}) collective-permute-start(bf16[4,2,64,128]{3,2,1,0:T(8,128)(2,1)S(1)} %get-tuple-element.34), channel_id=1, source_target_pairs={{0,130},{2,0},{128,2},{130,128},{1,131},{3,1},{129,3},{131,129},{4... | collective-permute-start | bytes 393224 | tf_op jit(solution)/shard_map/ppermute | solution.py:310
  42.2 0.0 collective-permute-done.10.refs_4_
  42.2 0.8 shard_map.99
  43.0 0.1 collective-permute-start.12
  43.1 3.7 %collective-permute-start.13 = (bf16[4,2,64,128]{3,2,1,0:T(8,128)(2,1)S(1)}, bf16[4,2,64,128]{3,2,1,0:T(8,128)(2,1)S(1)}, u32[]{:S(2)}, u32[]{:S(2)}) collective-permute-start(bf16[4,2,64,128]{3,2,1,0:T(8,128)(2,1)S(1)} %get-tuple-element.43), channel_id=1, source_target_pairs={{0,64},{32,96},{64,0},{96,32},{1,65},{33,97},{65,1},{97,33},{2,66}... | collective-permute-start | bytes 393224 | tf_op jit(solution)/shard_map/ppermute | solution.py:310
  46.8 1.6 %collective-permute-done.5.refs_1_ = bf16[4,2,64,128]{3,2,1,0:T(8,128)(2,1)S(1)} collective-permute-done((bf16[4,2,64,128]{3,2,1,0:T(8,128)(2,1)S(1)}, bf16[4,2,64,128]{3,2,1,0:T(8,128)(2,1)S(1)}, u32[]{:S(2)}, u32[]{:S(2)}) %collective-permute-start.5) | collective-permute-done | bytes 131104 | tf_op jit(solution)/shard_map/ppermute | solution.py:310
  48.4 0.0 collective-permute-start.14
  48.4 0.0 collective-permute-done.6.refs_2_
  48.4 0.0 collective-permute-done.7.refs_3_
  48.4 0.0 collective-permute-done.12.refs_5_
  48.4 2.1 %collective-permute-done.13.refs_6_ = bf16[4,2,64,128]{3,2,1,0:T(8,128)(2,1)S(1)} collective-permute-done((bf16[4,2,64,128]{3,2,1,0:T(8,128)(2,1)S(1)}, bf16[4,2,64,128]{3,2,1,0:T(8,128)(2,1)S(1)}, u32[]{:S(2)}, u32[]{:S(2)}) %collective-permute-start.13) | collective-permute-done | bytes 131104 | tf_op jit(solution)/shard_map/ppermute | solution.py:310
  50.6 2.1 %collective-permute-done.14.refs_7_ = bf16[4,2,64,128]{3,2,1,0:T(8,128)(2,1)S(1)} collective-permute-done((bf16[4,2,64,128]{3,2,1,0:T(8,128)(2,1)S(1)}, bf16[4,2,64,128]{3,2,1,0:T(8,128)(2,1)S(1)}, u32[]{:S(2)}, u32[]{:S(2)}) %collective-permute-start.14) | collective-permute-done | bytes 131104 | tf_op jit(solution)/shard_map/ppermute | solution.py:310
  52.7 0.3 shard_map.100
  53.0 16.1 %all_to_all.10.parts_ref = s16[8,144,128]{2,1,0:T(8,128)(2,1)S(1)} all-to-all(s16[8,144,128]{2,1,0:T(8,128)(2,1)S(1)} %shard_map.100), channel_id=1, replica_groups=mesh['xh'=2,'y'=4,'z'=8,'xl'=2,'core'=2] {'z'}, dimensions={0} | all-to-all | bytes 589824 | tf_op jit(solution)/shard_map/all_to_all | solution.py:342
  69.0 0.9 %shard_map.101 = f32[32,8,128]{2,1,0:T(8,128)S(1)} custom-call(s32[5]{0:T(128)S(1)} %stack.23.place_ref.refs_0_, s16[8,144,128]{2,1,0:T(8,128)(2,1)S(1)} %all_to_all.10.parts_ref, f32[2,64,128]{2,1,0:T(8,128)S(1)} %subtract_subtract_fusion.below_ref), custom_call_target="tpu_custom_call" | custom-call | tf_op jit(solution)/shard_map/pallas_call | solution.py:269
  69.9 17.5 %all_to_all.11.parts_ref = f32[32,8,128]{2,1,0:T(8,128)S(1)} all-to-all(f32[32,8,128]{2,1,0:T(8,128)S(1)} %shard_map.101), channel_id=1, replica_groups=mesh['xh'=2,'y'=4,'z'=8,'xl'=2,'core'=2] {'z','xl','core'}, dimensions={0} | all-to-all | bytes 262144 | tf_op jit(solution)/shard_map/all_to_all | solution.py:344
  87.5 1.2 %shard_map.102 = (f32[8,8,256]{2,1,0:T(8,128)}, f32[1,8]{1,0:T(1,128)}) custom-call(s32[5]{0:T(128)S(1)} %stack.23.place_ref.refs_0_, f32[32,8,128]{2,1,0:T(8,128)S(1)} %all_to_all.11.parts_ref), custom_call_target="tpu_custom_call" | custom-call | tf_op jit(solution)/shard_map/pallas_call | solution.py:299
  (13 shorter events, 0.1 us)
Async XLA Ops:
  0.6 8.5 %copy-start = (f32[4000]{0:T(1024)S(1)}, f32[4000]{0:T(1024)}, u32[]{:S(2)}) copy-start(f32[4000]{0:T(1024)} %param.13) | copy-start | bytes 48004
  1.3 7.7 %copy-start.2 = (s32[8]{0:T(128)S(1)}, s32[8]{0:T(128)}, u32[]{:S(2)}) copy-start(s32[8]{0:T(128)} %param.15) | copy-start | bytes 100
  1.3 7.7 %copy-start.1 = (f32[256]{0:T(256)S(1)}, f32[256]{0:T(256)}, u32[]{:S(2)}) copy-start(f32[256]{0:T(256)} %param.14) | copy-start | bytes 3076
  5.7 6.3 %collective-permute-start = (bf16[8,256,256]{2,1,0:T(8,128)(2,1)S(1)}, bf16[8,256,256]{2,1,0:T(8,128)(2,1)S(1)}, u32[]{:S(2)}, u32[]{:S(2)}) collective-permute-start(bf16[8,256,256]{2,1,0:T(8,128)(2,1)S(1)} %shard_map.95.own_ref), channel_id=1, source_target_pairs={{0,1},{1,0},{2,3},{3,2},{4,5},{5,4},{6,7},{7,6},{8,9},{9,8},{10,11... | collective-permute-start | bytes 3145736 | tf_op jit(solution)/shard_map/ppermute | solution.py:310
  14.7 14.8 %collective-permute-start.1 = (bf16[2,2,4,2,64,128]{5,4,3,2,1,0:T(8,128)(2,1)S(1)}, bf16[2,2,4,2,64,128]{5,4,3,2,1,0:T(8,128)(2,1)S(1)}, u32[]{:S(2)}, u32[]{:S(2)}) collective-permute-start(bf16[2,2,4,2,64,128]{5,4,3,2,1,0:T(8,128)(2,1)S(1)} %get-tuple-element.27), channel_id=1, source_target_pairs={{0,32},{32,64},{64,96},{96,0},{1,33},{33,65},{65,97},{97,1},{2,34}... | collective-permute-start | bytes 1572872 | tf_op jit(solution)/shard_map/ppermute | solution.py:310
  14.8 14.9 %collective-permute-start.2 = (bf16[2,2,4,2,64,128]{5,4,3,2,1,0:T(8,128)(2,1)S(1)}, bf16[2,2,4,2,64,128]{5,4,3,2,1,0:T(8,128)(2,1)S(1)}, u32[]{:S(2)}, u32[]{:S(2)}) collective-permute-start(bf16[2,2,4,2,64,128]{5,4,3,2,1,0:T(8,128)(2,1)S(1)} %get-tuple-element.28), channel_id=1, source_target_pairs={{0,96},{32,0},{64,32},{96,64},{1,97},{33,1},{65,33},{97,65},{2,98}... | collective-permute-start | bytes 1572872 | tf_op jit(solution)/shard_map/ppermute | solution.py:310
  19.8 14.2 %collective-permute-start.8 = (bf16[2,2,4,2,64,128]{5,4,3,2,1,0:T(8,128)(2,1)S(1)}, bf16[2,2,4,2,64,128]{5,4,3,2,1,0:T(8,128)(2,1)S(1)}, u32[]{:S(2)}, u32[]{:S(2)}) collective-permute-start(bf16[2,2,4,2,64,128]{5,4,3,2,1,0:T(8,128)(2,1)S(1)} %get-tuple-element.37), channel_id=1, source_target_pairs={{0,2},{2,128},{128,130},{130,0},{1,3},{3,129},{129,131},{131,1},{4... | collective-permute-start | bytes 1572872 | tf_op jit(solution)/shard_map/ppermute | solution.py:310
  19.9 14.2 %collective-permute-start.9 = (bf16[2,2,4,2,64,128]{5,4,3,2,1,0:T(8,128)(2,1)S(1)}, bf16[2,2,4,2,64,128]{5,4,3,2,1,0:T(8,128)(2,1)S(1)}, u32[]{:S(2)}, u32[]{:S(2)}) collective-permute-start(bf16[2,2,4,2,64,128]{5,4,3,2,1,0:T(8,128)(2,1)S(1)} %get-tuple-element.38), channel_id=1, source_target_pairs={{0,130},{2,0},{128,2},{130,128},{1,131},{3,1},{129,3},{131,129},{4... | collective-permute-start | bytes 1572872 | tf_op jit(solution)/shard_map/ppermute | solution.py:310
  29.6 8.3 %collective-permute-start.3 = (bf16[2,4,2,64,128]{4,3,2,1,0:T(8,128)(2,1)S(1)}, bf16[2,4,2,64,128]{4,3,2,1,0:T(8,128)(2,1)S(1)}, u32[]{:S(2)}, u32[]{:S(2)}) collective-permute-start(bf16[2,4,2,64,128]{4,3,2,1,0:T(8,128)(2,1)S(1)} %fusion.3), channel_id=1, source_target_pairs={{0,32},{32,64},{64,96},{96,0},{1,33},{33,65},{65,97},{97,1},{2,34}... | collective-permute-start | bytes 786440 | tf_op jit(solution)/shard_map/ppermute | solution.py:310
  29.8 8.1 %collective-permute-start.4 = (bf16[2,4,2,64,128]{4,3,2,1,0:T(8,128)(2,1)S(1)}, bf16[2,4,2,64,128]{4,3,2,1,0:T(8,128)(2,1)S(1)}, u32[]{:S(2)}, u32[]{:S(2)}) collective-permute-start(bf16[2,4,2,64,128]{4,3,2,1,0:T(8,128)(2,1)S(1)} %fusion.2), channel_id=1, source_target_pairs={{0,96},{32,0},{64,32},{96,64},{1,97},{33,1},{65,33},{97,65},{2,98}... | collective-permute-start | bytes 786440 | tf_op jit(solution)/shard_map/ppermute | solution.py:310
  34.0 8.2 %collective-permute-start.10 = (bf16[2,4,2,64,128]{4,3,2,1,0:T(8,128)(2,1)S(1)}, bf16[2,4,2,64,128]{4,3,2,1,0:T(8,128)(2,1)S(1)}, u32[]{:S(2)}, u32[]{:S(2)}) collective-permute-start(bf16[2,4,2,64,128]{4,3,2,1,0:T(8,128)(2,1)S(1)} %fusion.1), channel_id=1, source_target_pairs={{0,2},{2,128},{128,130},{130,0},{1,3},{3,129},{129,131},{131,1},{4... | collective-permute-start | bytes 786440 | tf_op jit(solution)/shard_map/ppermute | solution.py:310
  34.2 8.0 %collective-permute-start.11 = (bf16[2,4,2,64,128]{4,3,2,1,0:T(8,128)(2,1)S(1)}, bf16[2,4,2,64,128]{4,3,2,1,0:T(8,128)(2,1)S(1)}, u32[]{:S(2)}, u32[]{:S(2)}) collective-permute-start(bf16[2,4,2,64,128]{4,3,2,1,0:T(8,128)(2,1)S(1)} %fusion), channel_id=1, source_target_pairs={{0,130},{2,0},{128,2},{130,128},{1,131},{3,1},{129,3},{131,129},{4... | collective-permute-start | bytes 786440 | tf_op jit(solution)/shard_map/ppermute | solution.py:310
  38.7 9.7 %collective-permute-start.5 = (bf16[4,2,64,128]{3,2,1,0:T(8,128)(2,1)S(1)}, bf16[4,2,64,128]{3,2,1,0:T(8,128)(2,1)S(1)}, u32[]{:S(2)}, u32[]{:S(2)}) collective-permute-start(bf16[4,2,64,128]{3,2,1,0:T(8,128)(2,1)S(1)} %get-tuple-element.32), channel_id=1, source_target_pairs={{0,2},{2,128},{128,130},{130,0},{1,3},{3,129},{129,131},{131,1},{4... | collective-permute-start | bytes 393224 | tf_op jit(solution)/shard_map/ppermute | solution.py:310
  38.8 9.6 %collective-permute-start.6 = (bf16[4,2,64,128]{3,2,1,0:T(8,128)(2,1)S(1)}, bf16[4,2,64,128]{3,2,1,0:T(8,128)(2,1)S(1)}, u32[]{:S(2)}, u32[]{:S(2)}) collective-permute-start(bf16[4,2,64,128]{3,2,1,0:T(8,128)(2,1)S(1)} %get-tuple-element.33), channel_id=1, source_target_pairs={{0,128},{2,130},{128,0},{130,2},{1,129},{3,131},{129,1},{131,3},{4... | collective-permute-start | bytes 393224 | tf_op jit(solution)/shard_map/ppermute | solution.py:310
  40.9 7.5 %collective-permute-start.7 = (bf16[4,2,64,128]{3,2,1,0:T(8,128)(2,1)S(1)}, bf16[4,2,64,128]{3,2,1,0:T(8,128)(2,1)S(1)}, u32[]{:S(2)}, u32[]{:S(2)}) collective-permute-start(bf16[4,2,64,128]{3,2,1,0:T(8,128)(2,1)S(1)} %get-tuple-element.34), channel_id=1, source_target_pairs={{0,130},{2,0},{128,2},{130,128},{1,131},{3,1},{129,3},{131,129},{4... | collective-permute-start | bytes 393224 | tf_op jit(solution)/shard_map/ppermute | solution.py:310
  43.0 5.4 %collective-permute-start.12 = (bf16[4,2,64,128]{3,2,1,0:T(8,128)(2,1)S(1)}, bf16[4,2,64,128]{3,2,1,0:T(8,128)(2,1)S(1)}, u32[]{:S(2)}, u32[]{:S(2)}) collective-permute-start(bf16[4,2,64,128]{3,2,1,0:T(8,128)(2,1)S(1)} %get-tuple-element.42), channel_id=1, source_target_pairs={{0,32},{32,64},{64,96},{96,0},{1,33},{33,65},{65,97},{97,1},{2,34}... | collective-permute-start | bytes 393224 | tf_op jit(solution)/shard_map/ppermute | solution.py:310
  43.1 7.4 %collective-permute-start.13 = (bf16[4,2,64,128]{3,2,1,0:T(8,128)(2,1)S(1)}, bf16[4,2,64,128]{3,2,1,0:T(8,128)(2,1)S(1)}, u32[]{:S(2)}, u32[]{:S(2)}) collective-permute-start(bf16[4,2,64,128]{3,2,1,0:T(8,128)(2,1)S(1)} %get-tuple-element.43), channel_id=1, source_target_pairs={{0,64},{32,96},{64,0},{96,32},{1,65},{33,97},{65,1},{97,33},{2,66}... | collective-permute-start | bytes 393224 | tf_op jit(solution)/shard_map/ppermute | solution.py:310
  48.4 4.2 %collective-permute-start.14 = (bf16[4,2,64,128]{3,2,1,0:T(8,128)(2,1)S(1)}, bf16[4,2,64,128]{3,2,1,0:T(8,128)(2,1)S(1)}, u32[]{:S(2)}, u32[]{:S(2)}) collective-permute-start(bf16[4,2,64,128]{3,2,1,0:T(8,128)(2,1)S(1)} %get-tuple-element.44), channel_id=1, source_target_pairs={{0,96},{32,0},{64,32},{96,64},{1,97},{33,1},{65,33},{97,65},{2,98}... | collective-permute-start | bytes 393224 | tf_op jit(solution)/shard_map/ppermute | solution.py:310

commit v4 on v3

--- a/solution.py
+++ b/solution.py
@@ -100,6 +100,7 @@
 
 
 def product(core, first_j, turned, own_ref, other_ref, done):
+    left = lax.broadcasted_iota(jnp.int32, (64, 128), 1) < 64
     for half in range(2):
         columns = pl.ds(pl.multiple_of(lax.rem(core + half, 2) * 128, 128), 128)
         for pair in range(2):
@@ -108,15 +109,13 @@
                 [jnp.concatenate([ref[j + i, :, columns] for ref in (own_ref, other_ref)], axis=0) for i in range(2)],
                 axis=1,
             )
-            whole = jnp.dot(turned[half], right, preferred_element_type=F32).astype(BF16)
-            done[half, pair] = whole.reshape(OCC, 128, 256)
-
-
-def tile(done, half, j, o, low):
-    lane = lax.broadcasted_iota(jnp.int32, (64, 128), 1)
-    columns = pl.ds(j % 2 * 128, 128)
-    first, second = done[half, j // 2, o, 0:64, columns], done[half, j // 2, o, 64:128, columns]
-    return jnp.where(lax.rem(lane // 64 + low, 2) == 0, first.astype(F32), second.astype(F32)).astype(BF16)
+            whole = jnp.dot(turned[half], right, preferred_element_type=F32)
+            for o in range(OCC):
+                for i in range(2):
+                    first = whole[o * 128 : o * 128 + 64, i * 128 : i * 128 + 128]
+                    second = whole[o * 128 + 64 : o * 128 + 128, i * 128 : i * 128 + 128]
+                    done[half, 2 * pair + i, o, 0] = jnp.where(left, first, second).astype(BF16)
+                    done[half, 2 * pair + i, o, 1] = jnp.where(left, second, first).astype(BF16)
 
 
 def along_y_kernel(place_ref, own_ref, other_ref, *rest):
@@ -139,7 +138,7 @@
             for u in range(2):
                 for j in range(4):
                     for half in range(2):
-                        part = tile(done, half, j, h * 4 + lax.rem(y + d, 4), u)
+                        part = done[half, j, h * 4 + lax.rem(y + d, 4), u]
                         if at is None:
                             outs[which][u, j, half] = part
                         else:
@@ -157,7 +156,7 @@
             for u in range(2):
                 for j in range(4):
                     for half in range(2):
-                        part = tile(done, half, j, to // 2 * 4 + h * 2 + u, lax.rem(to, 2))
+                        part = done[half, j, to // 2 * 4 + h * 2 + u, lax.rem(to, 2)]
                         if at is None:
                             outs[which][u, j, half] = part
                         else:
@@ -171,7 +170,7 @@
     pair = jax.ShapeDtypeStruct((2, 2) + PART, BF16)
     single = jax.ShapeDtypeStruct((2,) + PART, BF16)
     outs = [pair, pair, single, single, pair]
-    done = pltpu.VMEM((2, 2, OCC, 128, 256), BF16)
+    done = pltpu.VMEM((2, 4, OCC, 2, 64, 128), BF16)
     *first, turned = pl.pallas_call(
         along_y_kernel,
         out_shape=outs + [jax.ShapeDtypeStruct((2, OCC * 128, 2 * ROWS), BF16)],
@@ -191,14 +190,16 @@
     return first, second
 
 
-def first_sum_kernel(place_ref, own, from_back, from_ahead, last_back, last_ahead, *rest, at):
-    outs, kept = rest[:4], rest[4]
-    for h, (one, two) in enumerate(((from_ahead, last_back), (from_back, last_ahead))):
-        for u in range(2):
-            total = own[h, u].astype(F32) + one[1, u].astype(F32) + two[u].astype(F32)
-            kept[h * 2 + u] = total.astype(BF16)
+def first_sum_kernel(place_ref, own, from_back, from_ahead, last_back, last_ahead, *outs, at):
     for d in range(4):
-        outs[d][...] = kept[lax.rem(place_ref[at] + d, 4)]
+        to = lax.rem(place_ref[at] + d, 4)
+        h, u = to // 2, lax.rem(to, 2)
+        for side, (one, two) in enumerate(((from_ahead, last_back), (from_back, last_ahead))):
+
+            @pl.when(h == side)
+            def _():
+                total = own[side, u].astype(F32) + one[1, u].astype(F32) + two[u].astype(F32)
+                outs[d][...] = total.astype(BF16)
 
 
 def first_sum(place, at, ins):
@@ -210,7 +211,6 @@
         out_shape=[jax.ShapeDtypeStruct(PART, BF16)] * 4,
         in_specs=[SMEM] + [VMEM] * 5,
         out_specs=[VMEM] * 4,
-        scratch_shapes=[pltpu.VMEM((4,) + PART, BF16)],
         compiler_params=params(6),
     )(place, *ins)
 
@@ -338,7 +338,7 @@
         minus = (minus.astype(F32) + from_ahead[0].astype(F32)).astype(BF16)
         last = moved(one, axis, 1), moved(minus, axis, -1)
         group = first_sum(place, at, (mine, from_back, from_ahead, *last))
-        ins += [group[0]] + [moved(group[d], (X, "y")[at], d) for d in range(1, 4)]
+        ins += [group[0]] + [moved(group[d], (X, "y")[at], d) for d in (2, 1, 3)]
     parts = lax.all_to_all(second_sum(ins), "z", 0, 0, tiled=True)
     sent = finish(place, parts, below)
     amplitudes, pair = collect(place, lax.all_to_all(sent, BLK, 0, 0, tiled=True))

time: 89 us -> 89 us (level)
  waiting for transfers between devices: 15 us -> 12.8 us
  blocking collectives: 33.6 us -> 35.7 us
    ppermute x15, waiting for transfers between devices: 15 us -> 12.8 us  [moved(): return lax.ppermute(x, axis, [(i, (i + by) % n) for i in range(n)])]
    all_to_all x1, blocking collectives: 16.1 us -> 17.9 us  [body(): parts = lax.all_to_all(second_sum(ins), 'z', 0, 0, tiled=True)]
where the time goes in v4:
time: 89 us; the launch traced here: 88.7 us
  blocking collectives  35.7 us (40%)
  starting transfers between devices  22.5 us (25%)
  Pallas kernels  12.9 us (14%)
  waiting for transfers between devices  12.8 us (14%)
  between operations  2.76 us (3%)
  other arithmetic  1.11 us (1%)
    ppermute x15, starting transfers between devices, moved(): return lax.ppermute(x, axis, [(i, (i + by) % n) for i in range(n)])  22.5 us
    all_to_all x1, blocking collectives, body(): parts = lax.all_to_all(second_sum(ins), 'z', 0, 0, tiled=True)  17.9 us
    all_to_all x1, blocking collectives, body(): lax.all_to_all(sent, BLK, 0, 0, tiled=True)  17.8 us
    ppermute x15, waiting for transfers between devices, moved(): return lax.ppermute(x, axis, [(i, (i + by) % n) for i in range(n)])  12.8 us
    pallas_call x1, Pallas kernels, half_transform(): pl.pallas_call(half_kernel, out_shape=jax.ShapeDtypeStruct((OCC, ROWS, VI...  4.36 us
    pallas_call x1, Pallas kernels, partial(): pl.pallas_call(along_y_kernel, out_shape=outs + [jax.ShapeDtypeStruct((2,...  2.58 us
    pallas_call x1, Pallas kernels, partial(): pl.pallas_call(along_x_kernel, out_shape=outs, in_specs=[SMEM, VMEM, VMEM...  1.94 us
  transfers between devices with their start and end apart: 15, of which 6 were waited for; matrix products, arithmetic and copies ran while one was open for 2% of the time, Pallas kernels for 4%

profile of v4, /device:TPU:1, one launch (start us, length us, event | category | flops | bytes accessed | tf_op | source)
XLA Modules:
  0.0 88.7 jit_solution(14685783002158825323)
XLA Ops:
  0.6 0.0 copy-start
  1.3 4.4 %shard_map.95.own_ref = bf16[8,256,256]{2,1,0:T(8,128)(2,1)S(1)} custom-call(s32[12]{0:T(128)} %block_hbm.1, s32[12]{0:T(128)} %kind_hbm.1, s32[1]{0:T(128)S(6)} %copy.10.live_hbm, bf16[12,8,128,128]{3,2,1,0:T(8,128)(2,1)} %three_ref.1, bf16[6144,256]{1,0:T(8,128)(2,1)} %coef_ref.1), custom_call_target="tpu_custom_call" | custom-call | tf_op jit(solution)/shard_map/pallas_call | solution.py:78
  5.7 3.3 %collective-permute-start = (bf16[8,256,256]{2,1,0:T(8,128)(2,1)S(1)}, bf16[8,256,256]{2,1,0:T(8,128)(2,1)S(1)}, u32[]{:S(2)}, u32[]{:S(2)}) collective-permute-start(bf16[8,256,256]{2,1,0:T(8,128)(2,1)S(1)} %shard_map.95.own_ref), channel_id=1, source_target_pairs={{0,1},{1,0},{2,3},{3,2},{4,5},{5,4},{6,7},{7,6},{8,9},{9,8},{10,11... | collective-permute-start | bytes 3145736 | tf_op jit(solution)/shard_map/ppermute | solution.py:310
  9.0 0.1 reshape.25
  9.2 0.6 gather_fusion
  9.8 0.7 fusion.6
  11.7 0.1 stack.23.place_ref.refs_0_
  11.9 0.1 subtract_subtract_fusion.below_ref
  12.0 0.0 collective-permute-done.other_ref
  12.0 2.6 %shard_map.96 = (bf16[2,2,4,2,64,128]{5,4,3,2,1,0:T(8,128)(2,1)S(1)}, bf16[2,2,4,2,64,128]{5,4,3,2,1,0:T(8,128)(2,1)S(1)}, bf16[2,4,2,64,128]{4,3,2,1,0:T(8,128)...) custom-call(s32[5]{0:T(128)S(1)} %stack.23.place_ref.refs_0_, ...), custom_call_target="tpu_custom_call" | custom-call | tf_op jit(solution)/shard_map/pallas_call | solution.py:174
  14.6 0.1 collective-permute-start.1
  14.7 2.7 %collective-permute-start.2 = (bf16[2,2,4,2,64,128]{5,4,3,2,1,0:T(8,128)(2,1)S(1)}, bf16[2,2,4,2,64,128]{5,4,3,2,1,0:T(8,128)(2,1)S(1)}, u32[]{:S(2)}, u32[]{:S(2)}) collective-permute-start(bf16[2,2,4,2,64,128]{5,4,3,2,1,0:T(8,128)(2,1)S(1)} %get-tuple-element.28), channel_id=1, source_target_pairs={{0,96},{32,0},{64,32},{96,64},{1,97},{33,1},{65,33},{97,65},{2,98}... | collective-permute-start | bytes 1572872 | tf_op jit(solution)/shard_map/ppermute | solution.py:310
  17.3 1.9 %shard_map.98 = (bf16[2,2,4,2,64,128]{5,4,3,2,1,0:T(8,128)(2,1)S(1)}, bf16[2,2,4,2,64,128]{5,4,3,2,1,0:T(8,128)(2,1)S(1)}, bf16[2,4,2,64,128]{4,3,2,1,0:T(8,128)...) custom-call(s32[5]{0:T(128)S(1)} %stack.23.place_ref.refs_0_, ...), custom_call_target="tpu_custom_call" | custom-call | tf_op jit(solution)/shard_map/pallas_call | solution.py:182
  19.3 0.1 collective-permute-start.8
  19.4 2.7 %collective-permute-start.9 = (bf16[2,2,4,2,64,128]{5,4,3,2,1,0:T(8,128)(2,1)S(1)}, bf16[2,2,4,2,64,128]{5,4,3,2,1,0:T(8,128)(2,1)S(1)}, u32[]{:S(2)}, u32[]{:S(2)}) collective-permute-start(bf16[2,2,4,2,64,128]{5,4,3,2,1,0:T(8,128)(2,1)S(1)} %get-tuple-element.38), channel_id=1, source_target_pairs={{0,130},{2,0},{128,2},{130,128},{1,131},{3,1},{129,3},{131,129},{4... | collective-permute-start | bytes 1572872 | tf_op jit(solution)/shard_map/ppermute | solution.py:310
  22.0 7.3 %collective-permute-done.1.refs_2_ = bf16[2,2,4,2,64,128]{5,4,3,2,1,0:T(8,128)(2,1)S(1)} collective-permute-done((bf16[2,2,4,2,64,128]{5,4,3,2,1,0:T(8,128)(2,1)S(1)}, bf16[2,2,4,2,64,128]{5,4,3,2,1,0:T(8,128)(2,1)S(1)}, u32[]{:S(2)}, u32[]{:S(2)}) %collective-permute-start.1) | collective-permute-done | bytes 524320 | tf_op jit(solution)/shard_map/ppermute | solution.py:310
  29.3 0.1 fusion.3
  29.4 0.1 collective-permute-start.3
  29.5 0.0 collective-permute-done.2.refs_3_
  29.5 0.1 fusion.2
  29.6 2.7 %collective-permute-start.4 = (bf16[2,4,2,64,128]{4,3,2,1,0:T(8,128)(2,1)S(1)}, bf16[2,4,2,64,128]{4,3,2,1,0:T(8,128)(2,1)S(1)}, u32[]{:S(2)}, u32[]{:S(2)}) collective-permute-start(bf16[2,4,2,64,128]{4,3,2,1,0:T(8,128)(2,1)S(1)} %fusion.2), channel_id=1, source_target_pairs={{0,96},{32,0},{64,32},{96,64},{1,97},{33,1},{65,33},{97,65},{2,98}... | collective-permute-start | bytes 786440 | tf_op jit(solution)/shard_map/ppermute | solution.py:310
  32.3 1.1 %collective-permute-done.8.refs_2_ = bf16[2,2,4,2,64,128]{5,4,3,2,1,0:T(8,128)(2,1)S(1)} collective-permute-done((bf16[2,2,4,2,64,128]{5,4,3,2,1,0:T(8,128)(2,1)S(1)}, bf16[2,2,4,2,64,128]{5,4,3,2,1,0:T(8,128)(2,1)S(1)}, u32[]{:S(2)}, u32[]{:S(2)}) %collective-permute-start.8) | collective-permute-done | bytes 524320 | tf_op jit(solution)/shard_map/ppermute | solution.py:310
  33.4 0.1 fusion.1
  33.5 0.1 collective-permute-start.10
  33.6 0.0 collective-permute-done.9.refs_3_
  33.6 0.1 fusion
  33.7 2.7 %collective-permute-start.11 = (bf16[2,4,2,64,128]{4,3,2,1,0:T(8,128)(2,1)S(1)}, bf16[2,4,2,64,128]{4,3,2,1,0:T(8,128)(2,1)S(1)}, u32[]{:S(2)}, u32[]{:S(2)}) collective-permute-start(bf16[2,4,2,64,128]{4,3,2,1,0:T(8,128)(2,1)S(1)} %fusion), channel_id=1, source_target_pairs={{0,130},{2,0},{128,2},{130,128},{1,131},{3,1},{129,3},{131,129},{4... | collective-permute-start | bytes 786440 | tf_op jit(solution)/shard_map/ppermute | solution.py:310
  36.4 1.3 %collective-permute-done.3.refs_4_ = bf16[2,4,2,64,128]{4,3,2,1,0:T(8,128)(2,1)S(1)} collective-permute-done((bf16[2,4,2,64,128]{4,3,2,1,0:T(8,128)(2,1)S(1)}, bf16[2,4,2,64,128]{4,3,2,1,0:T(8,128)(2,1)S(1)}, u32[]{:S(2)}, u32[]{:S(2)}) %collective-permute-start.3) | collective-permute-done | bytes 262176 | tf_op jit(solution)/shard_map/ppermute | solution.py:310
  37.7 0.0 collective-permute-done.4.refs_5_
  37.7 0.8 shard_map.97
  38.5 1.5 %collective-permute-start.5 = (bf16[4,2,64,128]{3,2,1,0:T(8,128)(2,1)S(1)}, bf16[4,2,64,128]{3,2,1,0:T(8,128)(2,1)S(1)}, u32[]{:S(2)}, u32[]{:S(2)}) collective-permute-start(bf16[4,2,64,128]{3,2,1,0:T(8,128)(2,1)S(1)} %get-tuple-element.32), channel_id=1, source_target_pairs={{0,128},{2,130},{128,0},{130,2},{1,129},{3,131},{129,1},{131,3},{4... | collective-permute-start | bytes 393224 | tf_op jit(solution)/shard_map/ppermute | solution.py:310
  40.0 0.3 collective-permute-start.6
  40.4 2.3 %collective-permute-start.7 = (bf16[4,2,64,128]{3,2,1,0:T(8,128)(2,1)S(1)}, bf16[4,2,64,128]{3,2,1,0:T(8,128)(2,1)S(1)}, u32[]{:S(2)}, u32[]{:S(2)}) collective-permute-start(bf16[4,2,64,128]{3,2,1,0:T(8,128)(2,1)S(1)} %get-tuple-element.34), channel_id=1, source_target_pairs={{0,130},{2,0},{128,2},{130,128},{1,131},{3,1},{129,3},{131,129},{4... | collective-permute-start | bytes 393224 | tf_op jit(solution)/shard_map/ppermute | solution.py:310
  42.7 0.0 collective-permute-done.10.refs_4_
  42.7 0.0 collective-permute-done.11.refs_5_
  42.7 0.8 shard_map.99
  43.5 1.2 %collective-permute-start.12 = (bf16[4,2,64,128]{3,2,1,0:T(8,128)(2,1)S(1)}, bf16[4,2,64,128]{3,2,1,0:T(8,128)(2,1)S(1)}, u32[]{:S(2)}, u32[]{:S(2)}) collective-permute-start(bf16[4,2,64,128]{3,2,1,0:T(8,128)(2,1)S(1)} %get-tuple-element.42), channel_id=1, source_target_pairs={{0,64},{32,96},{64,0},{96,32},{1,65},{33,97},{65,1},{97,33},{2,66}... | collective-permute-start | bytes 393224 | tf_op jit(solution)/shard_map/ppermute | solution.py:310
  44.7 2.0 %collective-permute-start.13 = (bf16[4,2,64,128]{3,2,1,0:T(8,128)(2,1)S(1)}, bf16[4,2,64,128]{3,2,1,0:T(8,128)(2,1)S(1)}, u32[]{:S(2)}, u32[]{:S(2)}) collective-permute-start(bf16[4,2,64,128]{3,2,1,0:T(8,128)(2,1)S(1)} %get-tuple-element.43), channel_id=1, source_target_pairs={{0,32},{32,64},{64,96},{96,0},{1,33},{33,65},{65,97},{97,1},{2,34}... | collective-permute-start | bytes 393224 | tf_op jit(solution)/shard_map/ppermute | solution.py:310
  46.7 0.7 collective-permute-start.14
  47.4 0.0 collective-permute-done.6.refs_2_
  47.4 1.6 %collective-permute-done.12.refs_5_ = bf16[4,2,64,128]{3,2,1,0:T(8,128)(2,1)S(1)} collective-permute-done((bf16[4,2,64,128]{3,2,1,0:T(8,128)(2,1)S(1)}, bf16[4,2,64,128]{3,2,1,0:T(8,128)(2,1)S(1)}, u32[]{:S(2)}, u32[]{:S(2)}) %collective-permute-start.12) | collective-permute-done | bytes 131104 | tf_op jit(solution)/shard_map/ppermute | solution.py:310
  49.0 1.3 %collective-permute-done.13.refs_6_ = bf16[4,2,64,128]{3,2,1,0:T(8,128)(2,1)S(1)} collective-permute-done((bf16[4,2,64,128]{3,2,1,0:T(8,128)(2,1)S(1)}, bf16[4,2,64,128]{3,2,1,0:T(8,128)(2,1)S(1)}, u32[]{:S(2)}, u32[]{:S(2)}) %collective-permute-start.13) | collective-permute-done | bytes 131104 | tf_op jit(solution)/shard_map/ppermute | solution.py:310
  50.4 0.2 collective-permute-done.14.refs_7_
  50.5 0.3 shard_map.100
  50.9 17.9 %all_to_all.10.parts_ref = s16[8,144,128]{2,1,0:T(8,128)(2,1)S(1)} all-to-all(s16[8,144,128]{2,1,0:T(8,128)(2,1)S(1)} %shard_map.100), channel_id=1, replica_groups=mesh['xh'=2,'y'=4,'z'=8,'xl'=2,'core'=2] {'z'}, dimensions={0} | all-to-all | bytes 589824 | tf_op jit(solution)/shard_map/all_to_all | solution.py:342
  68.8 0.9 %shard_map.101 = f32[32,8,128]{2,1,0:T(8,128)S(1)} custom-call(s32[5]{0:T(128)S(1)} %stack.23.place_ref.refs_0_, s16[8,144,128]{2,1,0:T(8,128)(2,1)S(1)} %all_to_all.10.parts_ref, f32[2,64,128]{2,1,0:T(8,128)S(1)} %subtract_subtract_fusion.below_ref), custom_call_target="tpu_custom_call" | custom-call | tf_op jit(solution)/shard_map/pallas_call | solution.py:269
  69.7 17.8 %all_to_all.11.parts_ref = f32[32,8,128]{2,1,0:T(8,128)S(1)} all-to-all(f32[32,8,128]{2,1,0:T(8,128)S(1)} %shard_map.101), channel_id=1, replica_groups=mesh['xh'=2,'y'=4,'z'=8,'xl'=2,'core'=2] {'z','xl','core'}, dimensions={0} | all-to-all | bytes 262144 | tf_op jit(solution)/shard_map/all_to_all | solution.py:344
  87.5 1.2 %shard_map.102 = (f32[8,8,256]{2,1,0:T(8,128)}, f32[1,8]{1,0:T(1,128)}) custom-call(s32[5]{0:T(128)S(1)} %stack.23.place_ref.refs_0_, f32[32,8,128]{2,1,0:T(8,128)S(1)} %all_to_all.11.parts_ref), custom_call_target="tpu_custom_call" | custom-call | tf_op jit(solution)/shard_map/pallas_call | solution.py:299
  (13 shorter events, 0.1 us)
Async XLA Ops:
  0.6 8.5 %copy-start = (f32[4000]{0:T(1024)S(1)}, f32[4000]{0:T(1024)}, u32[]{:S(2)}) copy-start(f32[4000]{0:T(1024)} %param.13) | copy-start | bytes 48004
  1.3 7.7 %copy-start.2 = (s32[8]{0:T(128)S(1)}, s32[8]{0:T(128)}, u32[]{:S(2)}) copy-start(s32[8]{0:T(128)} %param.15) | copy-start | bytes 100
  1.3 7.7 %copy-start.1 = (f32[256]{0:T(256)S(1)}, f32[256]{0:T(256)}, u32[]{:S(2)}) copy-start(f32[256]{0:T(256)} %param.14) | copy-start | bytes 3076
  5.7 6.3 %collective-permute-start = (bf16[8,256,256]{2,1,0:T(8,128)(2,1)S(1)}, bf16[8,256,256]{2,1,0:T(8,128)(2,1)S(1)}, u32[]{:S(2)}, u32[]{:S(2)}) collective-permute-start(bf16[8,256,256]{2,1,0:T(8,128)(2,1)S(1)} %shard_map.95.own_ref), channel_id=1, source_target_pairs={{0,1},{1,0},{2,3},{3,2},{4,5},{5,4},{6,7},{7,6},{8,9},{9,8},{10,11... | collective-permute-start | bytes 3145736 | tf_op jit(solution)/shard_map/ppermute | solution.py:310
  14.6 14.8 %collective-permute-start.1 = (bf16[2,2,4,2,64,128]{5,4,3,2,1,0:T(8,128)(2,1)S(1)}, bf16[2,2,4,2,64,128]{5,4,3,2,1,0:T(8,128)(2,1)S(1)}, u32[]{:S(2)}, u32[]{:S(2)}) collective-permute-start(bf16[2,2,4,2,64,128]{5,4,3,2,1,0:T(8,128)(2,1)S(1)} %get-tuple-element.27), channel_id=1, source_target_pairs={{0,32},{32,64},{64,96},{96,0},{1,33},{33,65},{65,97},{97,1},{2,34}... | collective-permute-start | bytes 1572872 | tf_op jit(solution)/shard_map/ppermute | solution.py:310
  14.7 14.9 %collective-permute-start.2 = (bf16[2,2,4,2,64,128]{5,4,3,2,1,0:T(8,128)(2,1)S(1)}, bf16[2,2,4,2,64,128]{5,4,3,2,1,0:T(8,128)(2,1)S(1)}, u32[]{:S(2)}, u32[]{:S(2)}) collective-permute-start(bf16[2,2,4,2,64,128]{5,4,3,2,1,0:T(8,128)(2,1)S(1)} %get-tuple-element.28), channel_id=1, source_target_pairs={{0,96},{32,0},{64,32},{96,64},{1,97},{33,1},{65,33},{97,65},{2,98}... | collective-permute-start | bytes 1572872 | tf_op jit(solution)/shard_map/ppermute | solution.py:310
  19.3 14.1 %collective-permute-start.8 = (bf16[2,2,4,2,64,128]{5,4,3,2,1,0:T(8,128)(2,1)S(1)}, bf16[2,2,4,2,64,128]{5,4,3,2,1,0:T(8,128)(2,1)S(1)}, u32[]{:S(2)}, u32[]{:S(2)}) collective-permute-start(bf16[2,2,4,2,64,128]{5,4,3,2,1,0:T(8,128)(2,1)S(1)} %get-tuple-element.37), channel_id=1, source_target_pairs={{0,2},{2,128},{128,130},{130,0},{1,3},{3,129},{129,131},{131,1},{4... | collective-permute-start | bytes 1572872 | tf_op jit(solution)/shard_map/ppermute | solution.py:310
  19.4 14.2 %collective-permute-start.9 = (bf16[2,2,4,2,64,128]{5,4,3,2,1,0:T(8,128)(2,1)S(1)}, bf16[2,2,4,2,64,128]{5,4,3,2,1,0:T(8,128)(2,1)S(1)}, u32[]{:S(2)}, u32[]{:S(2)}) collective-permute-start(bf16[2,2,4,2,64,128]{5,4,3,2,1,0:T(8,128)(2,1)S(1)} %get-tuple-element.38), channel_id=1, source_target_pairs={{0,130},{2,0},{128,2},{130,128},{1,131},{3,1},{129,3},{131,129},{4... | collective-permute-start | bytes 1572872 | tf_op jit(solution)/shard_map/ppermute | solution.py:310
  29.4 8.3 %collective-permute-start.3 = (bf16[2,4,2,64,128]{4,3,2,1,0:T(8,128)(2,1)S(1)}, bf16[2,4,2,64,128]{4,3,2,1,0:T(8,128)(2,1)S(1)}, u32[]{:S(2)}, u32[]{:S(2)}) collective-permute-start(bf16[2,4,2,64,128]{4,3,2,1,0:T(8,128)(2,1)S(1)} %fusion.3), channel_id=1, source_target_pairs={{0,32},{32,64},{64,96},{96,0},{1,33},{33,65},{65,97},{97,1},{2,34}... | collective-permute-start | bytes 786440 | tf_op jit(solution)/shard_map/ppermute | solution.py:310
  29.6 8.1 %collective-permute-start.4 = (bf16[2,4,2,64,128]{4,3,2,1,0:T(8,128)(2,1)S(1)}, bf16[2,4,2,64,128]{4,3,2,1,0:T(8,128)(2,1)S(1)}, u32[]{:S(2)}, u32[]{:S(2)}) collective-permute-start(bf16[2,4,2,64,128]{4,3,2,1,0:T(8,128)(2,1)S(1)} %fusion.2), channel_id=1, source_target_pairs={{0,96},{32,0},{64,32},{96,64},{1,97},{33,1},{65,33},{97,65},{2,98}... | collective-permute-start | bytes 786440 | tf_op jit(solution)/shard_map/ppermute | solution.py:310
  33.5 9.2 %collective-permute-start.10 = (bf16[2,4,2,64,128]{4,3,2,1,0:T(8,128)(2,1)S(1)}, bf16[2,4,2,64,128]{4,3,2,1,0:T(8,128)(2,1)S(1)}, u32[]{:S(2)}, u32[]{:S(2)}) collective-permute-start(bf16[2,4,2,64,128]{4,3,2,1,0:T(8,128)(2,1)S(1)} %fusion.1), channel_id=1, source_target_pairs={{0,2},{2,128},{128,130},{130,0},{1,3},{3,129},{129,131},{131,1},{4... | collective-permute-start | bytes 786440 | tf_op jit(solution)/shard_map/ppermute | solution.py:310
  33.7 9.1 %collective-permute-start.11 = (bf16[2,4,2,64,128]{4,3,2,1,0:T(8,128)(2,1)S(1)}, bf16[2,4,2,64,128]{4,3,2,1,0:T(8,128)(2,1)S(1)}, u32[]{:S(2)}, u32[]{:S(2)}) collective-permute-start(bf16[2,4,2,64,128]{4,3,2,1,0:T(8,128)(2,1)S(1)} %fusion), channel_id=1, source_target_pairs={{0,130},{2,0},{128,2},{130,128},{1,131},{3,1},{129,3},{131,129},{4... | collective-permute-start | bytes 786440 | tf_op jit(solution)/shard_map/ppermute | solution.py:310
  38.5 8.2 %collective-permute-start.5 = (bf16[4,2,64,128]{3,2,1,0:T(8,128)(2,1)S(1)}, bf16[4,2,64,128]{3,2,1,0:T(8,128)(2,1)S(1)}, u32[]{:S(2)}, u32[]{:S(2)}) collective-permute-start(bf16[4,2,64,128]{3,2,1,0:T(8,128)(2,1)S(1)} %get-tuple-element.32), channel_id=1, source_target_pairs={{0,128},{2,130},{128,0},{130,2},{1,129},{3,131},{129,1},{131,3},{4... | collective-permute-start | bytes 393224 | tf_op jit(solution)/shard_map/ppermute | solution.py:310
  40.0 7.4 %collective-permute-start.6 = (bf16[4,2,64,128]{3,2,1,0:T(8,128)(2,1)S(1)}, bf16[4,2,64,128]{3,2,1,0:T(8,128)(2,1)S(1)}, u32[]{:S(2)}, u32[]{:S(2)}) collective-permute-start(bf16[4,2,64,128]{3,2,1,0:T(8,128)(2,1)S(1)} %get-tuple-element.33), channel_id=1, source_target_pairs={{0,2},{2,128},{128,130},{130,0},{1,3},{3,129},{129,131},{131,1},{4... | collective-permute-start | bytes 393224 | tf_op jit(solution)/shard_map/ppermute | solution.py:310
  40.4 7.1 %collective-permute-start.7 = (bf16[4,2,64,128]{3,2,1,0:T(8,128)(2,1)S(1)}, bf16[4,2,64,128]{3,2,1,0:T(8,128)(2,1)S(1)}, u32[]{:S(2)}, u32[]{:S(2)}) collective-permute-start(bf16[4,2,64,128]{3,2,1,0:T(8,128)(2,1)S(1)} %get-tuple-element.34), channel_id=1, source_target_pairs={{0,130},{2,0},{128,2},{130,128},{1,131},{3,1},{129,3},{131,129},{4... | collective-permute-start | bytes 393224 | tf_op jit(solution)/shard_map/ppermute | solution.py:310
  43.5 5.5 %collective-permute-start.12 = (bf16[4,2,64,128]{3,2,1,0:T(8,128)(2,1)S(1)}, bf16[4,2,64,128]{3,2,1,0:T(8,128)(2,1)S(1)}, u32[]{:S(2)}, u32[]{:S(2)}) collective-permute-start(bf16[4,2,64,128]{3,2,1,0:T(8,128)(2,1)S(1)} %get-tuple-element.42), channel_id=1, source_target_pairs={{0,64},{32,96},{64,0},{96,32},{1,65},{33,97},{65,1},{97,33},{2,66}... | collective-permute-start | bytes 393224 | tf_op jit(solution)/shard_map/ppermute | solution.py:310
  44.7 5.6 %collective-permute-start.13 = (bf16[4,2,64,128]{3,2,1,0:T(8,128)(2,1)S(1)}, bf16[4,2,64,128]{3,2,1,0:T(8,128)(2,1)S(1)}, u32[]{:S(2)}, u32[]{:S(2)}) collective-permute-start(bf16[4,2,64,128]{3,2,1,0:T(8,128)(2,1)S(1)} %get-tuple-element.43), channel_id=1, source_target_pairs={{0,32},{32,64},{64,96},{96,0},{1,33},{33,65},{65,97},{97,1},{2,34}... | collective-permute-start | bytes 393224 | tf_op jit(solution)/shard_map/ppermute | solution.py:310
  46.7 3.8 %collective-permute-start.14 = (bf16[4,2,64,128]{3,2,1,0:T(8,128)(2,1)S(1)}, bf16[4,2,64,128]{3,2,1,0:T(8,128)(2,1)S(1)}, u32[]{:S(2)}, u32[]{:S(2)}) collective-permute-start(bf16[4,2,64,128]{3,2,1,0:T(8,128)(2,1)S(1)} %get-tuple-element.44), channel_id=1, source_target_pairs={{0,96},{32,0},{64,32},{96,64},{1,97},{33,1},{65,33},{97,65},{2,98}... | collective-permute-start | bytes 393224 | tf_op jit(solution)/shard_map/ppermute | solution.py:310

commit v5 on v4

--- a/solution.py
+++ b/solution.py
@@ -215,6 +215,14 @@
     )(place, *ins)
 
 
+def largest(x):
+    return jnp.max(jnp.abs(x), axis=(0, 1), keepdims=True)
+
+
+def power_above(x):
+    return jnp.ceil(jnp.log2(jnp.maximum(x, TINY)))
+
+
 def second_sum_kernel(*refs):
     ins, out = refs[:8], refs[8]
     for half in range(2):
@@ -223,8 +231,7 @@
             for d in range(1, 4):
                 total = total + ins[half * 4 + d][j].astype(F32)
             total = total.reshape(128, 128)
-            largest = jnp.max(jnp.abs(total), axis=(0, 1), keepdims=True)
-            power = jnp.ceil(jnp.log2(jnp.maximum(largest, TINY)))
+            power = power_above(largest(total))
             steps = jnp.round(total * jnp.exp2(-power) * STEPS)
             out[half * 4 + j, 0:128] = steps.astype(jnp.int32).astype(jnp.int16)
             out[half * 4 + j, 128:144] = jnp.broadcast_to(power, (16, 128)).astype(jnp.int32).astype(jnp.int16)
@@ -257,18 +264,26 @@
     amplitudes = [total[half] / below_ref[half] for half in range(2)]
     terms = [amplitudes[half] * (2.0 * total[half] - crossed[half]) for half in range(2)]
     energy = jnp.sum(terms[0] + terms[1], axis=(0, 1), keepdims=True)
+    power = power_above(jnp.maximum(largest(amplitudes[0]), largest(amplitudes[1])))
+    power_energy = power_above(jnp.abs(energy))
+    scaled = energy * jnp.exp2(-power_energy) * STEPS
+    high = jnp.round(scaled)
     lane = lax.broadcasted_iota(jnp.int32, (64, 128), 1)
+    which = lax.rem(lane, 4)
+    rest = jnp.where(which == 2, high, jnp.round((scaled - high) * STEPS))
+    rest = jnp.where(which == 0, power, jnp.where(which == 1, power_energy, rest))
     quarter = lax.rem(lane // 64 + low, 2)
     for half in range(2):
+        coded = jnp.round(amplitudes[half] * jnp.exp2(-power) * STEPS)
         for q in range(2):
-            sent = jnp.where(quarter == q, amplitudes[half], jnp.broadcast_to(energy, (64, 128)))
-            out_ref[pl.ds(half * 16 + q * 8, 8)] = sent.reshape(8, 8, 128)
+            sent = jnp.where(quarter == q, coded, rest).astype(jnp.int32).reshape(8, 8, 128)
+            out_ref[pl.ds(half * 16 + q * 8, 8)] = sent.astype(jnp.int16)
 
 
 def finish(place, parts, below):
     return pl.pallas_call(
         finish_kernel,
-        out_shape=jax.ShapeDtypeStruct((32, 8, 128), F32),
+        out_shape=jax.ShapeDtypeStruct((32, 8, 128), jnp.int16),
         in_specs=[SMEM, VMEM, VMEM],
         out_specs=VMEM,
         compiler_params=params(6),
@@ -280,17 +295,28 @@
     half, quarter = block // 16, lax.rem(block // 8, 2)
     lane = lax.broadcasted_iota(jnp.int32, (8, 128), 1)
     ours = lane // 64 == quarter
+    coded, rests = [], []
+    for j in range(OCC):
+        for side in range(2):
+            core = lax.rem(half + side, 2)
+            one, two = (parts_ref[j * 4 + low * 2 + core].astype(jnp.int32).astype(F32) for low in range(2))
+            coded.append(jnp.where(ours, one, two))
+            rests.append(jnp.where(ours, two, one)[0:1])
+    rest = jnp.concatenate(rests, axis=0)
+    first = lax.broadcasted_iota(jnp.int32, (2 * OCC, 128), 1) < 64
+    scale = jnp.where(first, jnp.exp2(rest[:, 64:65]), jnp.exp2(rest[:, 0:1])) * (1.0 / STEPS)
+    shares = jnp.zeros((2 * OCC, 1), F32)
+    for at in (0, 64):
+        number = (rest[:, at + 2 : at + 3] + rest[:, at + 3 : at + 4] * (1.0 / STEPS)) * (1.0 / STEPS)
+        shares = shares + number * jnp.exp2(rest[:, at + 1 : at + 2])
     energies = jnp.zeros((8, 128), F32)
     for j in range(OCC):
-        rest = jnp.zeros((8, 128), F32)
         for side in range(2):
-            core = lax.rem(half + side, 2)
-            one, two = parts_ref[j * 4 + core], parts_ref[j * 4 + 2 + core]
-            amp = jnp.where(ours, one, two)
-            rest = rest + jnp.where(ours, two, one)
+            k = 2 * j + side
+            amp = coded[k] * scale[k : k + 1]
             for r in range(8):
                 amp_ref[r, pl.ds(j, 1), pl.ds(side * 128, 128)] = amp[r : r + 1, :]
-        total = rest[:, 0:1] + rest[:, 64:65]
+        total = shares[2 * j : 2 * j + 1] + shares[2 * j + 1 : 2 * j + 2]
         energies = jnp.where(lane == j, jnp.broadcast_to(total, (8, 128)), energies)
     pair_ref[...] = energies[0:1, 0:OCC]
 

time: 89 us -> 88.2 us (level)
  blocking collectives: 35.7 us -> 34.6 us
    all_to_all x1, blocking collectives: 17.8 us -> 16.7 us  [body(): lax.all_to_all(sent, BLK, 0, 0, tiled=True)]
where the time goes in v5:
time: 88.2 us; the launch traced here: 87.9 us
  blocking collectives  34.6 us (39%)
  starting transfers between devices  22.5 us (26%)
  Pallas kernels  13.2 us (15%)
  waiting for transfers between devices  12.9 us (15%)
  between operations  2.76 us (3%)
  other arithmetic  1.11 us (1%)
    ppermute x15, starting transfers between devices, moved(): return lax.ppermute(x, axis, [(i, (i + by) % n) for i in range(n)])  22.5 us
    all_to_all x1, blocking collectives, body(): parts = lax.all_to_all(second_sum(ins), 'z', 0, 0, tiled=True)  17.9 us
    all_to_all x1, blocking collectives, body(): lax.all_to_all(sent, BLK, 0, 0, tiled=True)  16.7 us
    ppermute x15, waiting for transfers between devices, moved(): return lax.ppermute(x, axis, [(i, (i + by) % n) for i in range(n)])  12.9 us
    pallas_call x1, Pallas kernels, half_transform(): pl.pallas_call(half_kernel, out_shape=jax.ShapeDtypeStruct((OCC, ROWS, VI...  4.36 us
    pallas_call x1, Pallas kernels, partial(): pl.pallas_call(along_y_kernel, out_shape=outs + [jax.ShapeDtypeStruct((2,...  2.58 us
    pallas_call x1, Pallas kernels, partial(): pl.pallas_call(along_x_kernel, out_shape=outs, in_specs=[SMEM, VMEM, VMEM...  1.94 us
  transfers between devices with their start and end apart: 15, of which 6 were waited for; matrix products, arithmetic and copies ran while one was open for 2% of the time, Pallas kernels for 4%

profile of v5, /device:TPU:1, one launch (start us, length us, event | category | flops | bytes accessed | tf_op | source)
XLA Modules:
  0.0 87.9 jit_solution(8488520818138814944)
XLA Ops:
  0.6 0.0 copy-start
  1.3 4.4 %shard_map.95.own_ref = bf16[8,256,256]{2,1,0:T(8,128)(2,1)S(1)} custom-call(s32[12]{0:T(128)} %block_hbm.1, s32[12]{0:T(128)} %kind_hbm.1, s32[1]{0:T(128)S(6)} %copy.10.live_hbm, bf16[12,8,128,128]{3,2,1,0:T(8,128)(2,1)} %three_ref.1, bf16[6144,256]{1,0:T(8,128)(2,1)} %coef_ref.1), custom_call_target="tpu_custom_call" | custom-call | tf_op jit(solution)/shard_map/pallas_call | solution.py:78
  5.7 3.3 %collective-permute-start = (bf16[8,256,256]{2,1,0:T(8,128)(2,1)S(1)}, bf16[8,256,256]{2,1,0:T(8,128)(2,1)S(1)}, u32[]{:S(2)}, u32[]{:S(2)}) collective-permute-start(bf16[8,256,256]{2,1,0:T(8,128)(2,1)S(1)} %shard_map.95.own_ref), channel_id=1, source_target_pairs={{0,1},{1,0},{2,3},{3,2},{4,5},{5,4},{6,7},{7,6},{8,9},{9,8},{10,11... | collective-permute-start | bytes 3145736 | tf_op jit(solution)/shard_map/ppermute | solution.py:336
  9.0 0.1 reshape.25
  9.2 0.6 gather_fusion
  9.8 0.7 fusion.6
  11.7 0.1 stack.23.place_ref.refs_0_
  11.9 0.1 subtract_subtract_fusion.below_ref
  12.0 0.0 collective-permute-done.other_ref
  12.0 2.6 %shard_map.96 = (bf16[2,2,4,2,64,128]{5,4,3,2,1,0:T(8,128)(2,1)S(1)}, bf16[2,2,4,2,64,128]{5,4,3,2,1,0:T(8,128)(2,1)S(1)}, bf16[2,4,2,64,128]{4,3,2,1,0:T(8,128)...) custom-call(s32[5]{0:T(128)S(1)} %stack.23.place_ref.refs_0_, ...), custom_call_target="tpu_custom_call" | custom-call | tf_op jit(solution)/shard_map/pallas_call | solution.py:174
  14.6 0.1 collective-permute-start.1
  14.7 2.7 %collective-permute-start.2 = (bf16[2,2,4,2,64,128]{5,4,3,2,1,0:T(8,128)(2,1)S(1)}, bf16[2,2,4,2,64,128]{5,4,3,2,1,0:T(8,128)(2,1)S(1)}, u32[]{:S(2)}, u32[]{:S(2)}) collective-permute-start(bf16[2,2,4,2,64,128]{5,4,3,2,1,0:T(8,128)(2,1)S(1)} %get-tuple-element.28), channel_id=1, source_target_pairs={{0,96},{32,0},{64,32},{96,64},{1,97},{33,1},{65,33},{97,65},{2,98}... | collective-permute-start | bytes 1572872 | tf_op jit(solution)/shard_map/ppermute | solution.py:336
  17.3 1.9 %shard_map.98 = (bf16[2,2,4,2,64,128]{5,4,3,2,1,0:T(8,128)(2,1)S(1)}, bf16[2,2,4,2,64,128]{5,4,3,2,1,0:T(8,128)(2,1)S(1)}, bf16[2,4,2,64,128]{4,3,2,1,0:T(8,128)...) custom-call(s32[5]{0:T(128)S(1)} %stack.23.place_ref.refs_0_, ...), custom_call_target="tpu_custom_call" | custom-call | tf_op jit(solution)/shard_map/pallas_call | solution.py:182
  19.3 0.1 collective-permute-start.8
  19.4 2.7 %collective-permute-start.9 = (bf16[2,2,4,2,64,128]{5,4,3,2,1,0:T(8,128)(2,1)S(1)}, bf16[2,2,4,2,64,128]{5,4,3,2,1,0:T(8,128)(2,1)S(1)}, u32[]{:S(2)}, u32[]{:S(2)}) collective-permute-start(bf16[2,2,4,2,64,128]{5,4,3,2,1,0:T(8,128)(2,1)S(1)} %get-tuple-element.38), channel_id=1, source_target_pairs={{0,130},{2,0},{128,2},{130,128},{1,131},{3,1},{129,3},{131,129},{4... | collective-permute-start | bytes 1572872 | tf_op jit(solution)/shard_map/ppermute | solution.py:336
  22.0 7.3 %collective-permute-done.1.refs_2_ = bf16[2,2,4,2,64,128]{5,4,3,2,1,0:T(8,128)(2,1)S(1)} collective-permute-done((bf16[2,2,4,2,64,128]{5,4,3,2,1,0:T(8,128)(2,1)S(1)}, bf16[2,2,4,2,64,128]{5,4,3,2,1,0:T(8,128)(2,1)S(1)}, u32[]{:S(2)}, u32[]{:S(2)}) %collective-permute-start.1) | collective-permute-done | bytes 524320 | tf_op jit(solution)/shard_map/ppermute | solution.py:336
  29.3 0.1 fusion.3
  29.4 0.1 collective-permute-start.3
  29.5 0.0 collective-permute-done.2.refs_3_
  29.5 0.1 fusion.2
  29.6 2.7 %collective-permute-start.4 = (bf16[2,4,2,64,128]{4,3,2,1,0:T(8,128)(2,1)S(1)}, bf16[2,4,2,64,128]{4,3,2,1,0:T(8,128)(2,1)S(1)}, u32[]{:S(2)}, u32[]{:S(2)}) collective-permute-start(bf16[2,4,2,64,128]{4,3,2,1,0:T(8,128)(2,1)S(1)} %fusion.2), channel_id=1, source_target_pairs={{0,96},{32,0},{64,32},{96,64},{1,97},{33,1},{65,33},{97,65},{2,98}... | collective-permute-start | bytes 786440 | tf_op jit(solution)/shard_map/ppermute | solution.py:336
  32.3 1.1 %collective-permute-done.8.refs_2_ = bf16[2,2,4,2,64,128]{5,4,3,2,1,0:T(8,128)(2,1)S(1)} collective-permute-done((bf16[2,2,4,2,64,128]{5,4,3,2,1,0:T(8,128)(2,1)S(1)}, bf16[2,2,4,2,64,128]{5,4,3,2,1,0:T(8,128)(2,1)S(1)}, u32[]{:S(2)}, u32[]{:S(2)}) %collective-permute-start.8) | collective-permute-done | bytes 524320 | tf_op jit(solution)/shard_map/ppermute | solution.py:336
  33.4 0.1 fusion.1
  33.5 0.1 collective-permute-start.10
  33.6 0.0 collective-permute-done.9.refs_3_
  33.6 0.1 fusion
  33.7 2.7 %collective-permute-start.11 = (bf16[2,4,2,64,128]{4,3,2,1,0:T(8,128)(2,1)S(1)}, bf16[2,4,2,64,128]{4,3,2,1,0:T(8,128)(2,1)S(1)}, u32[]{:S(2)}, u32[]{:S(2)}) collective-permute-start(bf16[2,4,2,64,128]{4,3,2,1,0:T(8,128)(2,1)S(1)} %fusion), channel_id=1, source_target_pairs={{0,130},{2,0},{128,2},{130,128},{1,131},{3,1},{129,3},{131,129},{4... | collective-permute-start | bytes 786440 | tf_op jit(solution)/shard_map/ppermute | solution.py:336
  36.4 1.3 %collective-permute-done.3.refs_4_ = bf16[2,4,2,64,128]{4,3,2,1,0:T(8,128)(2,1)S(1)} collective-permute-done((bf16[2,4,2,64,128]{4,3,2,1,0:T(8,128)(2,1)S(1)}, bf16[2,4,2,64,128]{4,3,2,1,0:T(8,128)(2,1)S(1)}, u32[]{:S(2)}, u32[]{:S(2)}) %collective-permute-start.3) | collective-permute-done | bytes 262176 | tf_op jit(solution)/shard_map/ppermute | solution.py:336
  37.7 0.0 collective-permute-done.4.refs_5_
  37.7 0.8 shard_map.97
  38.5 1.5 %collective-permute-start.5 = (bf16[4,2,64,128]{3,2,1,0:T(8,128)(2,1)S(1)}, bf16[4,2,64,128]{3,2,1,0:T(8,128)(2,1)S(1)}, u32[]{:S(2)}, u32[]{:S(2)}) collective-permute-start(bf16[4,2,64,128]{3,2,1,0:T(8,128)(2,1)S(1)} %get-tuple-element.32), channel_id=1, source_target_pairs={{0,128},{2,130},{128,0},{130,2},{1,129},{3,131},{129,1},{131,3},{4... | collective-permute-start | bytes 393224 | tf_op jit(solution)/shard_map/ppermute | solution.py:336
  40.1 0.3 collective-permute-start.6
  40.4 2.4 %collective-permute-start.7 = (bf16[4,2,64,128]{3,2,1,0:T(8,128)(2,1)S(1)}, bf16[4,2,64,128]{3,2,1,0:T(8,128)(2,1)S(1)}, u32[]{:S(2)}, u32[]{:S(2)}) collective-permute-start(bf16[4,2,64,128]{3,2,1,0:T(8,128)(2,1)S(1)} %get-tuple-element.34), channel_id=1, source_target_pairs={{0,130},{2,0},{128,2},{130,128},{1,131},{3,1},{129,3},{131,129},{4... | collective-permute-start | bytes 393224 | tf_op jit(solution)/shard_map/ppermute | solution.py:336
  42.7 0.0 collective-permute-done.10.refs_4_
  42.7 0.8 shard_map.99
  43.6 1.2 %collective-permute-start.12 = (bf16[4,2,64,128]{3,2,1,0:T(8,128)(2,1)S(1)}, bf16[4,2,64,128]{3,2,1,0:T(8,128)(2,1)S(1)}, u32[]{:S(2)}, u32[]{:S(2)}) collective-permute-start(bf16[4,2,64,128]{3,2,1,0:T(8,128)(2,1)S(1)} %get-tuple-element.42), channel_id=1, source_target_pairs={{0,64},{32,96},{64,0},{96,32},{1,65},{33,97},{65,1},{97,33},{2,66}... | collective-permute-start | bytes 393224 | tf_op jit(solution)/shard_map/ppermute | solution.py:336
  44.8 2.0 %collective-permute-start.13 = (bf16[4,2,64,128]{3,2,1,0:T(8,128)(2,1)S(1)}, bf16[4,2,64,128]{3,2,1,0:T(8,128)(2,1)S(1)}, u32[]{:S(2)}, u32[]{:S(2)}) collective-permute-start(bf16[4,2,64,128]{3,2,1,0:T(8,128)(2,1)S(1)} %get-tuple-element.43), channel_id=1, source_target_pairs={{0,32},{32,64},{64,96},{96,0},{1,33},{33,65},{65,97},{97,1},{2,34}... | collective-permute-start | bytes 393224 | tf_op jit(solution)/shard_map/ppermute | solution.py:336
  46.8 0.0 collective-permute-done.5.refs_1_
  46.8 0.7 collective-permute-start.14
  47.4 0.0 collective-permute-done.6.refs_2_
  47.4 1.6 %collective-permute-done.12.refs_5_ = bf16[4,2,64,128]{3,2,1,0:T(8,128)(2,1)S(1)} collective-permute-done((bf16[4,2,64,128]{3,2,1,0:T(8,128)(2,1)S(1)}, bf16[4,2,64,128]{3,2,1,0:T(8,128)(2,1)S(1)}, u32[]{:S(2)}, u32[]{:S(2)}) %collective-permute-start.12) | collective-permute-done | bytes 131104 | tf_op jit(solution)/shard_map/ppermute | solution.py:336
  49.0 1.3 %collective-permute-done.13.refs_6_ = bf16[4,2,64,128]{3,2,1,0:T(8,128)(2,1)S(1)} collective-permute-done((bf16[4,2,64,128]{3,2,1,0:T(8,128)(2,1)S(1)}, bf16[4,2,64,128]{3,2,1,0:T(8,128)(2,1)S(1)}, u32[]{:S(2)}, u32[]{:S(2)}) %collective-permute-start.13) | collective-permute-done | bytes 131104 | tf_op jit(solution)/shard_map/ppermute | solution.py:336
  50.4 0.2 collective-permute-done.14.refs_7_
  50.6 0.3 shard_map.100
  50.9 17.9 %all_to_all.10.parts_ref = s16[8,144,128]{2,1,0:T(8,128)(2,1)S(1)} all-to-all(s16[8,144,128]{2,1,0:T(8,128)(2,1)S(1)} %shard_map.100), channel_id=1, replica_groups=mesh['xh'=2,'y'=4,'z'=8,'xl'=2,'core'=2] {'z'}, dimensions={0} | all-to-all | bytes 589824 | tf_op jit(solution)/shard_map/all_to_all | solution.py:368
  68.8 0.9 %shard_map.101 = s16[32,8,128]{2,1,0:T(8,128)(2,1)S(1)} custom-call(s32[5]{0:T(128)S(1)} %stack.23.place_ref.refs_0_, s16[8,144,128]{2,1,0:T(8,128)(2,1)S(1)} %all_to_all.10.parts_ref, f32[2,64,128]{2,1,0:T(8,128)S(1)} %subtract_subtract_fusion.below_ref), custom_call_target="tpu_custom_call" | custom-call | tf_op jit(solution)/shard_map/pallas_call | solution.py:284
  69.8 16.7 %all_to_all.11.parts_ref = s16[32,8,128]{2,1,0:T(8,128)(2,1)S(1)} all-to-all(s16[32,8,128]{2,1,0:T(8,128)(2,1)S(1)} %shard_map.101), channel_id=1, replica_groups=mesh['xh'=2,'y'=4,'z'=8,'xl'=2,'core'=2] {'z','xl','core'}, dimensions={0} | all-to-all | bytes 131072 | tf_op jit(solution)/shard_map/all_to_all | solution.py:370
  86.5 1.5 %shard_map.102 = (f32[8,8,256]{2,1,0:T(8,128)}, f32[1,8]{1,0:T(1,128)}) custom-call(s32[5]{0:T(128)S(1)} %stack.23.place_ref.refs_0_, s16[32,8,128]{2,1,0:T(8,128)(2,1)S(1)} %all_to_all.11.parts_ref), custom_call_target="tpu_custom_call" | custom-call | tf_op jit(solution)/shard_map/pallas_call | solution.py:325
  (13 shorter events, 0.1 us)
Async XLA Ops:
  0.6 8.5 %copy-start = (f32[4000]{0:T(1024)S(1)}, f32[4000]{0:T(1024)}, u32[]{:S(2)}) copy-start(f32[4000]{0:T(1024)} %param.13) | copy-start | bytes 48004
  1.3 7.7 %copy-start.2 = (s32[8]{0:T(128)S(1)}, s32[8]{0:T(128)}, u32[]{:S(2)}) copy-start(s32[8]{0:T(128)} %param.15) | copy-start | bytes 100
  1.3 7.7 %copy-start.1 = (f32[256]{0:T(256)S(1)}, f32[256]{0:T(256)}, u32[]{:S(2)}) copy-start(f32[256]{0:T(256)} %param.14) | copy-start | bytes 3076
  5.7 6.3 %collective-permute-start = (bf16[8,256,256]{2,1,0:T(8,128)(2,1)S(1)}, bf16[8,256,256]{2,1,0:T(8,128)(2,1)S(1)}, u32[]{:S(2)}, u32[]{:S(2)}) collective-permute-start(bf16[8,256,256]{2,1,0:T(8,128)(2,1)S(1)} %shard_map.95.own_ref), channel_id=1, source_target_pairs={{0,1},{1,0},{2,3},{3,2},{4,5},{5,4},{6,7},{7,6},{8,9},{9,8},{10,11... | collective-permute-start | bytes 3145736 | tf_op jit(solution)/shard_map/ppermute | solution.py:336
  14.6 14.8 %collective-permute-start.1 = (bf16[2,2,4,2,64,128]{5,4,3,2,1,0:T(8,128)(2,1)S(1)}, bf16[2,2,4,2,64,128]{5,4,3,2,1,0:T(8,128)(2,1)S(1)}, u32[]{:S(2)}, u32[]{:S(2)}) collective-permute-start(bf16[2,2,4,2,64,128]{5,4,3,2,1,0:T(8,128)(2,1)S(1)} %get-tuple-element.27), channel_id=1, source_target_pairs={{0,32},{32,64},{64,96},{96,0},{1,33},{33,65},{65,97},{97,1},{2,34}... | collective-permute-start | bytes 1572872 | tf_op jit(solution)/shard_map/ppermute | solution.py:336
  14.7 14.9 %collective-permute-start.2 = (bf16[2,2,4,2,64,128]{5,4,3,2,1,0:T(8,128)(2,1)S(1)}, bf16[2,2,4,2,64,128]{5,4,3,2,1,0:T(8,128)(2,1)S(1)}, u32[]{:S(2)}, u32[]{:S(2)}) collective-permute-start(bf16[2,2,4,2,64,128]{5,4,3,2,1,0:T(8,128)(2,1)S(1)} %get-tuple-element.28), channel_id=1, source_target_pairs={{0,96},{32,0},{64,32},{96,64},{1,97},{33,1},{65,33},{97,65},{2,98}... | collective-permute-start | bytes 1572872 | tf_op jit(solution)/shard_map/ppermute | solution.py:336
  19.3 14.1 %collective-permute-start.8 = (bf16[2,2,4,2,64,128]{5,4,3,2,1,0:T(8,128)(2,1)S(1)}, bf16[2,2,4,2,64,128]{5,4,3,2,1,0:T(8,128)(2,1)S(1)}, u32[]{:S(2)}, u32[]{:S(2)}) collective-permute-start(bf16[2,2,4,2,64,128]{5,4,3,2,1,0:T(8,128)(2,1)S(1)} %get-tuple-element.37), channel_id=1, source_target_pairs={{0,2},{2,128},{128,130},{130,0},{1,3},{3,129},{129,131},{131,1},{4... | collective-permute-start | bytes 1572872 | tf_op jit(solution)/shard_map/ppermute | solution.py:336
  19.4 14.2 %collective-permute-start.9 = (bf16[2,2,4,2,64,128]{5,4,3,2,1,0:T(8,128)(2,1)S(1)}, bf16[2,2,4,2,64,128]{5,4,3,2,1,0:T(8,128)(2,1)S(1)}, u32[]{:S(2)}, u32[]{:S(2)}) collective-permute-start(bf16[2,2,4,2,64,128]{5,4,3,2,1,0:T(8,128)(2,1)S(1)} %get-tuple-element.38), channel_id=1, source_target_pairs={{0,130},{2,0},{128,2},{130,128},{1,131},{3,1},{129,3},{131,129},{4... | collective-permute-start | bytes 1572872 | tf_op jit(solution)/shard_map/ppermute | solution.py:336
  29.4 8.3 %collective-permute-start.3 = (bf16[2,4,2,64,128]{4,3,2,1,0:T(8,128)(2,1)S(1)}, bf16[2,4,2,64,128]{4,3,2,1,0:T(8,128)(2,1)S(1)}, u32[]{:S(2)}, u32[]{:S(2)}) collective-permute-start(bf16[2,4,2,64,128]{4,3,2,1,0:T(8,128)(2,1)S(1)} %fusion.3), channel_id=1, source_target_pairs={{0,32},{32,64},{64,96},{96,0},{1,33},{33,65},{65,97},{97,1},{2,34}... | collective-permute-start | bytes 786440 | tf_op jit(solution)/shard_map/ppermute | solution.py:336
  29.6 8.1 %collective-permute-start.4 = (bf16[2,4,2,64,128]{4,3,2,1,0:T(8,128)(2,1)S(1)}, bf16[2,4,2,64,128]{4,3,2,1,0:T(8,128)(2,1)S(1)}, u32[]{:S(2)}, u32[]{:S(2)}) collective-permute-start(bf16[2,4,2,64,128]{4,3,2,1,0:T(8,128)(2,1)S(1)} %fusion.2), channel_id=1, source_target_pairs={{0,96},{32,0},{64,32},{96,64},{1,97},{33,1},{65,33},{97,65},{2,98}... | collective-permute-start | bytes 786440 | tf_op jit(solution)/shard_map/ppermute | solution.py:336
  33.5 9.3 %collective-permute-start.10 = (bf16[2,4,2,64,128]{4,3,2,1,0:T(8,128)(2,1)S(1)}, bf16[2,4,2,64,128]{4,3,2,1,0:T(8,128)(2,1)S(1)}, u32[]{:S(2)}, u32[]{:S(2)}) collective-permute-start(bf16[2,4,2,64,128]{4,3,2,1,0:T(8,128)(2,1)S(1)} %fusion.1), channel_id=1, source_target_pairs={{0,2},{2,128},{128,130},{130,0},{1,3},{3,129},{129,131},{131,1},{4... | collective-permute-start | bytes 786440 | tf_op jit(solution)/shard_map/ppermute | solution.py:336
  33.7 9.1 %collective-permute-start.11 = (bf16[2,4,2,64,128]{4,3,2,1,0:T(8,128)(2,1)S(1)}, bf16[2,4,2,64,128]{4,3,2,1,0:T(8,128)(2,1)S(1)}, u32[]{:S(2)}, u32[]{:S(2)}) collective-permute-start(bf16[2,4,2,64,128]{4,3,2,1,0:T(8,128)(2,1)S(1)} %fusion), channel_id=1, source_target_pairs={{0,130},{2,0},{128,2},{130,128},{1,131},{3,1},{129,3},{131,129},{4... | collective-permute-start | bytes 786440 | tf_op jit(solution)/shard_map/ppermute | solution.py:336
  38.5 8.2 %collective-permute-start.5 = (bf16[4,2,64,128]{3,2,1,0:T(8,128)(2,1)S(1)}, bf16[4,2,64,128]{3,2,1,0:T(8,128)(2,1)S(1)}, u32[]{:S(2)}, u32[]{:S(2)}) collective-permute-start(bf16[4,2,64,128]{3,2,1,0:T(8,128)(2,1)S(1)} %get-tuple-element.32), channel_id=1, source_target_pairs={{0,128},{2,130},{128,0},{130,2},{1,129},{3,131},{129,1},{131,3},{4... | collective-permute-start | bytes 393224 | tf_op jit(solution)/shard_map/ppermute | solution.py:336
  40.1 7.4 %collective-permute-start.6 = (bf16[4,2,64,128]{3,2,1,0:T(8,128)(2,1)S(1)}, bf16[4,2,64,128]{3,2,1,0:T(8,128)(2,1)S(1)}, u32[]{:S(2)}, u32[]{:S(2)}) collective-permute-start(bf16[4,2,64,128]{3,2,1,0:T(8,128)(2,1)S(1)} %get-tuple-element.33), channel_id=1, source_target_pairs={{0,2},{2,128},{128,130},{130,0},{1,3},{3,129},{129,131},{131,1},{4... | collective-permute-start | bytes 393224 | tf_op jit(solution)/shard_map/ppermute | solution.py:336
  40.4 7.1 %collective-permute-start.7 = (bf16[4,2,64,128]{3,2,1,0:T(8,128)(2,1)S(1)}, bf16[4,2,64,128]{3,2,1,0:T(8,128)(2,1)S(1)}, u32[]{:S(2)}, u32[]{:S(2)}) collective-permute-start(bf16[4,2,64,128]{3,2,1,0:T(8,128)(2,1)S(1)} %get-tuple-element.34), channel_id=1, source_target_pairs={{0,130},{2,0},{128,2},{130,128},{1,131},{3,1},{129,3},{131,129},{4... | collective-permute-start | bytes 393224 | tf_op jit(solution)/shard_map/ppermute | solution.py:336
  43.6 5.5 %collective-permute-start.12 = (bf16[4,2,64,128]{3,2,1,0:T(8,128)(2,1)S(1)}, bf16[4,2,64,128]{3,2,1,0:T(8,128)(2,1)S(1)}, u32[]{:S(2)}, u32[]{:S(2)}) collective-permute-start(bf16[4,2,64,128]{3,2,1,0:T(8,128)(2,1)S(1)} %get-tuple-element.42), channel_id=1, source_target_pairs={{0,64},{32,96},{64,0},{96,32},{1,65},{33,97},{65,1},{97,33},{2,66}... | collective-permute-start | bytes 393224 | tf_op jit(solution)/shard_map/ppermute | solution.py:336
  44.8 5.6 %collective-permute-start.13 = (bf16[4,2,64,128]{3,2,1,0:T(8,128)(2,1)S(1)}, bf16[4,2,64,128]{3,2,1,0:T(8,128)(2,1)S(1)}, u32[]{:S(2)}, u32[]{:S(2)}) collective-permute-start(bf16[4,2,64,128]{3,2,1,0:T(8,128)(2,1)S(1)} %get-tuple-element.43), channel_id=1, source_target_pairs={{0,32},{32,64},{64,96},{96,0},{1,33},{33,65},{65,97},{97,1},{2,34}... | collective-permute-start | bytes 393224 | tf_op jit(solution)/shard_map/ppermute | solution.py:336
  46.8 3.8 %collective-permute-start.14 = (bf16[4,2,64,128]{3,2,1,0:T(8,128)(2,1)S(1)}, bf16[4,2,64,128]{3,2,1,0:T(8,128)(2,1)S(1)}, u32[]{:S(2)}, u32[]{:S(2)}) collective-permute-start(bf16[4,2,64,128]{3,2,1,0:T(8,128)(2,1)S(1)} %get-tuple-element.44), channel_id=1, source_target_pairs={{0,96},{32,0},{64,32},{96,64},{1,97},{33,1},{65,33},{97,65},{2,98}... | collective-permute-start | bytes 393224 | tf_op jit(solution)/shard_map/ppermute | solution.py:336

commit v6 on v5

--- a/solution.py
+++ b/solution.py
@@ -33,7 +33,7 @@
     return pltpu.with_memory_space_constraint(x, pltpu.HBM)
 
 
-def half_kernel(block_hbm, kind_hbm, live_hbm, three_ref, coef_ref, out_ref, block_ref, kind_ref, live_ref, three, coef, weights, sems):
+def half_kernel(block_hbm, kind_hbm, live_hbm, three_ref, coef_ref, out_ref, weights, later, block_ref, kind_ref, live_ref, three, coef, sems):
     small = [
         pltpu.make_async_copy(here, there, sems.at[3 * SLOTS + i])
         for i, (here, there) in enumerate(((block_hbm, block_ref), (kind_hbm, kind_ref), (live_hbm, live_ref)))
@@ -45,7 +45,7 @@
         for s in range(SLOTS):
             rows, columns = pl.ds(half * 4, 4), pl.ds(s * SPAN, SPAN)
             large.append(
-                pltpu.make_async_copy(three_ref.at[s, rows], three.at[rows, :, columns], sems.at[(1 + half) * SLOTS + s])
+                pltpu.make_async_copy(three_ref.at[s, rows], (three, later)[half].at[:, :, columns], sems.at[(1 + half) * SLOTS + s])
             )
     for copy in large[:SLOTS]:
         copy.start()
@@ -64,47 +64,66 @@
         for k in range(KINDS):
             used = jnp.logical_and(kind_ref[s] == k, s < live_ref[0])
             weights[pl.ds(s * SPAN, SPAN), pl.ds(k * VIR, VIR)] = jnp.where(used, values, jnp.zeros_like(values))
-    for half in range(2):
-        for s in range(SLOTS):
-            large[half * SLOTS + s].wait()
-        left = three[pl.ds(half * 4, 4)].reshape(4 * SPAN, SLOTS * SPAN)
-        done = jnp.dot(left, weights[...], preferred_element_type=F32).astype(BF16)
-        for i in range(4):
-            for k in range(KINDS):
-                out_ref[half * 4 + i, pl.ds(k * SPAN, SPAN), :] = done[i * SPAN : (i + 1) * SPAN, k * VIR : (k + 1) * VIR]
+    for copy in large[:SLOTS]:
+        copy.wait()
+    four_rows(three, weights, out_ref)
+    for copy in large[SLOTS:]:
+        copy.wait()
+
+
+def four_rows(three, weights, out_ref):
+    left = three[...].reshape(4 * SPAN, SLOTS * SPAN)
+    done = jnp.dot(left, weights[...], preferred_element_type=F32).astype(BF16)
+    for i in range(4):
+        for k in range(KINDS):
+            out_ref[i, pl.ds(k * SPAN, SPAN), :] = done[i * SPAN : (i + 1) * SPAN, k * VIR : (k + 1) * VIR]
 
 
 def half_transform(slot_block, slot_aux, live_slots, three_center, vir_coef):
     return pl.pallas_call(
         half_kernel,
-        out_shape=jax.ShapeDtypeStruct((OCC, ROWS, VIR), BF16),
+        out_shape=[
+            jax.ShapeDtypeStruct((4, ROWS, VIR), BF16),
+            jax.ShapeDtypeStruct((SLOTS * SPAN, KINDS * VIR), BF16),
+            jax.ShapeDtypeStruct((4, SPAN, SLOTS * SPAN), BF16),
+        ],
         in_specs=[HBM] * 5,
-        out_specs=VMEM,
+        out_specs=[VMEM] * 3,
         scratch_shapes=[
             pltpu.SMEM((SLOTS,), jnp.int32),
             pltpu.SMEM((SLOTS,), jnp.int32),
             pltpu.SMEM((1,), jnp.int32),
-            pltpu.VMEM((OCC, SPAN, SLOTS * SPAN), BF16),
+            pltpu.VMEM((4, SPAN, SLOTS * SPAN), BF16),
             pltpu.VMEM((SLOTS, SPAN, VIR), BF16),
-            pltpu.VMEM((SLOTS * SPAN, KINDS * VIR), BF16),
             pltpu.SemaphoreType.DMA((3 * SLOTS + 3,)),
         ],
         compiler_params=params(12),
     )(*(in_hbm(x) for x in (slot_block, slot_aux)), live_slots, in_hbm(three_center), in_hbm(vir_coef))
 
 
+def other_half(later, weights):
+    return pl.pallas_call(
+        four_rows,
+        out_shape=jax.ShapeDtypeStruct((4, ROWS, VIR), BF16),
+        in_specs=[VMEM] * 2,
+        out_specs=VMEM,
+        compiler_params=params(10),
+        cost_estimate=pl.CostEstimate(flops=2 * 512 * 1536 * 512, bytes_accessed=4 * 2**20, transcendentals=0),
+    )(later, weights)
+
+
 PLACES = {
     (2, 0): (0, 0), (1, 1): (0, 1), (2, 1): (1, 0), (3, 0): (1, 1),
     (1, 0): (2, None), (3, 1): (3, None), (0, 0): (4, 0), (0, 1): (4, 1),
 }
 
 
-def product(core, first_j, turned, own_ref, other_ref, done):
+def product(core, turned, own_ref, other_ref, done):
     left = lax.broadcasted_iota(jnp.int32, (64, 128), 1) < 64
     for half in range(2):
         columns = pl.ds(pl.multiple_of(lax.rem(core + half, 2) * 128, 128), 128)
         for pair in range(2):
-            j = first_j + 2 * pair
+            j = 2 * pair
             right = jnp.concatenate(
                 [jnp.concatenate([ref[j + i, :, columns] for ref in (own_ref, other_ref)], axis=0) for i in range(2)],
                 axis=1,
@@ -118,7 +137,7 @@
                     done[half, 2 * pair + i, o, 1] = jnp.where(left, second, first).astype(BF16)
 
 
-def along_y_kernel(place_ref, own_ref, other_ref, *rest):
+def along_y_kernel(place_ref, own_ref, other_ref, own_later, other_later, *rest):
     outs, turned, done = rest[:5], rest[5], rest[6]
     y, core = place_ref[1], place_ref[2]
     unit = (
@@ -126,12 +145,12 @@
     ).astype(F32).astype(BF16)
     for o in range(OCC):
         for half in range(2):
-            for i, ref in enumerate((own_ref, other_ref)):
+            for i, ref in enumerate((own_ref, other_ref) if o < 4 else (own_later, other_later)):
                 across = lax.dot_general(
-                    unit, ref[o, :, half * 128 : half * 128 + 128], (((1,), (1,)), ((), ())), preferred_element_type=F32
+                    unit, ref[o % 4, :, half * 128 : half * 128 + 128], (((1,), (1,)), ((), ())), preferred_element_type=F32
                 )
                 turned[half, pl.ds(o * 128, 128), pl.ds(i * ROWS, ROWS)] = across.astype(BF16)
-    product(core, 0, turned, own_ref, other_ref, done)
+    product(core, turned, own_ref, other_ref, done)
     for d in range(4):
         for h in range(2):
             which, at = PLACES[d, h]
@@ -148,7 +167,7 @@
 def along_x_kernel(place_ref, own_ref, other_ref, turned, *rest):
     outs, done = rest[:5], rest[5]
     x, core = place_ref[0], place_ref[2]
-    product(core, 4, turned, own_ref, other_ref, done)
+    product(core, turned, own_ref, other_ref, done)
     for d in range(4):
         to = lax.rem(x + d, 4)
         for h in range(2):
@@ -166,7 +185,7 @@
 PART = (4, 2, 64, 128)
 
 
-def partial(place, own, other):
+def partial(place, own, other, own_later, other_later):
     pair = jax.ShapeDtypeStruct((2, 2) + PART, BF16)
     single = jax.ShapeDtypeStruct((2,) + PART, BF16)
     outs = [pair, pair, single, single, pair]
@@ -174,11 +193,11 @@
     *first, turned = pl.pallas_call(
         along_y_kernel,
         out_shape=outs + [jax.ShapeDtypeStruct((2, OCC * 128, 2 * ROWS), BF16)],
-        in_specs=[SMEM, VMEM, VMEM],
+        in_specs=[SMEM] + [VMEM] * 4,
         out_specs=[VMEM] * 6,
         scratch_shapes=[done],
         compiler_params=params(10),
-    )(place, own, other)
+    )(place, own, other, own_later, other_later)
     second = pl.pallas_call(
         along_x_kernel,
         out_shape=outs,
@@ -186,7 +205,7 @@
         out_specs=[VMEM] * 5,
         scratch_shapes=[done],
         compiler_params=params(10),
-    )(place, own, other, turned)
+    )(place, own_later, other_later, turned)
     return first, second
 
 
@@ -350,13 +369,15 @@
 def body(three_center, slot_block, slot_aux, live_slots, vir_coef, eps_occ, eps_vir, occ_index):
     x, y, core, low = lax.axis_index(X), lax.axis_index("y"), lax.axis_index("core"), lax.axis_index("xl")
     place = jnp.stack([x, y, core, low, lax.axis_index(BLK)]).astype(jnp.int32)
-    own = half_transform(slot_block, slot_aux, live_slots, three_center, vir_coef)
+    own, weights, later = half_transform(slot_block, slot_aux, live_slots, three_center, vir_coef)
     other = moved(own, "core", 1)
+    own_later = other_half(later, weights)
+    other_later = moved(own_later, "core", 1)
     below = denominators(eps_occ, eps_vir, occ_index, core, low)
-    other, below = lax.optimization_barrier((other, below))
+    other_later, below = lax.optimization_barrier((other_later, below))
 
     got = []
-    for axis, (ahead, back, one, minus, mine) in zip(("y", X), partial(place, own, other)):
+    for axis, (ahead, back, one, minus, mine) in zip(("y", X), partial(place, own, other, own_later, other_later)):
         got.append((axis, moved(ahead, axis, 1), moved(back, axis, -1), one, minus, mine))
     ins = []
     for at, (axis, from_back, from_ahead, one, minus, mine) in enumerate(got):

time: 88.2 us -> 87.8 us (level)
  waiting for transfers between devices: 12.9 us -> 12 us
    ppermute x15 -> x16, waiting for transfers between devices: 12.9 us -> 12 us  [moved(): return lax.ppermute(x, axis, [(i, (i + by) % n) for i in range(n)])]
    pallas_call x1 -> x2, Pallas kernels: 4.36 us -> 4.23 us  [the longest x1 3.25 us: half_transform(): pl.pallas_call(half_kernel, out_shape=[jax.ShapeDtypeStruct((4, ROWS, VIR...]
    ppermute x15 -> x16, starting transfers between devices: 22.5 us -> 22.4 us  [moved(): return lax.ppermute(x, axis, [(i, (i + by) % n) for i in range(n)])]
  transfers between devices with their start and end apart: 15 -> 16, of which waited for: 6 -> 7; matrix products, arithmetic and copies ran while one was open for 2% -> 2% of each run, Pallas kernels for 4% -> 4%
where the time goes in v6:
time: 87.8 us; the launch traced here: 87.6 us
  blocking collectives  35.1 us (40%)
  starting transfers between devices  22.4 us (26%)
  Pallas kernels  13.3 us (15%)
  waiting for transfers between devices  12 us (14%)
  between operations  2.83 us (3%)
  other arithmetic  1.12 us (1%)
    ppermute x16, starting transfers between devices, moved(): return lax.ppermute(x, axis, [(i, (i + by) % n) for i in range(n)])  22.4 us
    all_to_all x1, blocking collectives, body(): parts = lax.all_to_all(second_sum(ins), 'z', 0, 0, tiled=True)  17.7 us
    all_to_all x1, blocking collectives, body(): lax.all_to_all(sent, BLK, 0, 0, tiled=True)  17.4 us
    ppermute x16, waiting for transfers between devices, moved(): return lax.ppermute(x, axis, [(i, (i + by) % n) for i in range(n)])  12 us
    pallas_call x1, Pallas kernels, half_transform(): pl.pallas_call(half_kernel, out_shape=[jax.ShapeDtypeStruct((4, ROWS, VIR...  3.25 us
    pallas_call x1, Pallas kernels, partial(): pl.pallas_call(along_y_kernel, out_shape=outs + [jax.ShapeDtypeStruct((2,...  2.58 us
    pallas_call x1, Pallas kernels, partial(): pl.pallas_call(along_x_kernel, out_shape=outs, in_specs=[SMEM, VMEM, VMEM...  1.94 us
    pallas_call x2, Pallas kernels, first_sum(): pl.pallas_call(kernel, out_shape=[jax.ShapeDtypeStruct(PART, BF16)] * 4,...  1.81 us
  transfers between devices with their start and end apart: 16, of which 7 were waited for; matrix products, arithmetic and copies ran while one was open for 2% of the time, Pallas kernels for 4%

profile of v6, /device:TPU:1, one launch (start us, length us, event | category | flops | bytes accessed | tf_op | source)
XLA Modules:
  0.0 87.6 jit_solution(3381634521207153957)
XLA Ops:
  0.6 0.0 copy-start
  1.3 3.3 %shard_map.95 = (bf16[4,256,256]{2,1,0:T(8,128)(2,1)S(1)}, bf16[1536,512]{1,0:T(8,128)(2,1)S(1)}, bf16[4,128,1536]{2,1,0:T(8,128)(2,1)S(1)}) custom-call(s32[12]{0:T(128)} %block_hbm.1, s32[12]{0:T(128)} %kind_hbm.1, s32[1]{0:T(128)S(6)} %copy.10.live_hbm, bf16[12,8,128,128]{3,2,1,0:T(8,128)(2,1)} %three_ref.1, bf16[6144,256]{1,0:T(8,128)(2,1)} %coef_ref.1), custom_call_target="tpu_custom_call" | custom-call | tf_op jit(solution)/shard_map/pallas_call | solution.py:83
  4.6 0.0 copy-start.2
  4.6 0.0 copy-start.1
  4.6 1.0 %shard_map.96.own_later.own_ref = bf16[4,256,256]{2,1,0:T(8,128)(2,1)S(1)} custom-call(bf16[4,128,1536]{2,1,0:T(8,128)(2,1)S(1)} %get-tuple-element.29.three, bf16[1536,512]{1,0:T(8,128)(2,1)S(1)} %get-tuple-element.30.weights), custom_call_target="tpu_custom_call" | custom-call | flops 805306368 | bytes 4194304 | tf_op jit(solution)/shard_map/pallas_call | solution.py:105
  5.6 3.3 %collective-permute-start.1 = (bf16[4,256,256]{2,1,0:T(8,128)(2,1)S(1)}, bf16[4,256,256]{2,1,0:T(8,128)(2,1)S(1)}, u32[]{:S(2)}, u32[]{:S(2)}) collective-permute-start(bf16[4,256,256]{2,1,0:T(8,128)(2,1)S(1)} %shard_map.96.own_later.own_ref), channel_id=1, source_target_pairs={{0,1},{1,0},{2,3},{3,2},{4,5},{5,4},{6,7},{7,6},{8,9},{9,8},{10,11... | collective-permute-start | bytes 1572872 | tf_op jit(solution)/shard_map/ppermute | solution.py:355
  8.9 0.1 collective-permute-start
  9.0 0.1 reshape.25
  9.1 0.6 gather_fusion
  9.8 0.7 fusion.6
  11.8 0.1 stack.23.place_ref.refs_0_
  11.9 0.1 subtract_subtract_fusion.below_ref
  12.0 0.0 collective-permute-done.other_ref
  12.0 2.6 %shard_map.97 = (bf16[2,2,4,2,64,128]{5,4,3,2,1,0:T(8,128)(2,1)S(1)}, bf16[2,2,4,2,64,128]{5,4,3,2,1,0:T(8,128)(2,1)S(1)}, bf16[2,4,2,64,128]{4,3,2,1,0:T(8,128)...) custom-call(s32[5]{0:T(128)S(1)} %stack.23.place_ref.refs_0_, ...), custom_call_target="tpu_custom_call" | custom-call | tf_op jit(solution)/shard_map/pallas_call | solution.py:193
  14.6 0.1 collective-permute-start.2
  14.7 2.7 %collective-permute-start.3 = (bf16[2,2,4,2,64,128]{5,4,3,2,1,0:T(8,128)(2,1)S(1)}, bf16[2,2,4,2,64,128]{5,4,3,2,1,0:T(8,128)(2,1)S(1)}, u32[]{:S(2)}, u32[]{:S(2)}) collective-permute-start(bf16[2,2,4,2,64,128]{5,4,3,2,1,0:T(8,128)(2,1)S(1)} %get-tuple-element.34), channel_id=1, source_target_pairs={{0,96},{32,0},{64,32},{96,64},{1,97},{33,1},{65,33},{97,65},{2,98}... | collective-permute-start | bytes 1572872 | tf_op jit(solution)/shard_map/ppermute | solution.py:355
  17.4 1.9 %shard_map.99 = (bf16[2,2,4,2,64,128]{5,4,3,2,1,0:T(8,128)(2,1)S(1)}, bf16[2,2,4,2,64,128]{5,4,3,2,1,0:T(8,128)(2,1)S(1)}, bf16[2,4,2,64,128]{4,3,2,1,0:T(8,128)...) custom-call(s32[5]{0:T(128)S(1)} %stack.23.place_ref.refs_0_, ...), custom_call_target="tpu_custom_call" | custom-call | tf_op jit(solution)/shard_map/pallas_call | solution.py:201
  19.3 0.1 collective-permute-start.9
  19.4 2.7 %collective-permute-start.10 = (bf16[2,2,4,2,64,128]{5,4,3,2,1,0:T(8,128)(2,1)S(1)}, bf16[2,2,4,2,64,128]{5,4,3,2,1,0:T(8,128)(2,1)S(1)}, u32[]{:S(2)}, u32[]{:S(2)}) collective-permute-start(bf16[2,2,4,2,64,128]{5,4,3,2,1,0:T(8,128)(2,1)S(1)} %get-tuple-element.44), channel_id=1, source_target_pairs={{0,130},{2,0},{128,2},{130,128},{1,131},{3,1},{129,3},{131,129},{4... | collective-permute-start | bytes 1572872 | tf_op jit(solution)/shard_map/ppermute | solution.py:355
  22.1 6.9 %collective-permute-done.2.refs_2_ = bf16[2,2,4,2,64,128]{5,4,3,2,1,0:T(8,128)(2,1)S(1)} collective-permute-done((bf16[2,2,4,2,64,128]{5,4,3,2,1,0:T(8,128)(2,1)S(1)}, bf16[2,2,4,2,64,128]{5,4,3,2,1,0:T(8,128)(2,1)S(1)}, u32[]{:S(2)}, u32[]{:S(2)}) %collective-permute-start.2) | collective-permute-done | bytes 524320 | tf_op jit(solution)/shard_map/ppermute | solution.py:355
  29.0 0.1 fusion.3
  29.1 0.1 collective-permute-start.4
  29.2 0.0 collective-permute-done.3.refs_3_
  29.2 0.1 fusion.2
  29.3 2.7 %collective-permute-start.5 = (bf16[2,4,2,64,128]{4,3,2,1,0:T(8,128)(2,1)S(1)}, bf16[2,4,2,64,128]{4,3,2,1,0:T(8,128)(2,1)S(1)}, u32[]{:S(2)}, u32[]{:S(2)}) collective-permute-start(bf16[2,4,2,64,128]{4,3,2,1,0:T(8,128)(2,1)S(1)} %fusion.2), channel_id=1, source_target_pairs={{0,96},{32,0},{64,32},{96,64},{1,97},{33,1},{65,33},{97,65},{2,98}... | collective-permute-start | bytes 786440 | tf_op jit(solution)/shard_map/ppermute | solution.py:355
  32.0 1.1 %collective-permute-done.9.refs_2_ = bf16[2,2,4,2,64,128]{5,4,3,2,1,0:T(8,128)(2,1)S(1)} collective-permute-done((bf16[2,2,4,2,64,128]{5,4,3,2,1,0:T(8,128)(2,1)S(1)}, bf16[2,2,4,2,64,128]{5,4,3,2,1,0:T(8,128)(2,1)S(1)}, u32[]{:S(2)}, u32[]{:S(2)}) %collective-permute-start.9) | collective-permute-done | bytes 524320 | tf_op jit(solution)/shard_map/ppermute | solution.py:355
  33.1 0.1 fusion.1
  33.1 0.1 collective-permute-start.11
  33.2 0.1 fusion
  33.3 2.7 %collective-permute-start.12 = (bf16[2,4,2,64,128]{4,3,2,1,0:T(8,128)(2,1)S(1)}, bf16[2,4,2,64,128]{4,3,2,1,0:T(8,128)(2,1)S(1)}, u32[]{:S(2)}, u32[]{:S(2)}) collective-permute-start(bf16[2,4,2,64,128]{4,3,2,1,0:T(8,128)(2,1)S(1)} %fusion), channel_id=1, source_target_pairs={{0,130},{2,0},{128,2},{130,128},{1,131},{3,1},{129,3},{131,129},{4... | collective-permute-start | bytes 786440 | tf_op jit(solution)/shard_map/ppermute | solution.py:355
  36.1 0.9 collective-permute-done.4.refs_4_
  36.9 1.0 %shard_map.98 = (bf16[4,2,64,128]{3,2,1,0:T(8,128)(2,1)S(1)}, bf16[4,2,64,128]{3,2,1,0:T(8,128)(2,1)S(1)}, bf16[4,2,64,128]{3,2,1,0:T(8,128)(2,1)S(1)}, bf16[4,2,64,128]{3,2,1,0:T(8,128)(2,1)S(1)}) custom-call(s32[5]{0:T(128)S(1)} %stack.23.place_ref.refs_0_, bf16[2,2,4,2,64,128]{5,4,3,2,1,0:T(8,128)(2,1)S(1)} %get-tuple-element.32.refs_1_, ...), custom_call_target="tpu_custom_call" | custom-call | tf_op jit(solution)/shard_map/pallas_call | solution.py:228
  37.9 1.3 %collective-permute-start.6 = (bf16[4,2,64,128]{3,2,1,0:T(8,128)(2,1)S(1)}, bf16[4,2,64,128]{3,2,1,0:T(8,128)(2,1)S(1)}, u32[]{:S(2)}, u32[]{:S(2)}) collective-permute-start(bf16[4,2,64,128]{3,2,1,0:T(8,128)(2,1)S(1)} %get-tuple-element.38), channel_id=1, source_target_pairs={{0,128},{2,130},{128,0},{130,2},{1,129},{3,131},{129,1},{131,3},{4... | collective-permute-start | bytes 393224 | tf_op jit(solution)/shard_map/ppermute | solution.py:355
  39.2 0.3 collective-permute-start.7
  39.6 2.3 %collective-permute-start.8 = (bf16[4,2,64,128]{3,2,1,0:T(8,128)(2,1)S(1)}, bf16[4,2,64,128]{3,2,1,0:T(8,128)(2,1)S(1)}, u32[]{:S(2)}, u32[]{:S(2)}) collective-permute-start(bf16[4,2,64,128]{3,2,1,0:T(8,128)(2,1)S(1)} %get-tuple-element.40), channel_id=1, source_target_pairs={{0,130},{2,0},{128,2},{130,128},{1,131},{3,1},{129,3},{131,129},{4... | collective-permute-start | bytes 393224 | tf_op jit(solution)/shard_map/ppermute | solution.py:355
  41.9 0.8 shard_map.100
  42.7 1.2 %collective-permute-start.13 = (bf16[4,2,64,128]{3,2,1,0:T(8,128)(2,1)S(1)}, bf16[4,2,64,128]{3,2,1,0:T(8,128)(2,1)S(1)}, u32[]{:S(2)}, u32[]{:S(2)}) collective-permute-start(bf16[4,2,64,128]{3,2,1,0:T(8,128)(2,1)S(1)} %get-tuple-element.48), channel_id=1, source_target_pairs={{0,64},{32,96},{64,0},{96,32},{1,65},{33,97},{65,1},{97,33},{2,66}... | collective-permute-start | bytes 393224 | tf_op jit(solution)/shard_map/ppermute | solution.py:355
  44.0 2.0 %collective-permute-start.14 = (bf16[4,2,64,128]{3,2,1,0:T(8,128)(2,1)S(1)}, bf16[4,2,64,128]{3,2,1,0:T(8,128)(2,1)S(1)}, u32[]{:S(2)}, u32[]{:S(2)}) collective-permute-start(bf16[4,2,64,128]{3,2,1,0:T(8,128)(2,1)S(1)} %get-tuple-element.49), channel_id=1, source_target_pairs={{0,32},{32,64},{64,96},{96,0},{1,33},{33,65},{65,97},{97,1},{2,34}... | collective-permute-start | bytes 393224 | tf_op jit(solution)/shard_map/ppermute | solution.py:355
  46.0 0.7 collective-permute-start.15
  46.7 0.6 collective-permute-done.7.refs_2_
  47.3 0.9 %collective-permute-done.13.refs_5_ = bf16[4,2,64,128]{3,2,1,0:T(8,128)(2,1)S(1)} collective-permute-done((bf16[4,2,64,128]{3,2,1,0:T(8,128)(2,1)S(1)}, bf16[4,2,64,128]{3,2,1,0:T(8,128)(2,1)S(1)}, u32[]{:S(2)}, u32[]{:S(2)}) %collective-permute-start.13) | collective-permute-done | bytes 131104 | tf_op jit(solution)/shard_map/ppermute | solution.py:355
  48.2 1.3 %collective-permute-done.14.refs_6_ = bf16[4,2,64,128]{3,2,1,0:T(8,128)(2,1)S(1)} collective-permute-done((bf16[4,2,64,128]{3,2,1,0:T(8,128)(2,1)S(1)}, bf16[4,2,64,128]{3,2,1,0:T(8,128)(2,1)S(1)}, u32[]{:S(2)}, u32[]{:S(2)}) %collective-permute-start.14) | collective-permute-done | bytes 131104 | tf_op jit(solution)/shard_map/ppermute | solution.py:355
  49.5 0.2 collective-permute-done.15.refs_7_
  49.8 0.3 shard_map.101
  50.1 17.7 %all_to_all.10.parts_ref = s16[8,144,128]{2,1,0:T(8,128)(2,1)S(1)} all-to-all(s16[8,144,128]{2,1,0:T(8,128)(2,1)S(1)} %shard_map.101), channel_id=1, replica_groups=mesh['xh'=2,'y'=4,'z'=8,'xl'=2,'core'=2] {'z'}, dimensions={0} | all-to-all | bytes 589824 | tf_op jit(solution)/shard_map/all_to_all | solution.py:389
  67.8 0.9 %shard_map.102 = s16[32,8,128]{2,1,0:T(8,128)(2,1)S(1)} custom-call(s32[5]{0:T(128)S(1)} %stack.23.place_ref.refs_0_, s16[8,144,128]{2,1,0:T(8,128)(2,1)S(1)} %all_to_all.10.parts_ref, f32[2,64,128]{2,1,0:T(8,128)S(1)} %subtract_subtract_fusion.below_ref), custom_call_target="tpu_custom_call" | custom-call | tf_op jit(solution)/shard_map/pallas_call | solution.py:303
  68.7 17.4 %all_to_all.11.parts_ref = s16[32,8,128]{2,1,0:T(8,128)(2,1)S(1)} all-to-all(s16[32,8,128]{2,1,0:T(8,128)(2,1)S(1)} %shard_map.102), channel_id=1, replica_groups=mesh['xh'=2,'y'=4,'z'=8,'xl'=2,'core'=2] {'z','xl','core'}, dimensions={0} | all-to-all | bytes 131072 | tf_op jit(solution)/shard_map/all_to_all | solution.py:391
  86.1 1.5 %shard_map.103 = (f32[8,8,256]{2,1,0:T(8,128)}, f32[1,8]{1,0:T(1,128)}) custom-call(s32[5]{0:T(128)S(1)} %stack.23.place_ref.refs_0_, s16[32,8,128]{2,1,0:T(8,128)(2,1)S(1)} %all_to_all.11.parts_ref), custom_call_target="tpu_custom_call" | custom-call | tf_op jit(solution)/shard_map/pallas_call | solution.py:344
  (16 shorter events, 0.1 us)
Async XLA Ops:
  0.6 8.5 %copy-start = (f32[4000]{0:T(1024)S(1)}, f32[4000]{0:T(1024)}, u32[]{:S(2)}) copy-start(f32[4000]{0:T(1024)} %param.13) | copy-start | bytes 48004
  4.6 4.4 %copy-start.2 = (s32[8]{0:T(128)S(1)}, s32[8]{0:T(128)}, u32[]{:S(2)}) copy-start(s32[8]{0:T(128)} %param.15) | copy-start | bytes 100
  4.6 4.4 %copy-start.1 = (f32[256]{0:T(256)S(1)}, f32[256]{0:T(256)}, u32[]{:S(2)}) copy-start(f32[256]{0:T(256)} %param.14) | copy-start | bytes 3076
  5.6 6.5 %collective-permute-start.1 = (bf16[4,256,256]{2,1,0:T(8,128)(2,1)S(1)}, bf16[4,256,256]{2,1,0:T(8,128)(2,1)S(1)}, u32[]{:S(2)}, u32[]{:S(2)}) collective-permute-start(bf16[4,256,256]{2,1,0:T(8,128)(2,1)S(1)} %shard_map.96.own_later.own_ref), channel_id=1, source_target_pairs={{0,1},{1,0},{2,3},{3,2},{4,5},{5,4},{6,7},{7,6},{8,9},{9,8},{10,11... | collective-permute-start | bytes 1572872 | tf_op jit(solution)/shard_map/ppermute | solution.py:355
  8.9 3.1 %collective-permute-start = (bf16[4,256,256]{2,1,0:T(8,128)(2,1)S(1)}, bf16[4,256,256]{2,1,0:T(8,128)(2,1)S(1)}, u32[]{:S(2)}, u32[]{:S(2)}) collective-permute-start(bf16[4,256,256]{2,1,0:T(8,128)(2,1)S(1)} %get-tuple-element.28.own_ref), channel_id=1, source_target_pairs={{0,1},{1,0},{2,3},{3,2},{4,5},{5,4},{6,7},{7,6},{8,9},{9,8},{10,11... | collective-permute-start | bytes 1572872 | tf_op jit(solution)/shard_map/ppermute | solution.py:355
  14.6 14.4 %collective-permute-start.2 = (bf16[2,2,4,2,64,128]{5,4,3,2,1,0:T(8,128)(2,1)S(1)}, bf16[2,2,4,2,64,128]{5,4,3,2,1,0:T(8,128)(2,1)S(1)}, u32[]{:S(2)}, u32[]{:S(2)}) collective-permute-start(bf16[2,2,4,2,64,128]{5,4,3,2,1,0:T(8,128)(2,1)S(1)} %get-tuple-element.33), channel_id=1, source_target_pairs={{0,32},{32,64},{64,96},{96,0},{1,33},{33,65},{65,97},{97,1},{2,34}... | collective-permute-start | bytes 1572872 | tf_op jit(solution)/shard_map/ppermute | solution.py:355
  14.7 14.5 %collective-permute-start.3 = (bf16[2,2,4,2,64,128]{5,4,3,2,1,0:T(8,128)(2,1)S(1)}, bf16[2,2,4,2,64,128]{5,4,3,2,1,0:T(8,128)(2,1)S(1)}, u32[]{:S(2)}, u32[]{:S(2)}) collective-permute-start(bf16[2,2,4,2,64,128]{5,4,3,2,1,0:T(8,128)(2,1)S(1)} %get-tuple-element.34), channel_id=1, source_target_pairs={{0,96},{32,0},{64,32},{96,64},{1,97},{33,1},{65,33},{97,65},{2,98}... | collective-permute-start | bytes 1572872 | tf_op jit(solution)/shard_map/ppermute | solution.py:355
  19.3 13.7 %collective-permute-start.9 = (bf16[2,2,4,2,64,128]{5,4,3,2,1,0:T(8,128)(2,1)S(1)}, bf16[2,2,4,2,64,128]{5,4,3,2,1,0:T(8,128)(2,1)S(1)}, u32[]{:S(2)}, u32[]{:S(2)}) collective-permute-start(bf16[2,2,4,2,64,128]{5,4,3,2,1,0:T(8,128)(2,1)S(1)} %get-tuple-element.43), channel_id=1, source_target_pairs={{0,2},{2,128},{128,130},{130,0},{1,3},{3,129},{129,131},{131,1},{4... | collective-permute-start | bytes 1572872 | tf_op jit(solution)/shard_map/ppermute | solution.py:355
  19.4 13.8 %collective-permute-start.10 = (bf16[2,2,4,2,64,128]{5,4,3,2,1,0:T(8,128)(2,1)S(1)}, bf16[2,2,4,2,64,128]{5,4,3,2,1,0:T(8,128)(2,1)S(1)}, u32[]{:S(2)}, u32[]{:S(2)}) collective-permute-start(bf16[2,2,4,2,64,128]{5,4,3,2,1,0:T(8,128)(2,1)S(1)} %get-tuple-element.44), channel_id=1, source_target_pairs={{0,130},{2,0},{128,2},{130,128},{1,131},{3,1},{129,3},{131,129},{4... | collective-permute-start | bytes 1572872 | tf_op jit(solution)/shard_map/ppermute | solution.py:355
  29.1 7.8 %collective-permute-start.4 = (bf16[2,4,2,64,128]{4,3,2,1,0:T(8,128)(2,1)S(1)}, bf16[2,4,2,64,128]{4,3,2,1,0:T(8,128)(2,1)S(1)}, u32[]{:S(2)}, u32[]{:S(2)}) collective-permute-start(bf16[2,4,2,64,128]{4,3,2,1,0:T(8,128)(2,1)S(1)} %fusion.3), channel_id=1, source_target_pairs={{0,32},{32,64},{64,96},{96,0},{1,33},{33,65},{65,97},{97,1},{2,34}... | collective-permute-start | bytes 786440 | tf_op jit(solution)/shard_map/ppermute | solution.py:355
  29.3 7.7 %collective-permute-start.5 = (bf16[2,4,2,64,128]{4,3,2,1,0:T(8,128)(2,1)S(1)}, bf16[2,4,2,64,128]{4,3,2,1,0:T(8,128)(2,1)S(1)}, u32[]{:S(2)}, u32[]{:S(2)}) collective-permute-start(bf16[2,4,2,64,128]{4,3,2,1,0:T(8,128)(2,1)S(1)} %fusion.2), channel_id=1, source_target_pairs={{0,96},{32,0},{64,32},{96,64},{1,97},{33,1},{65,33},{97,65},{2,98}... | collective-permute-start | bytes 786440 | tf_op jit(solution)/shard_map/ppermute | solution.py:355
  33.1 8.8 %collective-permute-start.11 = (bf16[2,4,2,64,128]{4,3,2,1,0:T(8,128)(2,1)S(1)}, bf16[2,4,2,64,128]{4,3,2,1,0:T(8,128)(2,1)S(1)}, u32[]{:S(2)}, u32[]{:S(2)}) collective-permute-start(bf16[2,4,2,64,128]{4,3,2,1,0:T(8,128)(2,1)S(1)} %fusion.1), channel_id=1, source_target_pairs={{0,2},{2,128},{128,130},{130,0},{1,3},{3,129},{129,131},{131,1},{4... | collective-permute-start | bytes 786440 | tf_op jit(solution)/shard_map/ppermute | solution.py:355
  33.3 8.6 %collective-permute-start.12 = (bf16[2,4,2,64,128]{4,3,2,1,0:T(8,128)(2,1)S(1)}, bf16[2,4,2,64,128]{4,3,2,1,0:T(8,128)(2,1)S(1)}, u32[]{:S(2)}, u32[]{:S(2)}) collective-permute-start(bf16[2,4,2,64,128]{4,3,2,1,0:T(8,128)(2,1)S(1)} %fusion), channel_id=1, source_target_pairs={{0,130},{2,0},{128,2},{130,128},{1,131},{3,1},{129,3},{131,129},{4... | collective-permute-start | bytes 786440 | tf_op jit(solution)/shard_map/ppermute | solution.py:355
  37.9 8.0 %collective-permute-start.6 = (bf16[4,2,64,128]{3,2,1,0:T(8,128)(2,1)S(1)}, bf16[4,2,64,128]{3,2,1,0:T(8,128)(2,1)S(1)}, u32[]{:S(2)}, u32[]{:S(2)}) collective-permute-start(bf16[4,2,64,128]{3,2,1,0:T(8,128)(2,1)S(1)} %get-tuple-element.38), channel_id=1, source_target_pairs={{0,128},{2,130},{128,0},{130,2},{1,129},{3,131},{129,1},{131,3},{4... | collective-permute-start | bytes 393224 | tf_op jit(solution)/shard_map/ppermute | solution.py:355
  39.2 8.1 %collective-permute-start.7 = (bf16[4,2,64,128]{3,2,1,0:T(8,128)(2,1)S(1)}, bf16[4,2,64,128]{3,2,1,0:T(8,128)(2,1)S(1)}, u32[]{:S(2)}, u32[]{:S(2)}) collective-permute-start(bf16[4,2,64,128]{3,2,1,0:T(8,128)(2,1)S(1)} %get-tuple-element.39), channel_id=1, source_target_pairs={{0,2},{2,128},{128,130},{130,0},{1,3},{3,129},{129,131},{131,1},{4... | collective-permute-start | bytes 393224 | tf_op jit(solution)/shard_map/ppermute | solution.py:355
  39.6 7.7 %collective-permute-start.8 = (bf16[4,2,64,128]{3,2,1,0:T(8,128)(2,1)S(1)}, bf16[4,2,64,128]{3,2,1,0:T(8,128)(2,1)S(1)}, u32[]{:S(2)}, u32[]{:S(2)}) collective-permute-start(bf16[4,2,64,128]{3,2,1,0:T(8,128)(2,1)S(1)} %get-tuple-element.40), channel_id=1, source_target_pairs={{0,130},{2,0},{128,2},{130,128},{1,131},{3,1},{129,3},{131,129},{4... | collective-permute-start | bytes 393224 | tf_op jit(solution)/shard_map/ppermute | solution.py:355
  42.7 5.5 %collective-permute-start.13 = (bf16[4,2,64,128]{3,2,1,0:T(8,128)(2,1)S(1)}, bf16[4,2,64,128]{3,2,1,0:T(8,128)(2,1)S(1)}, u32[]{:S(2)}, u32[]{:S(2)}) collective-permute-start(bf16[4,2,64,128]{3,2,1,0:T(8,128)(2,1)S(1)} %get-tuple-element.48), channel_id=1, source_target_pairs={{0,64},{32,96},{64,0},{96,32},{1,65},{33,97},{65,1},{97,33},{2,66}... | collective-permute-start | bytes 393224 | tf_op jit(solution)/shard_map/ppermute | solution.py:355
  44.0 5.6 %collective-permute-start.14 = (bf16[4,2,64,128]{3,2,1,0:T(8,128)(2,1)S(1)}, bf16[4,2,64,128]{3,2,1,0:T(8,128)(2,1)S(1)}, u32[]{:S(2)}, u32[]{:S(2)}) collective-permute-start(bf16[4,2,64,128]{3,2,1,0:T(8,128)(2,1)S(1)} %get-tuple-element.49), channel_id=1, source_target_pairs={{0,32},{32,64},{64,96},{96,0},{1,33},{33,65},{65,97},{97,1},{2,34}... | collective-permute-start | bytes 393224 | tf_op jit(solution)/shard_map/ppermute | solution.py:355
  46.0 3.8 %collective-permute-start.15 = (bf16[4,2,64,128]{3,2,1,0:T(8,128)(2,1)S(1)}, bf16[4,2,64,128]{3,2,1,0:T(8,128)(2,1)S(1)}, u32[]{:S(2)}, u32[]{:S(2)}) collective-permute-start(bf16[4,2,64,128]{3,2,1,0:T(8,128)(2,1)S(1)} %get-tuple-element.50), channel_id=1, source_target_pairs={{0,96},{32,0},{64,32},{96,64},{1,97},{33,1},{65,33},{97,65},{2,98}... | collective-permute-start | bytes 393224 | tf_op jit(solution)/shard_map/ppermute | solution.py:355
